TPU v7x, 32 devices: a whole 2x2x4 slice. The times are simulated.
32 devices in a mesh: blade: 4 (over y, x), span: 8 (over z, core).
Axes of the slice: x: 2, y: 2, z: 4, core: 2. Of those that a mesh axis runs over, the one named last changes fastest.
Arguments:
- adj_source: float32 [8, 1024, 1024], P(None, 'blade', 'span'), may hold values from -4 to 4
- face_flux: float32 [8, 32768], P(None, ('blade', 'span')), may hold values from -6 to 6
- face_owner: int32 [32768], P(('blade', 'span')), may hold values from 0 to 3, as said below
- face_cell: int32 [32768], P(('blade', 'span')), may hold values from 0 to 32767
- block_inverse: float32 [1024, 128], P('span'), may hold values from -4 to 4
- carry_gain: float32 [1024, 128], P('span'), may hold values from -1 to 1
Outputs:
- adjoint: float32 [8, 1024, 1024], P(None, 'blade', 'span')
Inputs may be any that keep to these rules, and one draw needn't show every extreme that they name: `face_owner`: the faces of one device name each owner at most 512 times; in every group of devices of one span index, one owner is named exactly 512 times by each of its devices.
All inputs are finite; a program needn't handle non-finite values.
Results may differ from a plain program's by a relative error of at most 0.0001.
Values sent between devices are 32-bit elements; how exact they have to be, the bound alone decides.
No kernel may reach another device: no remote copies, remote signals or barrier semaphores. Data moves between devices by JAX's collectives and lax.ppermute only.
A program may use at most 128 MiB of HBM per device.

v0:
```python
import jax
import jax.numpy as jnp
from jax import lax
from jax.sharding import PartitionSpec as P

ITERS = 3


coupling = 0.05
highest = lax.Precision.HIGHEST


def extended(block, sides, width):
    for axis, dim in sides:
        count = lax.axis_size(axis)
        forward = [(i, i + 1) for i in range(count - 1)]
        forward.append((count - 1, 0))
        backward = [(target, source) for source, target in forward]
        low = lax.ppermute(
            lax.slice_in_dim(block, block.shape[dim] - width, None, axis=dim), axis, forward
        )
        high = lax.ppermute(lax.slice_in_dim(block, 0, width, axis=dim), axis, backward)
        block = jnp.concatenate([low, block, high], axis=dim)
    return block


def pencil_solve(pencil, blocks, gains):
    harm_rows, columns, radial = pencil.shape
    nblocks, block_rows, _ = blocks.shape
    lines_all = pencil.reshape(harm_rows * columns, nblocks, block_rows)
    product = jnp.einsum("ckj,kij->kci", lines_all, blocks, precision=highest)

    def advance(running, element):
        local_part, gain = element
        updated = local_part + lax.dot_general(
            running,
            gain,
            (((1,), (1,)), ((), ())),
            precision=highest,
            preferred_element_type=jnp.float32,
        )
        return (updated, updated)

    initial = jnp.zeros((harm_rows * columns, block_rows), jnp.float32)
    _, solved = lax.scan(advance, initial, (product, gains))
    return jnp.transpose(solved, (1, 0, 2)).reshape(harm_rows, columns, radial)


def row_rhs(right_side, field):
    widened = extended(field, (("blade", 1),), 1)
    return right_side + coupling * (widened[:, :-2, :] + widened[:, 2:, :])


def body(adj_source, face_flux, face_owner, face_cell, block_inverse, carry_gain):
    harm_rows, circum, block_rows = adj_source.shape
    blades = lax.axis_size("blade")
    faces_dev = face_owner.shape[0]
    capacity = faces_dev // 2
    onehot = (face_owner[:, None] == jnp.arange(blades, dtype=jnp.int32)[None, :]).astype(jnp.int32)
    rank_in = jnp.sum((jnp.cumsum(onehot, axis=0) - 1) * onehot, axis=1)
    slot_ids = face_owner * capacity + rank_in
    send_flux = (
        jnp.zeros((harm_rows, blades * capacity), jnp.float32)
        .at[:, slot_ids]
        .set(face_flux)
        .reshape(harm_rows, blades, capacity)
    )
    send_cell = (
        jnp.zeros((blades * capacity,), jnp.int32)
        .at[slot_ids]
        .set(face_cell)
        .reshape(1, blades, capacity)
    )
    fluxes, cell_ids = (
        lax.all_to_all(send_flux, "blade", split_axis=1, concat_axis=1, tiled=True),
        lax.all_to_all(send_cell, "blade", split_axis=1, concat_axis=1, tiled=True),
    )
    fluxes = fluxes.reshape(harm_rows, blades * capacity)
    cell_ids = cell_ids.reshape(blades * capacity)
    wall_flux = jnp.zeros((harm_rows, circum * block_rows), jnp.float32).at[:, cell_ids].add(fluxes)
    right_side = adj_source + wall_flux.reshape(harm_rows, circum, block_rows)
    inverses, couplings = (
        lax.all_gather(block_inverse, "span", axis=0, tiled=True),
        lax.all_gather(carry_gain, "span", axis=0, tiled=True),
    )
    blocks = inverses.reshape(-1, block_rows, block_rows)
    gains = couplings.reshape(-1, block_rows, block_rows)

    def transposed(rhs_rows):
        pencil = lax.all_to_all(rhs_rows, "span", split_axis=1, concat_axis=2, tiled=True)
        return lax.all_to_all(
            pencil_solve(pencil, blocks, gains), "span", split_axis=2, concat_axis=1, tiled=True
        )

    field = transposed(right_side)
    for sweep_index in range(1, ITERS):
        field = transposed(row_rhs(right_side, field))
    return field


def solution(mesh):
    in_specs = (
        P(None, "blade", "span"),
        P(None, ("blade", "span")),
        P(("blade", "span")),
        P(("blade", "span")),
        P("span", None),
        P("span", None),
    )
    out_specs = P(None, "blade", "span")
    return jax.shard_map(body, mesh=mesh, in_specs=in_specs, out_specs=out_specs, check_vma=False)
```

profile of v0, /device:TPU:0, one launch (start us, length us, event | category | flops | bytes accessed | tf_op | source)
XLA Modules:
  0.0 337.8 jit_solution(4415771665171273126)
XLA Ops:
  3.7 5.0 %scatter_custom_fusion = s32[2048]{0:T(1024)} fusion(s32[1024]{0:T(1024)S(1)} %compare_select_fusion.1, s32[1024]{0:T(1024)} %param.15, s32[]{:T(128)} %constant.44.clone.1), kind=kCustom, calls=%fused_computation.58 | custom fusion | bytes 8704 | tf_op jit(solution)/shard_map/scatter | solution.py:71
  8.7 5.2 %all-to-all-start = ((s32[1,4,512]{2,0,1:T(1,128)}), s32[1,4,512]{2,0,1:T(1,128)S(1)}, u32[]{:S(2)}, u32[]{:S(2)}) async-start(s32[1,4,512]{2,0,1:T(1,128)} %bitcast.2), calls=%async_computation | async-start | bytes 16384 | tf_op jit(solution)/shard_map/all_to_all | solution.py:76
  14.9 3.3 scatter_custom_fusion.1
  19.1 4.2 %all-to-all-start.1 = ((f32[8,4,512]{2,0,1:T(8,128)}), f32[8,4,512]{2,0,1:T(8,128)S(1)}, u32[]{:S(2)}, u32[]{:S(2)}) async-start(f32[8,4,512]{2,0,1:T(8,128)} %copy.65), calls=%async_computation.1 | async-start | bytes 131072 | tf_op jit(solution)/shard_map/all_to_all | solution.py:75
  23.4 4.8 %all-to-all-done.1 = f32[8,4,512]{2,0,1:T(8,128)S(1)} async-done(((f32[8,4,512]{2,0,1:T(8,128)}), f32[8,4,512]{2,0,1:T(8,128)S(1)}, u32[]{:S(2)}, u32[]{:S(2)}) %all-to-all-start.1) | async-done | bytes 65568 | tf_op jit(solution)/shard_map/all_to_all | solution.py:75
  28.6 20.4 %scatter_custom_fusion.2 = f32[8,32768]{0,1:T(8,128)} fusion(s32[2048]{0:T(1024)S(1)} %bitcast.154, f32[2048,8]{1,0:T(8,128)S(1)} %copy.66, f32[]{:T(128)} %constant.45.clone.1), kind=kCustom, calls=%fused_computation.33 | custom fusion | flops 16384 | bytes 1048580 | tf_op jit(solution)/shard_map/scatter-add | solution.py:80
  48.9 9.2 %copy.68 = f32[8,256,128]{2,0,1:T(8,128)S(1)} copy(f32[8,256,128]{0,2,1:T(8,128)} %bitcast.124) | data formatting | bytes 2097152 | tf_op jit(solution)/shard_map/reshape | solution.py:81
  59.7 4.9 %all-to-all-start.2 = ((f32[8,256,128]{2,0,1:T(8,128)}), f32[8,256,128]{2,0,1:T(8,128)S(1)}, u32[]{:S(2)}, u32[]{:S(2)}) async-start(f32[8,256,128]{2,0,1:T(8,128)} %copy_add_fusion), calls=%async_computation.2 | async-start | bytes 2097152 | tf_op jit(solution)/shard_map/all_to_all | solution.py:90
  64.6 34.7 %all_gather.6 = f32[1024,128]{1,0:T(8,128)S(1)} all-gather(f32[128,128]{1,0:T(8,128)S(1)} %copy-done.1), channel_id=1, replica_groups=mesh['blade'=4,'span'=8] {'span'}, dimensions={0}, use_global_device_ids=true | all-gather | bytes 589824 | tf_op jit(solution)/shard_map/all_gather | solution.py:83
  99.3 15.0 %all_gather.7 = f32[1024,128]{1,0:T(8,128)S(1)} all-gather(f32[128,128]{1,0:T(8,128)S(1)} %copy-done.2), channel_id=1, replica_groups=mesh['blade'=4,'span'=8] {'span'}, dimensions={0}, use_global_device_ids=true | all-gather | bytes 589824 | tf_op jit(solution)/shard_map/all_gather | solution.py:84
  120.5 3.9 %reshape.138 = f32[8,1,32768]{2,1,0:T(1,128)S(1)} reshape(f32[1024,8,32]{2,1,0:T(8,128)} %bitcast.125) | data formatting | bytes 2097152
  124.4 30.7 %all_to_all.109 = f32[8,1,32768]{2,1,0:T(1,128)S(1)} all-to-all(f32[8,1,32768]{2,1,0:T(1,128)S(1)} %reshape.138), channel_id=1, replica_groups=mesh['blade'=4,'span'=8] {'span'}, dimensions={0} | all-to-all | bytes 2097152 | tf_op jit(solution)/shard_map/all_to_all | solution.py:91
  158.7 3.3 reshape.139
  171.8 3.6 %all-to-all-start.4 = ((f32[8,256,128]{2,0,1:T(8,128)}), f32[8,256,128]{2,0,1:T(8,128)S(1)}, u32[]{:S(2)}, u32[]{:S(2)}) async-start(f32[8,256,128]{2,0,1:T(8,128)} %fusion.31), calls=%async_computation.4 | async-start | bytes 2097152 | tf_op jit(solution)/shard_map/all_to_all | solution.py:90
  175.4 26.5 %all-to-all-done.4 = f32[8,256,128]{2,0,1:T(8,128)S(1)} async-done(((f32[8,256,128]{2,0,1:T(8,128)}), f32[8,256,128]{2,0,1:T(8,128)S(1)}, u32[]{:S(2)}, u32[]{:S(2)}) %all-to-all-start.4) | async-done | bytes 1048608 | tf_op jit(solution)/shard_map/all_to_all | solution.py:90
  208.1 3.9 %reshape.140 = f32[8,1,32768]{2,1,0:T(1,128)S(1)} reshape(f32[1024,8,32]{2,1,0:T(8,128)} %bitcast.127) | data formatting | bytes 2097152
  212.1 29.0 %all_to_all.110 = f32[8,1,32768]{2,1,0:T(1,128)S(1)} all-to-all(f32[8,1,32768]{2,1,0:T(1,128)S(1)} %reshape.140), channel_id=1, replica_groups=mesh['blade'=4,'span'=8] {'span'}, dimensions={0} | all-to-all | bytes 2097152 | tf_op jit(solution)/shard_map/all_to_all | solution.py:91
  244.2 3.3 reshape.141
  258.5 3.6 %all-to-all-start.6 = ((f32[8,256,128]{2,0,1:T(8,128)}), f32[8,256,128]{2,0,1:T(8,128)S(1)}, u32[]{:S(2)}, u32[]{:S(2)}) async-start(f32[8,256,128]{2,0,1:T(8,128)} %fusion.28), calls=%async_computation.6 | async-start | bytes 2097152 | tf_op jit(solution)/shard_map/all_to_all | solution.py:90
  262.1 26.5 %all-to-all-done.6 = f32[8,256,128]{2,0,1:T(8,128)S(1)} async-done(((f32[8,256,128]{2,0,1:T(8,128)}), f32[8,256,128]{2,0,1:T(8,128)S(1)}, u32[]{:S(2)}, u32[]{:S(2)}) %all-to-all-start.6) | async-done | bytes 1048608 | tf_op jit(solution)/shard_map/all_to_all | solution.py:90
  294.9 3.9 %reshape.142 = f32[8,1,32768]{2,1,0:T(1,128)S(1)} reshape(f32[1024,8,32]{2,1,0:T(8,128)} %bitcast.129) | data formatting | bytes 2097152
  298.8 29.0 %all_to_all.111 = f32[8,1,32768]{2,1,0:T(1,128)S(1)} all-to-all(f32[8,1,32768]{2,1,0:T(1,128)S(1)} %reshape.142), channel_id=1, replica_groups=mesh['blade'=4,'span'=8] {'span'}, dimensions={0} | all-to-all | bytes 2097152 | tf_op jit(solution)/shard_map/all_to_all | solution.py:91
  330.9 3.3 reshape.143
  334.2 3.6 %copy.84 = f32[8,8,32,128]{3,2,1,0:T(8,128)} copy(f32[8,8,32,128]{2,0,3,1:T(8,128)} %bitcast.130) | data formatting | bytes 2097152 | tf_op jit(solution)/shard_map/all_to_all | solution.py:91
  (104 shorter events, 63.5 us)
Async XLA Ops:
  8.7 10.4 %all-to-all-start = ((s32[1,4,512]{2,0,1:T(1,128)}), s32[1,4,512]{2,0,1:T(1,128)S(1)}, u32[]{:S(2)}, u32[]{:S(2)}) async-start(s32[1,4,512]{2,0,1:T(1,128)} %bitcast.2), calls=%async_computation | async-start | bytes 16384 | tf_op jit(solution)/shard_map/all_to_all | solution.py:76
  19.1 9.0 %all-to-all-start.1 = ((f32[8,4,512]{2,0,1:T(8,128)}), f32[8,4,512]{2,0,1:T(8,128)S(1)}, u32[]{:S(2)}, u32[]{:S(2)}) async-start(f32[8,4,512]{2,0,1:T(8,128)} %copy.65), calls=%async_computation.1 | async-start | bytes 131072 | tf_op jit(solution)/shard_map/all_to_all | solution.py:75
  28.5 29.6 %copy-start = (f32[8,256,128]{2,1,0:T(8,128)S(1)}, f32[8,256,128]{2,1,0:T(8,128)}, u32[]{:S(2)}) copy-start(f32[8,256,128]{2,1,0:T(8,128)} %param.12) | copy-start | bytes 3145732
  28.5 36.1 %copy-start.1 = (f32[128,128]{1,0:T(8,128)S(1)}, f32[128,128]{1,0:T(8,128)}, u32[]{:S(2)}) copy-start(f32[128,128]{1,0:T(8,128)} %param.16) | copy-start | bytes 196612
  28.5 70.7 %copy-start.2 = (f32[128,128]{1,0:T(8,128)S(1)}, f32[128,128]{1,0:T(8,128)}, u32[]{:S(2)}) copy-start(f32[128,128]{1,0:T(8,128)} %param.17) | copy-start | bytes 196612
  59.7 54.5 %all-to-all-start.2 = ((f32[8,256,128]{2,0,1:T(8,128)}), f32[8,256,128]{2,0,1:T(8,128)S(1)}, u32[]{:S(2)}, u32[]{:S(2)}) async-start(f32[8,256,128]{2,0,1:T(8,128)} %copy_add_fusion), calls=%async_computation.2 | async-start | bytes 2097152 | tf_op jit(solution)/shard_map/all_to_all | solution.py:90
  164.9 4.6 %collective-permute-start = (f32[8,1,128]{2,0,1:T(8,128)S(1)}, f32[8,1,128]{2,0,1:T(8,128)S(1)}, u32[]{:S(2)}, u32[]{:S(2)}) collective-permute-start(f32[8,1,128]{2,0,1:T(8,128)S(1)} %get-tuple-element.256), channel_id=1, source_target_pairs={{0,8},{8,16},{16,24},{24,0},{1,9},{9,17},{17,25},{25,1},{2,10},{10... | collective-permute-start | bytes 12296 | tf_op jit(solution)/shard_map/ppermute | solution.py:19
  165.7 3.7 %collective-permute-start.1 = (f32[8,1,128]{2,0,1:T(8,128)S(1)}, f32[8,1,128]{2,0,1:T(8,128)S(1)}, u32[]{:S(2)}, u32[]{:S(2)}) collective-permute-start(f32[8,1,128]{2,0,1:T(8,128)S(1)} %get-tuple-element.257), channel_id=1, source_target_pairs={{8,0},{16,8},{24,16},{0,24},{9,1},{17,9},{25,17},{1,25},{10,2},{18... | collective-permute-start | bytes 12296 | tf_op jit(solution)/shard_map/ppermute | solution.py:22
  171.8 30.1 %all-to-all-start.4 = ((f32[8,256,128]{2,0,1:T(8,128)}), f32[8,256,128]{2,0,1:T(8,128)S(1)}, u32[]{:S(2)}, u32[]{:S(2)}) async-start(f32[8,256,128]{2,0,1:T(8,128)} %fusion.31), calls=%async_computation.4 | async-start | bytes 2097152 | tf_op jit(solution)/shard_map/all_to_all | solution.py:90
  250.3 4.6 %collective-permute-start.2 = (f32[8,1,128]{2,0,1:T(8,128)S(1)}, f32[8,1,128]{2,0,1:T(8,128)S(1)}, u32[]{:S(2)}, u32[]{:S(2)}) collective-permute-start(f32[8,1,128]{2,0,1:T(8,128)S(1)} %get-tuple-element.254), channel_id=1, source_target_pairs={{0,8},{8,16},{16,24},{24,0},{1,9},{9,17},{17,25},{25,1},{2,10},{10... | collective-permute-start | bytes 12296 | tf_op jit(solution)/shard_map/ppermute | solution.py:19
  252.6 3.6 %collective-permute-start.3 = (f32[8,1,128]{2,0,1:T(8,128)S(1)}, f32[8,1,128]{2,0,1:T(8,128)S(1)}, u32[]{:S(2)}, u32[]{:S(2)}) collective-permute-start(f32[8,1,128]{2,0,1:T(8,128)S(1)} %get-tuple-element.255), channel_id=1, source_target_pairs={{8,0},{16,8},{24,16},{0,24},{9,1},{17,9},{25,17},{1,25},{10,2},{18... | collective-permute-start | bytes 12296 | tf_op jit(solution)/shard_map/ppermute | solution.py:22
  258.5 30.1 %all-to-all-start.6 = ((f32[8,256,128]{2,0,1:T(8,128)}), f32[8,256,128]{2,0,1:T(8,128)S(1)}, u32[]{:S(2)}, u32[]{:S(2)}) async-start(f32[8,256,128]{2,0,1:T(8,128)} %fusion.28), calls=%async_computation.6 | async-start | bytes 2097152 | tf_op jit(solution)/shard_map/all_to_all | solution.py:90
where the time goes:
time: 338 us
  blocking collectives  138 us (41%)
  waiting for transfers between devices  62.3 us (18%)
  local copies, waits for them, and re-layouts  59.8 us (18%)
  other arithmetic  39.4 us (12%)
  starting transfers between devices  27.4 us (8%)
  matrix products  9.59 us (3%)
    all_to_all x3, blocking collectives, transposed(): lax.all_to_all(pencil_solve(pencil, blocks, gains), 'span', split_axis=2,...  88.7 us
    all_to_all x3, waiting for transfers between devices, transposed(): lax.all_to_all(rhs_rows, 'span', split_axis=1, concat_axis=2, tiled=True)  53 us
    all_gather x1, blocking collectives, body(): lax.all_gather(block_inverse, 'span', axis=0, tiled=True)  34.7 us
    unnamed x13, local copies, waits for them, and re-layouts  22.6 us
    scatter-add x1, other arithmetic, body(): jnp.zeros((harm_rows, circum * block_rows), jnp.float32).at[:, cell_ids]  20.4 us
    all_gather x1, blocking collectives, body(): lax.all_gather(carry_gain, 'span', axis=0, tiled=True)  15 us
    all_to_all x3, starting transfers between devices, transposed(): lax.all_to_all(rhs_rows, 'span', split_axis=1, concat_axis=2, tiled=True)  12 us
    all_to_all x4, local copies, waits for them, and re-layouts, transposed(): lax.all_to_all(pencil_solve(pencil, blocks, gains), 'span', split_axis=2,...  9.8 us
  transfers between devices with their start and end apart: 9, of which 6 were waited for; matrix products, arithmetic and copies ran while one was open for 2% of the time, Pallas kernels for 0%

commit v1 on v0

--- a/solution.py
+++ b/solution.py
@@ -1,14 +1,290 @@
 import jax
 import jax.numpy as jnp
 from jax import lax
+from jax.experimental import pallas as pl
+from jax.experimental.pallas import tpu as pltpu
 from jax.sharding import PartitionSpec as P
 
 ITERS = 3
-
+HALO = ITERS - 1
 
 coupling = 0.05
 highest = lax.Precision.HIGHEST
-
+VMEM = pl.BlockSpec(memory_space=pltpu.VMEM)
+VMEM_LIMIT = 48 * 1024 * 1024
+
+
+def params():
+    return pltpu.CompilerParams(vmem_limit_bytes=VMEM_LIMIT)
+
+
+def split(x):
+    hi = x.astype(jnp.bfloat16)
+    return hi, (x - hi.astype(jnp.float32)).astype(jnp.bfloat16)
+
+
+def pack_kernel(flux, owner, cell, first, last, near, far, diag):
+    groups = flux.shape[1] // 128
+    odd = lax.rem(lax.axis_index("blade"), 2)
+    for message in (near, far, diag):
+        for group in range(groups):
+            message[group] = flux[:, group * 128 : (group + 1) * 128]
+        message[groups] = owner[...].astype(jnp.float32)
+        message[groups + 1] = cell[...].astype(jnp.float32)
+    rows = first.shape[1]
+    for row in range(HALO):
+        low = first[:, row, :]
+        high = last[:, rows - HALO + row, :]
+        near[groups + 2 + row] = jnp.where(odd == 0, high, low)
+        diag[groups + 2 + row] = jnp.where(odd == 0, low, high)
+
+
+def pack(adj_source, face_flux, face_owner, face_cell):
+    harm_rows, circum, block_rows = adj_source.shape
+    groups = face_owner.shape[0] // 128
+    with_halo = jax.ShapeDtypeStruct((groups + 2 + HALO, 8, 128), jnp.float32)
+    faces = jax.ShapeDtypeStruct((groups + 2, 8, 128), jnp.float32)
+    whole = lambda *shape: pl.BlockSpec(shape, lambda i: (0,) * len(shape))
+    last_tile = circum // 8 - 1
+    return pl.pallas_call(
+        pack_kernel,
+        grid=(1,),
+        out_shape=(with_halo, faces, with_halo),
+        in_specs=[
+            whole(*face_flux.shape),
+            whole(groups, 128),
+            whole(groups, 128),
+            pl.BlockSpec((harm_rows, 8, block_rows), lambda i: (0, 0, 0)),
+            pl.BlockSpec((harm_rows, 8, block_rows), lambda i: (0, last_tile, 0)),
+        ],
+        out_specs=(whole(*with_halo.shape), whole(*faces.shape), whole(*with_halo.shape)),
+        compiler_params=params(),
+        cost_estimate=pl.CostEstimate(flops=0, bytes_accessed=1 << 20, transcendentals=0),
+        name="pack",
+    )(
+        face_flux,
+        face_owner.reshape(groups, 128),
+        face_cell.reshape(groups, 128),
+        adj_source,
+        adj_source,
+    )
+
+
+def right_kernel(adj, own, near, far, diag, *rest):
+    outs, (hot_rows, weights, acc) = rest[:-3], rest[-3:]
+    harm_rows, circum, block_rows = adj.shape
+    blades = lax.axis_size("blade")
+    blade = lax.axis_index("blade")
+    span = lax.axis_index("span")
+    total = circum * blades
+    groups = own.shape[0] - 2
+    rows = hot_rows.shape[0]
+    row = lax.broadcasted_iota(jnp.int32, (rows, 128), 0)
+    low_at = circum + 8 - HALO
+    label = jnp.where(
+        row < circum + HALO,
+        row,
+        jnp.where((row >= low_at) & (row < circum + 8), row - (circum + 8) + total, -1),
+    )
+    radial = lax.broadcasted_iota(jnp.int32, (block_rows, 128), 0)
+    for step, message in enumerate((own, near, far, diag)):
+        owner = message[groups].astype(jnp.int32)
+        cell = message[groups + 1].astype(jnp.int32)
+        place = (owner - blade) * circum + cell // block_rows
+        place = jnp.where(place < 0, place + total, place)
+        inner = cell % block_rows
+        for group in range(groups):
+            lanes = slice(group * 128, (group + 1) * 128)
+            lanes_low = slice((groups + group) * 128, (groups + group + 1) * 128)
+            hot = jnp.where(label == place[group : group + 1, :], 1.0, 0.0).astype(jnp.bfloat16)
+            hot_rows[:, lanes] = hot
+            hot_rows[:, lanes_low] = hot
+            mask = radial == inner[group : group + 1, :]
+            flux_hi, flux_lo = split(message[group])
+            flux_hi, flux_lo = flux_hi.astype(jnp.float32), flux_lo.astype(jnp.float32)
+            for h in range(harm_rows):
+                part = slice(h * block_rows, (h + 1) * block_rows)
+                weights[part, lanes] = jnp.where(mask, flux_hi[h : h + 1, :], 0.0).astype(
+                    jnp.bfloat16
+                )
+                weights[part, lanes_low] = jnp.where(mask, flux_lo[h : h + 1, :], 0.0).astype(
+                    jnp.bfloat16
+                )
+        product = lax.dot_general(
+            hot_rows[...],
+            weights[...],
+            (((1,), (1,)), ((), ())),
+            preferred_element_type=jnp.float32,
+        )
+        if step == 0:
+            acc[...] = product
+        else:
+            acc[...] += product
+    odd = lax.rem(blade, 2)
+    above = [
+        jnp.where(odd == 0, near[groups + 2 + i], diag[groups + 2 + i]) for i in range(HALO)
+    ]
+    below = [
+        jnp.where(odd == 0, diag[groups + 2 + i], near[groups + 2 + i]) for i in range(HALO)
+    ]
+    gap = jnp.zeros((8 - 2 * HALO, 128), jnp.float32)
+    tiles = jnp.stack(
+        [
+            jnp.concatenate(
+                [v[h : h + 1] for v in above] + [gap] + [v[h : h + 1] for v in below], axis=0
+            )
+            for h in range(harm_rows)
+        ]
+    )
+    for h in range(harm_rows):
+        acc[circum : circum + 8, h * block_rows : (h + 1) * block_rows] += tiles[h]
+    for i, out in enumerate(outs):
+        h = lax.bitwise_xor(span, i)
+        lanes = pl.ds(pl.multiple_of(h * block_rows, block_rows), block_rows)
+        out[0:circum, :] = adj[h] + acc[0:circum, lanes]
+        out[circum : circum + 8, :] = acc[circum : circum + 8, lanes]
+
+
+def right_pieces(adj_source, messages):
+    harm_rows, circum, block_rows = adj_source.shape
+    faces = (messages[0].shape[0] - 2) * 128
+    piece = jax.ShapeDtypeStruct((circum + 8, block_rows), jnp.float32)
+    return pl.pallas_call(
+        right_kernel,
+        out_shape=(piece,) * harm_rows,
+        in_specs=[VMEM] * 5,
+        out_specs=(VMEM,) * harm_rows,
+        scratch_shapes=[
+            pltpu.VMEM((circum + 16, 2 * faces), jnp.bfloat16),
+            pltpu.VMEM((harm_rows * block_rows, 2 * faces), jnp.bfloat16),
+            pltpu.VMEM((circum + 16, harm_rows * block_rows), jnp.float32),
+        ],
+        compiler_params=params(),
+        cost_estimate=pl.CostEstimate(
+            flops=5_000_000_000, bytes_accessed=3 << 20, transcendentals=0
+        ),
+        name="right_side",
+    )(adj_source, *messages)
+
+
+def sweep_kernel(*refs):
+    count = lax.axis_size("span")
+    pieces, (mine, partner) = refs[:count], refs[count : count + 2]
+    outs = refs[count + 2 : 2 * count + 2]
+    right, weights, solved = refs[2 * count + 2 :]
+    span = lax.axis_index("span")
+    circum, block_rows = outs[0].shape
+    rows = right.shape[1]
+    for i in range(count):
+        k = lax.bitwise_xor(span, i)
+        right[k, 0 : circum + 8, :] = pieces[i][...]
+        right[k, circum + 8 : circum + 16, :] = pieces[i][circum : circum + 8, :]
+        blocks = (mine, partner)[i % 2]
+        for part in range(2):
+            hi, lo = split(blocks[i // 2, part * block_rows : (part + 1) * block_rows, :])
+            lanes = slice(part * block_rows, (part + 1) * block_rows)
+            weights[k, 0:block_rows, lanes] = hi
+            weights[k, block_rows : 2 * block_rows, lanes] = lo
+
+    def solve(rhs, below, k):
+        rhs_hi, rhs_lo = split(rhs)
+        below_hi, below_lo = split(below)
+        left = jnp.concatenate(
+            [
+                jnp.concatenate([rhs_hi, below_hi], axis=1),
+                jnp.concatenate([rhs_lo, below_lo], axis=1),
+            ],
+            axis=0,
+        )
+        product = lax.dot_general(
+            left, weights[k], (((1,), (1,)), ((), ())), preferred_element_type=jnp.float32
+        )
+        high, low = product[:rows], product[rows:]
+        return (high[:, :block_rows] + (low[:, :block_rows] + high[:, block_rows:])) + low[
+            :, block_rows:
+        ]
+
+    fields = [jnp.zeros((rows, block_rows), jnp.float32)] * ITERS
+    for k in range(count):
+        rhs = right[k]
+        base = rhs
+        for sweep in range(ITERS):
+            if sweep > 0:
+                field = fields[sweep - 1]
+                around = pltpu.roll(field, 1, 0) + pltpu.roll(field, rows - 1, 0)
+                rhs = base + coupling * around
+            fields[sweep] = solve(rhs, fields[sweep], k)
+        solved[k] = fields[-1][:circum]
+    for i in range(count):
+        outs[i][...] = solved[lax.bitwise_xor(span, i)]
+
+
+def sweep_pieces(pieces, mine, partner):
+    count = len(pieces)
+    rows, block_rows = pieces[0].shape
+    circum = rows - 8
+    piece = jax.ShapeDtypeStruct((circum, block_rows), jnp.float32)
+    return pl.pallas_call(
+        sweep_kernel,
+        out_shape=(piece,) * count,
+        in_specs=[VMEM] * (count + 2),
+        out_specs=(VMEM,) * count,
+        scratch_shapes=[
+            pltpu.VMEM((count, circum + 16, block_rows), jnp.float32),
+            pltpu.VMEM((count, 2 * block_rows, 2 * block_rows), jnp.bfloat16),
+            pltpu.VMEM((count, circum, block_rows), jnp.float32),
+        ],
+        compiler_params=params(),
+        cost_estimate=pl.CostEstimate(
+            flops=2_000_000_000, bytes_accessed=3 << 20, transcendentals=0
+        ),
+        name="sweeps",
+    )(*pieces, mine, partner)
+
+
+def place_kernel(*refs):
+    pieces, out = refs[:-1], refs[-1]
+    span = lax.axis_index("span")
+    for i, piece in enumerate(pieces):
+        out[lax.bitwise_xor(span, i)] = piece[...]
+
+
+def place(pieces):
+    return pl.pallas_call(
+        place_kernel,
+        out_shape=jax.ShapeDtypeStruct((len(pieces), *pieces[0].shape), jnp.float32),
+        in_specs=[VMEM] * len(pieces),
+        out_specs=VMEM,
+        compiler_params=params(),
+        cost_estimate=pl.CostEstimate(flops=0, bytes_accessed=2 << 20, transcendentals=0),
+        name="place",
+    )(*pieces)
+
+
+def exchange(array, axis, bits):
+    count = lax.axis_size(axis)
+    return lax.ppermute(array, axis, [(i, i ^ bits) for i in range(count)])
+
+
+def by_harmonics(adj_source, face_flux, face_owner, face_cell, block_inverse, carry_gain):
+    count = lax.axis_size("span")
+    near, far, diag = pack(adj_source, face_flux, face_owner, face_cell)
+    operators = jnp.concatenate([block_inverse, carry_gain], axis=0)
+    messages = [
+        far,
+        exchange(near, "blade", 1),
+        exchange(far, "blade", 2),
+        exchange(diag, "blade", 3),
+    ]
+    mine = jnp.stack(
+        [operators] + [exchange(operators, "span", bits) for bits in range(2, count, 2)]
+    )
+    partner = exchange(mine, "span", 1)
+    pieces = right_pieces(adj_source, messages)
+    pieces = [p if i == 0 else exchange(p, "span", i) for i, p in enumerate(pieces)]
+    pieces = sweep_pieces(pieces, mine, partner)
+    pieces = [p if i == 0 else exchange(p, "span", i) for i, p in enumerate(pieces)]
+    return place(pieces)
 
 def extended(block, sides, width):
     for axis, dim in sides:
@@ -51,7 +327,7 @@
     return right_side + coupling * (widened[:, :-2, :] + widened[:, 2:, :])
 
 
-def body(adj_source, face_flux, face_owner, face_cell, block_inverse, carry_gain):
+def by_lines(adj_source, face_flux, face_owner, face_cell, block_inverse, carry_gain):
     harm_rows, circum, block_rows = adj_source.shape
     blades = lax.axis_size("blade")
     faces_dev = face_owner.shape[0]
@@ -98,6 +374,13 @@
     return field
 
 
+def body(adj_source, *others):
+    harm_rows, circum, block_rows = adj_source.shape
+    if lax.axis_size("span") == harm_rows == 8 and lax.axis_size("blade") == 4:
+        return by_harmonics(adj_source, *others)
+    return by_lines(adj_source, *others)
+
+
 def solution(mesh):
     in_specs = (
         P(None, "blade", "span"),

time: 338 us -> 86.2 us (0.26)
  the two profiles are of different devices: /device:TPU:0 before, /device:TPU:9 now
where the time goes in v1:
time: 86.2 us; the launch traced here: 86 us
  waiting for transfers between devices  40.7 us (47%)
  starting transfers between devices  29.7 us (34%)
  Pallas kernels  13.4 us (16%)
  local copies, waits for them, and re-layouts  2.13 us (2%)
    ppermute x21, waiting for transfers between devices, exchange(): return lax.ppermute(array, axis, [(i, i ^ bits) for i in range(count)])  40.7 us
    ppermute x21, starting transfers between devices, exchange(): return lax.ppermute(array, axis, [(i, i ^ bits) for i in range(count)])  29.7 us
    pallas_call x1, Pallas kernels, right_pieces(): pl.pallas_call(right_kernel, out_shape=(piece,) * harm_rows, in_specs=[VM...  8.25 us
    pallas_call x1, Pallas kernels, sweep_pieces(): pl.pallas_call(sweep_kernel, out_shape=(piece,) * count, in_specs=[VMEM]...  4.04 us
    unnamed x13, local copies, waits for them, and re-layouts  2.12 us
  transfers between devices with their start and end apart: 21, of which 11 were waited for; matrix products, arithmetic and copies ran while one was open for 0% of the time, Pallas kernels for 10%

profile of v1, /device:TPU:9, one launch (start us, length us, event | category | flops | bytes accessed | tf_op | source)
XLA Modules:
  0.0 86.0 jit_solution(16640181780813992379)
XLA Ops:
  0.9 1.4 %collective-permute-start.12 = (f32[256,128]{1,0:T(8,128)S(1)}, f32[256,128]{1,0:T(8,128)S(1)}, u32[]{:S(2)}, u32[]{:S(2)}) collective-permute-start(f32[256,128]{1,0:T(8,128)S(1)} %constant_dynamic-update-slice_fusion), channel_id=1, source_target_pairs={{0,6},{1,7},{2,4},{3,5},{4,2},{5,3},{6,0},{7,1},{8,14},{9,15},{10,... | collective-permute-start | bytes 393224 | tf_op jit(solution)/shard_map/ppermute | solution.py:266
  4.5 1.2 %copy-done = f32[8,256,128]{2,1,0:T(8,128)S(1)} copy-done((f32[8,256,128]{2,1,0:T(8,128)S(1)}, f32[8,256,128]{2,1,0:T(8,128)}, u32[]{:S(2)}) %copy-start) | copy-done | bytes 1048600
  5.8 1.3 %collective-permute-start.1 = (f32[10,8,128]{2,1,0:T(8,128)S(1)}, f32[10,8,128]{2,1,0:T(8,128)S(1)}, u32[]{:S(2)}, u32[]{:S(2)}) collective-permute-start(f32[10,8,128]{2,1,0:T(8,128)S(1)} %get-tuple-element.24.own), channel_id=1, source_target_pairs={{0,16},{8,24},{16,0},{24,8},{1,17},{9,25},{17,1},{25,9},{2,18},{10... | collective-permute-start | bytes 122888 | tf_op jit(solution)/shard_map/ppermute | solution.py:266
  7.1 1.2 %collective-permute-start = (f32[12,8,128]{2,1,0:T(8,128)S(1)}, f32[12,8,128]{2,1,0:T(8,128)S(1)}, u32[]{:S(2)}, u32[]{:S(2)}) collective-permute-start(f32[12,8,128]{2,1,0:T(8,128)S(1)} %get-tuple-element.25), channel_id=1, source_target_pairs={{0,8},{8,0},{16,24},{24,16},{1,9},{9,1},{17,25},{25,17},{2,10},{10... | collective-permute-start | bytes 147464 | tf_op jit(solution)/shard_map/ppermute | solution.py:266
  8.3 2.9 %collective-permute-done.12 = f32[256,128]{1,0:T(8,128)S(1)} collective-permute-done((f32[256,128]{1,0:T(8,128)S(1)}, f32[256,128]{1,0:T(8,128)S(1)}, u32[]{:S(2)}, u32[]{:S(2)}) %collective-permute-start.12) | collective-permute-done | bytes 131104 | tf_op jit(solution)/shard_map/ppermute | solution.py:266
  11.2 2.1 %collective-permute-start.2 = (f32[12,8,128]{2,1,0:T(8,128)S(1)}, f32[12,8,128]{2,1,0:T(8,128)S(1)}, u32[]{:S(2)}, u32[]{:S(2)}) collective-permute-start(f32[12,8,128]{2,1,0:T(8,128)S(1)} %get-tuple-element.26), channel_id=1, source_target_pairs={{0,24},{8,16},{16,8},{24,0},{1,25},{9,17},{17,9},{25,1},{2,26},{10... | collective-permute-start | bytes 147464 | tf_op jit(solution)/shard_map/ppermute | solution.py:266
  13.3 2.8 %collective-permute-start.13 = (f32[4,256,128]{2,1,0:T(8,128)S(1)}, f32[4,256,128]{2,1,0:T(8,128)S(1)}, u32[]{:S(2)}, u32[]{:S(2)}) collective-permute-start(f32[4,256,128]{2,1,0:T(8,128)S(1)} %pad_maximum_fusion.refs_8_), channel_id=1, source_target_pairs={{0,1},{1,0},{2,3},{3,2},{4,5},{5,4},{6,7},{7,6},{8,9},{9,8},{10,11... | collective-permute-start | bytes 1572872 | tf_op jit(solution)/shard_map/ppermute | solution.py:266
  16.1 8.2 %right_side.1 = (f32[264,128]{1,0:T(8,128)S(1)}, f32[264,128]{1,0:T(8,128)S(1)}, f32[264,128]{1,0:T(8,128)S(1)}, f32[264,128]{1,0:T(8,128)S(1)}, f32[264,128]{1,...) custom-call(f32[8,256,128]{2,1,0:T(8,128)S(1)} %copy-done.1, ...), custom_call_target="tpu_custom_call" | custom-call | flops 5000000000 | bytes 3145728 | tf_op jit(solution)/shard_map/right_side/pallas_call | solution.py:152
  24.3 2.5 %collective-permute-start.3 = (f32[264,128]{1,0:T(8,128)S(1)}, f32[264,128]{1,0:T(8,128)S(1)}, u32[]{:S(2)}, u32[]{:S(2)}) collective-permute-start(f32[264,128]{1,0:T(8,128)S(1)} %get-tuple-element.28), channel_id=1, source_target_pairs={{0,1},{1,0},{2,3},{3,2},{4,5},{5,4},{6,7},{7,6},{8,9},{9,8},{10,11... | collective-permute-start | bytes 405512 | tf_op jit(solution)/shard_map/ppermute | solution.py:266
  26.8 1.7 %collective-permute-start.5 = (f32[264,128]{1,0:T(8,128)S(1)}, f32[264,128]{1,0:T(8,128)S(1)}, u32[]{:S(2)}, u32[]{:S(2)}) collective-permute-start(f32[264,128]{1,0:T(8,128)S(1)} %get-tuple-element.30), channel_id=1, source_target_pairs={{0,3},{1,2},{2,1},{3,0},{4,7},{5,6},{6,5},{7,4},{8,11},{9,10},{10,... | collective-permute-start | bytes 405512 | tf_op jit(solution)/shard_map/ppermute | solution.py:266
  29.5 1.7 %collective-permute-start.7 = (f32[264,128]{1,0:T(8,128)S(1)}, f32[264,128]{1,0:T(8,128)S(1)}, u32[]{:S(2)}, u32[]{:S(2)}) collective-permute-start(f32[264,128]{1,0:T(8,128)S(1)} %get-tuple-element.32), channel_id=1, source_target_pairs={{0,5},{1,4},{2,7},{3,6},{4,1},{5,0},{6,3},{7,2},{8,13},{9,12},{10,... | collective-permute-start | bytes 405512 | tf_op jit(solution)/shard_map/ppermute | solution.py:266
  32.0 1.5 %collective-permute-start.8 = (f32[264,128]{1,0:T(8,128)S(1)}, f32[264,128]{1,0:T(8,128)S(1)}, u32[]{:S(2)}, u32[]{:S(2)}) collective-permute-start(f32[264,128]{1,0:T(8,128)S(1)} %get-tuple-element.33), channel_id=1, source_target_pairs={{0,6},{1,7},{2,4},{3,5},{4,2},{5,3},{6,0},{7,1},{8,14},{9,15},{10,... | collective-permute-start | bytes 405512 | tf_op jit(solution)/shard_map/ppermute | solution.py:266
  33.4 4.7 %collective-permute-done.5.refs_3_ = f32[264,128]{1,0:T(8,128)S(1)} collective-permute-done((f32[264,128]{1,0:T(8,128)S(1)}, f32[264,128]{1,0:T(8,128)S(1)}, u32[]{:S(2)}, u32[]{:S(2)}) %collective-permute-start.5) | collective-permute-done | bytes 135200 | tf_op jit(solution)/shard_map/ppermute | solution.py:266
  39.2 7.3 %collective-permute-done.7.refs_5_ = f32[264,128]{1,0:T(8,128)S(1)} collective-permute-done((f32[264,128]{1,0:T(8,128)S(1)}, f32[264,128]{1,0:T(8,128)S(1)}, u32[]{:S(2)}, u32[]{:S(2)}) %collective-permute-start.7) | collective-permute-done | bytes 135200 | tf_op jit(solution)/shard_map/ppermute | solution.py:266
  46.5 4.9 %collective-permute-done.8.refs_6_ = f32[264,128]{1,0:T(8,128)S(1)} collective-permute-done((f32[264,128]{1,0:T(8,128)S(1)}, f32[264,128]{1,0:T(8,128)S(1)}, u32[]{:S(2)}, u32[]{:S(2)}) %collective-permute-start.8) | collective-permute-done | bytes 135200 | tf_op jit(solution)/shard_map/ppermute | solution.py:266
  51.4 2.9 %collective-permute-done.9.refs_7_ = f32[264,128]{1,0:T(8,128)S(1)} collective-permute-done((f32[264,128]{1,0:T(8,128)S(1)}, f32[264,128]{1,0:T(8,128)S(1)}, u32[]{:S(2)}, u32[]{:S(2)}) %collective-permute-start.9) | collective-permute-done | bytes 135200 | tf_op jit(solution)/shard_map/ppermute | solution.py:266
  54.3 4.0 %sweeps.1 = (f32[256,128]{1,0:T(8,128)S(1)}, f32[256,128]{1,0:T(8,128)S(1)}, f32[256,128]{1,0:T(8,128)S(1)}, f32[256,128]{1,0:T(8,128)S(1)}, f32[256,128]{1,0:T(...) custom-call(f32[264,128]{1,0:T(8,128)S(1)} %get-tuple-element.27.refs_0_, ...), custom_call_target="tpu_custom_call" | custom-call | flops 2000000000 | bytes 3145728 | tf_op jit(solution)/shard_map/sweeps/pallas_call | solution.py:227
  58.8 1.7 %collective-permute-start.16 = (f32[256,128]{1,0:T(8,128)S(1)}, f32[256,128]{1,0:T(8,128)S(1)}, u32[]{:S(2)}, u32[]{:S(2)}) collective-permute-start(f32[256,128]{1,0:T(8,128)S(1)} %get-tuple-element.38), channel_id=1, source_target_pairs={{0,3},{1,2},{2,1},{3,0},{4,7},{5,6},{6,5},{7,4},{8,11},{9,10},{10,... | collective-permute-start | bytes 393224 | tf_op jit(solution)/shard_map/ppermute | solution.py:266
  60.9 2.4 %collective-permute-start.18 = (f32[256,128]{1,0:T(8,128)S(1)}, f32[256,128]{1,0:T(8,128)S(1)}, u32[]{:S(2)}, u32[]{:S(2)}) collective-permute-start(f32[256,128]{1,0:T(8,128)S(1)} %get-tuple-element.40), channel_id=1, source_target_pairs={{0,5},{1,4},{2,7},{3,6},{4,1},{5,0},{6,3},{7,2},{8,13},{9,12},{10,... | collective-permute-start | bytes 393224 | tf_op jit(solution)/shard_map/ppermute | solution.py:266
  63.9 4.0 %collective-permute-start.20 = (f32[256,128]{1,0:T(8,128)S(1)}, f32[256,128]{1,0:T(8,128)S(1)}, u32[]{:S(2)}, u32[]{:S(2)}) collective-permute-start(f32[256,128]{1,0:T(8,128)S(1)} %get-tuple-element.42), channel_id=1, source_target_pairs={{0,7},{1,6},{2,5},{3,4},{4,3},{5,2},{6,1},{7,0},{8,15},{9,14},{10,... | collective-permute-start | bytes 393224 | tf_op jit(solution)/shard_map/ppermute | solution.py:266
  67.8 1.5 %collective-permute-done.16.refs_3_ = f32[256,128]{1,0:T(8,128)S(1)} collective-permute-done((f32[256,128]{1,0:T(8,128)S(1)}, f32[256,128]{1,0:T(8,128)S(1)}, u32[]{:S(2)}, u32[]{:S(2)}) %collective-permute-start.16) | collective-permute-done | bytes 131104 | tf_op jit(solution)/shard_map/ppermute | solution.py:266
  69.4 8.3 %collective-permute-done.18.refs_5_ = f32[256,128]{1,0:T(8,128)S(1)} collective-permute-done((f32[256,128]{1,0:T(8,128)S(1)}, f32[256,128]{1,0:T(8,128)S(1)}, u32[]{:S(2)}, u32[]{:S(2)}) %collective-permute-start.18) | collective-permute-done | bytes 131104 | tf_op jit(solution)/shard_map/ppermute | solution.py:266
  77.7 4.2 %collective-permute-done.19.refs_6_ = f32[256,128]{1,0:T(8,128)S(1)} collective-permute-done((f32[256,128]{1,0:T(8,128)S(1)}, f32[256,128]{1,0:T(8,128)S(1)}, u32[]{:S(2)}, u32[]{:S(2)}) %collective-permute-start.19) | collective-permute-done | bytes 131104 | tf_op jit(solution)/shard_map/ppermute | solution.py:266
  81.9 3.1 %collective-permute-done.20.refs_7_ = f32[256,128]{1,0:T(8,128)S(1)} collective-permute-done((f32[256,128]{1,0:T(8,128)S(1)}, f32[256,128]{1,0:T(8,128)S(1)}, u32[]{:S(2)}, u32[]{:S(2)}) %collective-permute-start.20) | collective-permute-done | bytes 131104 | tf_op jit(solution)/shard_map/ppermute | solution.py:266
  (37 shorter events, 8.5 us)
Async XLA Ops:
  0.9 3.6 %copy-start.2 = (f32[8,1024]{1,0:T(8,128)S(1)}, f32[8,1024]{1,0:T(8,128)}, u32[]{:S(2)}) copy-start(f32[8,1024]{1,0:T(8,128)} %flux.1) | copy-start | bytes 98308
  0.9 3.6 %copy-start.3 = (s32[1024]{0:T(1024)S(1)}, s32[1024]{0:T(1024)}, u32[]{:S(2)}) copy-start(s32[1024]{0:T(1024)} %param.8) | copy-start | bytes 12292
  0.9 10.2 %collective-permute-start.12 = (f32[256,128]{1,0:T(8,128)S(1)}, f32[256,128]{1,0:T(8,128)S(1)}, u32[]{:S(2)}, u32[]{:S(2)}) collective-permute-start(f32[256,128]{1,0:T(8,128)S(1)} %constant_dynamic-update-slice_fusion), channel_id=1, source_target_pairs={{0,6},{1,7},{2,4},{3,5},{4,2},{5,3},{6,0},{7,1},{8,14},{9,15},{10,... | collective-permute-start | bytes 393224 | tf_op jit(solution)/shard_map/ppermute | solution.py:266
  2.3 11.0 %collective-permute-start.11 = (f32[256,128]{1,0:T(8,128)S(1)}, f32[256,128]{1,0:T(8,128)S(1)}, u32[]{:S(2)}, u32[]{:S(2)}) collective-permute-start(f32[256,128]{1,0:T(8,128)S(1)} %constant_dynamic-update-slice_fusion), channel_id=1, source_target_pairs={{0,4},{1,5},{2,6},{3,7},{4,0},{5,1},{6,2},{7,3},{8,12},{9,13},{10,... | collective-permute-start | bytes 393224 | tf_op jit(solution)/shard_map/ppermute | solution.py:266
  3.4 9.9 %collective-permute-start.10 = (f32[256,128]{1,0:T(8,128)S(1)}, f32[256,128]{1,0:T(8,128)S(1)}, u32[]{:S(2)}, u32[]{:S(2)}) collective-permute-start(f32[256,128]{1,0:T(8,128)S(1)} %constant_dynamic-update-slice_fusion), channel_id=1, source_target_pairs={{0,2},{1,3},{2,0},{3,1},{4,6},{5,7},{6,4},{7,5},{8,10},{9,11},{10,... | collective-permute-start | bytes 393224 | tf_op jit(solution)/shard_map/ppermute | solution.py:266
  5.8 10.3 %copy-start.1 = (f32[8,256,128]{2,1,0:T(8,128)S(1)}, f32[8,256,128]{2,1,0:T(8,128)}, u32[]{:S(2)}) copy-start(f32[8,256,128]{2,1,0:T(8,128)} %adj.1) | copy-start | bytes 3145732
  5.8 10.3 %collective-permute-start.1 = (f32[10,8,128]{2,1,0:T(8,128)S(1)}, f32[10,8,128]{2,1,0:T(8,128)S(1)}, u32[]{:S(2)}, u32[]{:S(2)}) collective-permute-start(f32[10,8,128]{2,1,0:T(8,128)S(1)} %get-tuple-element.24.own), channel_id=1, source_target_pairs={{0,16},{8,24},{16,0},{24,8},{1,17},{9,25},{17,1},{25,9},{2,18},{10... | collective-permute-start | bytes 122888 | tf_op jit(solution)/shard_map/ppermute | solution.py:266
  7.1 9.0 %collective-permute-start = (f32[12,8,128]{2,1,0:T(8,128)S(1)}, f32[12,8,128]{2,1,0:T(8,128)S(1)}, u32[]{:S(2)}, u32[]{:S(2)}) collective-permute-start(f32[12,8,128]{2,1,0:T(8,128)S(1)} %get-tuple-element.25), channel_id=1, source_target_pairs={{0,8},{8,0},{16,24},{24,16},{1,9},{9,1},{17,25},{25,17},{2,10},{10... | collective-permute-start | bytes 147464 | tf_op jit(solution)/shard_map/ppermute | solution.py:266
  11.2 4.9 %collective-permute-start.2 = (f32[12,8,128]{2,1,0:T(8,128)S(1)}, f32[12,8,128]{2,1,0:T(8,128)S(1)}, u32[]{:S(2)}, u32[]{:S(2)}) collective-permute-start(f32[12,8,128]{2,1,0:T(8,128)S(1)} %get-tuple-element.26), channel_id=1, source_target_pairs={{0,24},{8,16},{16,8},{24,0},{1,25},{9,17},{17,9},{25,1},{2,26},{10... | collective-permute-start | bytes 147464 | tf_op jit(solution)/shard_map/ppermute | solution.py:266
  13.3 41.0 %collective-permute-start.13 = (f32[4,256,128]{2,1,0:T(8,128)S(1)}, f32[4,256,128]{2,1,0:T(8,128)S(1)}, u32[]{:S(2)}, u32[]{:S(2)}) collective-permute-start(f32[4,256,128]{2,1,0:T(8,128)S(1)} %pad_maximum_fusion.refs_8_), channel_id=1, source_target_pairs={{0,1},{1,0},{2,3},{3,2},{4,5},{5,4},{6,7},{7,6},{8,9},{9,8},{10,11... | collective-permute-start | bytes 1572872 | tf_op jit(solution)/shard_map/ppermute | solution.py:266
  24.3 5.2 %collective-permute-start.3 = (f32[264,128]{1,0:T(8,128)S(1)}, f32[264,128]{1,0:T(8,128)S(1)}, u32[]{:S(2)}, u32[]{:S(2)}) collective-permute-start(f32[264,128]{1,0:T(8,128)S(1)} %get-tuple-element.28), channel_id=1, source_target_pairs={{0,1},{1,0},{2,3},{3,2},{4,5},{5,4},{6,7},{7,6},{8,9},{9,8},{10,11... | collective-permute-start | bytes 405512 | tf_op jit(solution)/shard_map/ppermute | solution.py:266
  26.8 5.2 %collective-permute-start.4 = (f32[264,128]{1,0:T(8,128)S(1)}, f32[264,128]{1,0:T(8,128)S(1)}, u32[]{:S(2)}, u32[]{:S(2)}) collective-permute-start(f32[264,128]{1,0:T(8,128)S(1)} %get-tuple-element.29), channel_id=1, source_target_pairs={{0,2},{1,3},{2,0},{3,1},{4,6},{5,7},{6,4},{7,5},{8,10},{9,11},{10,... | collective-permute-start | bytes 405512 | tf_op jit(solution)/shard_map/ppermute | solution.py:266
  26.8 11.4 %collective-permute-start.5 = (f32[264,128]{1,0:T(8,128)S(1)}, f32[264,128]{1,0:T(8,128)S(1)}, u32[]{:S(2)}, u32[]{:S(2)}) collective-permute-start(f32[264,128]{1,0:T(8,128)S(1)} %get-tuple-element.30), channel_id=1, source_target_pairs={{0,3},{1,2},{2,1},{3,0},{4,7},{5,6},{6,5},{7,4},{8,11},{9,10},{10,... | collective-permute-start | bytes 405512 | tf_op jit(solution)/shard_map/ppermute | solution.py:266
  28.5 10.7 %collective-permute-start.6 = (f32[264,128]{1,0:T(8,128)S(1)}, f32[264,128]{1,0:T(8,128)S(1)}, u32[]{:S(2)}, u32[]{:S(2)}) collective-permute-start(f32[264,128]{1,0:T(8,128)S(1)} %get-tuple-element.31), channel_id=1, source_target_pairs={{0,4},{1,5},{2,6},{3,7},{4,0},{5,1},{6,2},{7,3},{8,12},{9,13},{10,... | collective-permute-start | bytes 405512 | tf_op jit(solution)/shard_map/ppermute | solution.py:266
  29.5 17.0 %collective-permute-start.7 = (f32[264,128]{1,0:T(8,128)S(1)}, f32[264,128]{1,0:T(8,128)S(1)}, u32[]{:S(2)}, u32[]{:S(2)}) collective-permute-start(f32[264,128]{1,0:T(8,128)S(1)} %get-tuple-element.32), channel_id=1, source_target_pairs={{0,5},{1,4},{2,7},{3,6},{4,1},{5,0},{6,3},{7,2},{8,13},{9,12},{10,... | collective-permute-start | bytes 405512 | tf_op jit(solution)/shard_map/ppermute | solution.py:266
  32.0 19.4 %collective-permute-start.8 = (f32[264,128]{1,0:T(8,128)S(1)}, f32[264,128]{1,0:T(8,128)S(1)}, u32[]{:S(2)}, u32[]{:S(2)}) collective-permute-start(f32[264,128]{1,0:T(8,128)S(1)} %get-tuple-element.33), channel_id=1, source_target_pairs={{0,6},{1,7},{2,4},{3,5},{4,2},{5,3},{6,0},{7,1},{8,14},{9,15},{10,... | collective-permute-start | bytes 405512 | tf_op jit(solution)/shard_map/ppermute | solution.py:266
  38.2 16.1 %collective-permute-start.9 = (f32[264,128]{1,0:T(8,128)S(1)}, f32[264,128]{1,0:T(8,128)S(1)}, u32[]{:S(2)}, u32[]{:S(2)}) collective-permute-start(f32[264,128]{1,0:T(8,128)S(1)} %get-tuple-element.34), channel_id=1, source_target_pairs={{0,7},{1,6},{2,5},{3,4},{4,3},{5,2},{6,1},{7,0},{8,15},{9,14},{10,... | collective-permute-start | bytes 405512 | tf_op jit(solution)/shard_map/ppermute | solution.py:266
  58.3 4.9 %collective-permute-start.14 = (f32[256,128]{1,0:T(8,128)S(1)}, f32[256,128]{1,0:T(8,128)S(1)}, u32[]{:S(2)}, u32[]{:S(2)}) collective-permute-start(f32[256,128]{1,0:T(8,128)S(1)} %get-tuple-element.36), channel_id=1, source_target_pairs={{0,1},{1,0},{2,3},{3,2},{4,5},{5,4},{6,7},{7,6},{8,9},{9,8},{10,11... | collective-permute-start | bytes 393224 | tf_op jit(solution)/shard_map/ppermute | solution.py:266
  58.8 5.1 %collective-permute-start.15 = (f32[256,128]{1,0:T(8,128)S(1)}, f32[256,128]{1,0:T(8,128)S(1)}, u32[]{:S(2)}, u32[]{:S(2)}) collective-permute-start(f32[256,128]{1,0:T(8,128)S(1)} %get-tuple-element.37), channel_id=1, source_target_pairs={{0,2},{1,3},{2,0},{3,1},{4,6},{5,7},{6,4},{7,5},{8,10},{9,11},{10,... | collective-permute-start | bytes 393224 | tf_op jit(solution)/shard_map/ppermute | solution.py:266
  58.8 10.5 %collective-permute-start.16 = (f32[256,128]{1,0:T(8,128)S(1)}, f32[256,128]{1,0:T(8,128)S(1)}, u32[]{:S(2)}, u32[]{:S(2)}) collective-permute-start(f32[256,128]{1,0:T(8,128)S(1)} %get-tuple-element.38), channel_id=1, source_target_pairs={{0,3},{1,2},{2,1},{3,0},{4,7},{5,6},{6,5},{7,4},{8,11},{9,10},{10,... | collective-permute-start | bytes 393224 | tf_op jit(solution)/shard_map/ppermute | solution.py:266
  60.5 8.8 %collective-permute-start.17 = (f32[256,128]{1,0:T(8,128)S(1)}, f32[256,128]{1,0:T(8,128)S(1)}, u32[]{:S(2)}, u32[]{:S(2)}) collective-permute-start(f32[256,128]{1,0:T(8,128)S(1)} %get-tuple-element.39), channel_id=1, source_target_pairs={{0,4},{1,5},{2,6},{3,7},{4,0},{5,1},{6,2},{7,3},{8,12},{9,13},{10,... | collective-permute-start | bytes 393224 | tf_op jit(solution)/shard_map/ppermute | solution.py:266
  60.9 16.8 %collective-permute-start.18 = (f32[256,128]{1,0:T(8,128)S(1)}, f32[256,128]{1,0:T(8,128)S(1)}, u32[]{:S(2)}, u32[]{:S(2)}) collective-permute-start(f32[256,128]{1,0:T(8,128)S(1)} %get-tuple-element.40), channel_id=1, source_target_pairs={{0,5},{1,4},{2,7},{3,6},{4,1},{5,0},{6,3},{7,2},{8,13},{9,12},{10,... | collective-permute-start | bytes 393224 | tf_op jit(solution)/shard_map/ppermute | solution.py:266
  63.2 18.6 %collective-permute-start.19 = (f32[256,128]{1,0:T(8,128)S(1)}, f32[256,128]{1,0:T(8,128)S(1)}, u32[]{:S(2)}, u32[]{:S(2)}) collective-permute-start(f32[256,128]{1,0:T(8,128)S(1)} %get-tuple-element.41), channel_id=1, source_target_pairs={{0,6},{1,7},{2,4},{3,5},{4,2},{5,3},{6,0},{7,1},{8,14},{9,15},{10,... | collective-permute-start | bytes 393224 | tf_op jit(solution)/shard_map/ppermute | solution.py:266
  63.9 21.1 %collective-permute-start.20 = (f32[256,128]{1,0:T(8,128)S(1)}, f32[256,128]{1,0:T(8,128)S(1)}, u32[]{:S(2)}, u32[]{:S(2)}) collective-permute-start(f32[256,128]{1,0:T(8,128)S(1)} %get-tuple-element.42), channel_id=1, source_target_pairs={{0,7},{1,6},{2,5},{3,4},{4,3},{5,2},{6,1},{7,0},{8,15},{9,14},{10,... | collective-permute-start | bytes 393224 | tf_op jit(solution)/shard_map/ppermute | solution.py:266
  (3 other events, 5.7 us)

commit v2 on v0

--- a/solution.py
+++ b/solution.py
@@ -1,13 +1,429 @@
+import functools
+
 import jax
 import jax.numpy as jnp
 from jax import lax
+from jax.experimental import pallas as pl
+from jax.experimental.pallas import tpu as pltpu
 from jax.sharding import PartitionSpec as P
 
 ITERS = 3
-
+HALO = ITERS - 1
 
 coupling = 0.05
 highest = lax.Precision.HIGHEST
+VMEM = pl.BlockSpec(memory_space=pltpu.VMEM)
+ANY = pl.BlockSpec(memory_space=pl.ANY)
+HBM = pl.BlockSpec(memory_space=pltpu.HBM)
+F32 = jnp.float32
+BF16 = jnp.bfloat16
+
+
+def call(kernel, outs, ins, scratch, flops, name, out_specs=None, vmem=24):
+    shapes = tuple(jax.ShapeDtypeStruct(shape, dtype) for shape, dtype in outs)
+    return pl.pallas_call(
+        kernel,
+        out_shape=shapes,
+        in_specs=ins,
+        out_specs=out_specs or (VMEM,) * len(outs),
+        scratch_shapes=scratch,
+        compiler_params=pltpu.CompilerParams(vmem_limit_bytes=vmem * 1024 * 1024),
+        cost_estimate=pl.CostEstimate(flops=flops, bytes_accessed=1 << 20, transcendentals=0),
+        name=name,
+    )
+
+
+def split(x):
+    hi = x.astype(BF16)
+    return hi, (x - hi.astype(F32)).astype(BF16)
+
+
+def peer(i):
+    return lax.bitwise_xor(lax.axis_index("span"), i)
+
+
+def pack_kernel(flux, owner, cell, adj, inverse, gain, near, far, diag, operators, *scratch):
+    faces, owners, cells, first, last, sems = scratch
+    groups, circum, block_rows = owner.shape[0], adj.shape[1], inverse.shape[0]
+    odd = lax.rem(lax.axis_index("blade"), 2)
+    pairs = (
+        (flux, faces),
+        (owner, owners),
+        (cell, cells),
+        (adj.at[:, 0:8, :], first),
+        (adj.at[:, circum - 8 : circum, :], last),
+        (inverse, operators.at[0:block_rows, :]),
+        (gain, operators.at[block_rows : 2 * block_rows, :]),
+    )
+    copies = [pltpu.make_async_copy(a, b, sems.at[i]) for i, (a, b) in enumerate(pairs)]
+    for copy in copies:
+        copy.start()
+    for copy in copies:
+        copy.wait()
+    for message in (near, far, diag):
+        for group in range(groups):
+            message[group] = faces[:, group * 128 : (group + 1) * 128]
+        message[groups] = owners[...].astype(F32)
+        message[groups + 1] = cells[...].astype(F32)
+    for row in range(HALO):
+        low = first[:, row, :]
+        high = last[:, 8 - HALO + row, :]
+        near[groups + 2 + row] = jnp.where(odd == 0, high, low)
+        diag[groups + 2 + row] = jnp.where(odd == 0, low, high)
+
+
+def pack(adj_source, face_flux, face_owner, face_cell, block_inverse, carry_gain):
+    groups = face_owner.shape[0] // 128
+    block_rows = adj_source.shape[2]
+    with_halo = ((groups + 2 + HALO, 8, 128), F32)
+    faces = ((groups + 2, 8, 128), F32)
+    edge = pltpu.VMEM((8, 8, block_rows), F32)
+    return call(
+        pack_kernel,
+        (with_halo, faces, with_halo, ((2 * block_rows, block_rows), F32)),
+        [HBM] * 6,
+        [
+            pltpu.VMEM(face_flux.shape, F32),
+            pltpu.VMEM((groups, 128), jnp.int32),
+            pltpu.VMEM((groups, 128), jnp.int32),
+            edge,
+            edge,
+            pltpu.SemaphoreType.DMA((7,)),
+        ],
+        0,
+        "pack",
+        vmem=60,
+    )(
+        face_flux,
+        face_owner.reshape(groups, 128),
+        face_cell.reshape(groups, 128),
+        adj_source,
+        block_inverse,
+        carry_gain,
+    )
+
+
+def face_product(message, hot_rows, weights, harmonics, circum, block_rows):
+    blades = lax.axis_size("blade")
+    blade = lax.axis_index("blade")
+    total = circum * blades
+    groups = weights.shape[1] // 256
+    rows = hot_rows.shape[0]
+    row = lax.broadcasted_iota(jnp.int32, (rows, 128), 0)
+    label = jnp.where(
+        row < circum + HALO,
+        row,
+        jnp.where(
+            (row >= circum + 8 - HALO) & (row < circum + 8), row - (circum + 8) + total, -1
+        ),
+    )
+    radial = lax.broadcasted_iota(jnp.int32, (block_rows, 128), 0)
+    owner = message[groups].astype(jnp.int32)
+    cell = message[groups + 1].astype(jnp.int32)
+    place = (owner - blade) * circum + cell // block_rows
+    place = jnp.where(place < 0, place + total, place)
+    inner = cell % block_rows
+    for group in range(groups):
+        lanes = slice(group * 128, (group + 1) * 128)
+        lanes_low = slice((groups + group) * 128, (groups + group + 1) * 128)
+        hot = jnp.where(label == place[group : group + 1, :], 1.0, 0.0).astype(BF16)
+        hot_rows[:, lanes] = hot
+        hot_rows[:, lanes_low] = hot
+        hit = jnp.where(radial == inner[group : group + 1, :], 1.0, 0.0).astype(BF16)
+        hit = hit.reshape(block_rows // 16, 16, 128)
+        for at, h in enumerate(harmonics):
+            flux = jnp.broadcast_to(message[group, pl.ds(h, 1), :], (16, 128))
+            flux_hi, flux_lo = split(flux)
+            part = slice(at * block_rows, (at + 1) * block_rows)
+            weights[part, lanes] = (hit * flux_hi[None]).reshape(block_rows, 128)
+            weights[part, lanes_low] = (hit * flux_lo[None]).reshape(block_rows, 128)
+    return lax.dot_general(
+        hot_rows[...], weights[...], (((1,), (1,)), ((), ())), preferred_element_type=F32
+    )
+
+
+def own_faces_kernel(own, acc, hot_rows, weights):
+    block_rows = 128
+    circum = acc.shape[0] - 16
+    harmonics = range(acc.shape[1] // block_rows)
+    acc[...] = face_product(own, hot_rows, weights, harmonics, circum, block_rows)
+
+
+def own_faces(own, harm_rows, circum):
+    faces = (own.shape[0] - 2) * 128
+    rows, lanes = circum + 16, harm_rows * 128
+    return call(
+        own_faces_kernel,
+        (((rows, lanes), F32),),
+        [VMEM],
+        [pltpu.VMEM((rows, 2 * faces), BF16), pltpu.VMEM((lanes, 2 * faces), BF16)],
+        1_200_000_000,
+        "own_faces",
+    )(own)[0]
+
+
+def right_kernel(peers, adj, start, near, far, diag, *rest):
+    count = len(peers)
+    *outs, hot_rows, weights, acc, source, sems = rest
+    del outs[: len(outs) - count - 1]
+    outs[count][...] = jnp.zeros_like(outs[count])
+    _, circum, block_rows = adj.shape
+    copies = [
+        pltpu.make_async_copy(adj.at[peer(i)], source.at[at], sems.at[at])
+        for at, i in enumerate(peers)
+    ]
+    for copy in copies:
+        copy.start()
+    groups = weights.shape[2] // 256
+    odd = lax.rem(lax.axis_index("blade"), 2)
+    harmonics = [peer(i) for i in peers]
+    for at, h in enumerate(harmonics):
+        lanes = pl.ds(pl.multiple_of(h * block_rows, block_rows), block_rows)
+        acc[:, at * block_rows : (at + 1) * block_rows] = start[:, lanes]
+    for step, message in enumerate((near, far, diag)):
+        product = face_product(
+            message, hot_rows.at[step], weights.at[step], harmonics, circum, block_rows
+        )
+        acc[...] += product
+    gap = jnp.zeros((8 - 2 * HALO, 128), F32)
+    for copy in copies:
+        copy.wait()
+    for at, (i, out) in enumerate(zip(peers, outs[:count], strict=True)):
+        row = pl.ds(peer(i), 1)
+        one = [near[groups + 2 + j, row, :] for j in range(HALO)]
+        three = [diag[groups + 2 + j, row, :] for j in range(HALO)]
+        above = [jnp.where(odd == 0, a, b) for a, b in zip(one, three, strict=True)]
+        below = [jnp.where(odd == 0, b, a) for a, b in zip(one, three, strict=True)]
+        part = slice(at * block_rows, (at + 1) * block_rows)
+        out[0:circum, :] = source[at] + acc[0:circum, part]
+        out[circum : circum + 8, :] = acc[circum : circum + 8, part] + jnp.concatenate(
+            above + [gap] + below, axis=0
+        )
+
+
+def right_pieces(peers, adj_source, start, messages, after, name):
+    _, circum, block_rows = adj_source.shape
+    count = len(peers)
+    faces = (messages[1].shape[0] - 2) * 128
+    rows = circum + 16
+    return call(
+        functools.partial(right_kernel, peers),
+        (((circum + 8, block_rows), F32),) * count + (((8, 128), F32),),
+        [HBM] + [VMEM] * 4 + [ANY] * len(after),
+        [
+            pltpu.VMEM((3, rows, 2 * faces), BF16),
+            pltpu.VMEM((3, count * block_rows, 2 * faces), BF16),
+            pltpu.VMEM((rows, count * block_rows), F32),
+            pltpu.VMEM((count, circum, block_rows), F32),
+            pltpu.SemaphoreType.DMA((count,)),
+        ],
+        1_800_000_000,
+        name,
+    )(adj_source, start, *messages, *after)
+
+
+def solve_half(pieces, weights, first, fields, right, solved):
+    half = len(pieces)
+    rows, block_rows = right.shape[1:]
+    circum = rows - 16
+    for i, piece in enumerate(pieces):
+        k = lax.rem(peer(i), half)
+        right[k, 0 : circum + 8, :] = piece[...]
+        right[k, circum + 8 : rows, :] = piece[circum : circum + 8, :]
+
+    def solve(rhs, below, k):
+        rhs_hi, rhs_lo = split(rhs)
+        below_hi, below_lo = split(below)
+        left = jnp.concatenate(
+            [
+                jnp.concatenate([rhs_hi, below_hi], axis=1),
+                jnp.concatenate([rhs_lo, below_lo], axis=1),
+            ],
+            axis=0,
+        )
+        product = lax.dot_general(
+            left, weights[first + k], (((1,), (1,)), ((), ())), preferred_element_type=F32
+        )
+        high, low = product[:rows], product[rows:]
+        cross = low[:, :block_rows] + high[:, block_rows:]
+        return (high[:, :block_rows] + cross) + low[:, block_rows:]
+
+    fields = list(fields)
+    for k in range(half):
+        base = rhs = right[k]
+        for sweep in range(ITERS):
+            if sweep > 0:
+                field = fields[sweep - 1]
+                around = pltpu.roll(field, 1, 0) + pltpu.roll(field, rows - 1, 0)
+                rhs = base + coupling * around
+            fields[sweep] = solve(rhs, fields[sweep], k)
+        solved[k] = fields[-1][:circum]
+    return fields
+
+
+def stack_kernel(*refs):
+    *pieces, _, out = refs
+    for i, piece in enumerate(pieces):
+        out[i] = piece[...]
+
+
+def operators_kernel(mine, partner, weights):
+    block_rows = mine.shape[2]
+    for i in range(weights.shape[0]):
+        k = peer(i)
+        source = (mine, partner)[i % 2]
+        for matrix in range(2):
+            part = slice(matrix * block_rows, (matrix + 1) * block_rows)
+            hi, lo = split(source[i // 2, part, :])
+            weights[k, 0:block_rows, part] = hi
+            weights[k, block_rows : 2 * block_rows, part] = lo
+
+
+def lower_kernel(half, *refs):
+    *rest, weights, state, solved, right = refs
+    pieces = rest[len(rest) - half :]
+    upper = lax.axis_index("span") // half
+    zero = jnp.zeros(state.shape[1:], F32)
+
+    @pl.when(upper == 0)
+    def _():
+        for sweep, field in enumerate(
+            solve_half(pieces, weights, 0, [zero] * ITERS, right, solved)
+        ):
+            state[sweep] = field
+
+    @pl.when(upper != 0)
+    def _():
+        for sweep in range(ITERS):
+            state[sweep] = zero
+
+
+def far_kernel(half, *refs):
+    pieces, (weights, state) = refs[:half], refs[half : half + 2]
+    outs = refs[half + 2 : 2 * half + 2]
+    after, right, solved = refs[2 * half + 2 :]
+    upper = lax.axis_index("span") // half
+    fields = solve_half(
+        pieces, weights, (1 - upper) * half, [state[i] for i in range(ITERS)], right, solved
+    )
+    for i, out in enumerate(outs):
+        out[...] = solved[lax.rem(peer(i), half)]
+    for sweep, field in enumerate(fields):
+        after[sweep] = field
+
+
+def upper_kernel(half, *refs):
+    pieces, (weights, state, done) = refs[:half], refs[half : half + 3]
+    outs = refs[half + 3 : 2 * half + 3]
+    right, solved = refs[2 * half + 3 :]
+    upper = lax.axis_index("span") // half
+
+    @pl.when(upper == 0)
+    def _():
+        for i, out in enumerate(outs):
+            out[...] = done[lax.rem(peer(i), half)]
+
+    @pl.when(upper != 0)
+    def _():
+        solve_half(pieces, weights, half, [state[i] for i in range(ITERS)], right, solved)
+        for i, out in enumerate(outs):
+            out[...] = solved[lax.rem(peer(i), half)]
+
+
+def place_kernel(peers, *refs):
+    *pieces, out, sems = refs
+    copies = [
+        pltpu.make_async_copy(piece, out.at[peer(i)], sems.at[i])
+        for i, piece in zip(peers, pieces, strict=True)
+    ]
+    for copy in copies:
+        copy.start()
+    for copy in copies:
+        copy.wait()
+
+
+def exchange(array, axis, bits):
+    count = lax.axis_size(axis)
+    return lax.ppermute(array, axis, [(i, i ^ bits) for i in range(count)])
+
+
+def by_harmonics(adj_source, face_flux, face_owner, face_cell, block_inverse, carry_gain):
+    harm_rows, circum, block_rows = adj_source.shape
+    count = lax.axis_size("span")
+    half = count // 2
+    near, far, diag, operators = pack(
+        adj_source, face_flux, face_owner, face_cell, block_inverse, carry_gain
+    )
+    messages = [
+        exchange(near, "blade", 1),
+        exchange(far, "blade", 2),
+        exchange(diag, "blade", 3),
+    ]
+    start = own_faces(far, harm_rows, circum)
+    operators = [operators] + [exchange(operators, "span", bits) for bits in range(2, count, 2)]
+    far_peers, near_peers = range(half, count), range(half)
+    *far_right, token = right_pieces(far_peers, adj_source, start, messages, [], "right_far")
+    far_right = [exchange(p, "span", i) for p, i in zip(far_right, far_peers, strict=True)]
+    mine = call(
+        stack_kernel,
+        (((half, *operators[0].shape), F32),),
+        [VMEM] * half + [ANY],
+        [],
+        0,
+        "stack",
+    )(*operators, token)[0]
+    partner = exchange(mine, "span", 1)
+    weights = call(
+        operators_kernel,
+        (((count, 2 * block_rows, 2 * block_rows), BF16),),
+        [VMEM] * 2,
+        [],
+        0,
+        "operators",
+    )(mine, partner)[0]
+    *near_right, _ = right_pieces(near_peers, adj_source, start, messages, [token, weights], "right_near")
+    near_right = [p if i == 0 else exchange(p, "span", i) for i, p in enumerate(near_right)]
+
+    rows = circum + 16
+    right = pltpu.VMEM((half, rows, block_rows), F32)
+    solved = pltpu.VMEM((half, circum, block_rows), F32)
+    state_shape = ((ITERS, rows, block_rows), F32)
+    piece = ((circum, block_rows), F32)
+    state, done = call(
+        functools.partial(lower_kernel, half),
+        (state_shape, ((half, circum, block_rows), F32)),
+        [ANY] * 3 + [VMEM] * (half + 1),
+        [right],
+        1_000_000_000,
+        "sweeps_lower",
+    )(*far_right[:3], *near_right, weights)
+    *far_solved, state = call(
+        functools.partial(far_kernel, half),
+        (piece,) * half + (state_shape,),
+        [VMEM] * (half + 2),
+        [right, solved],
+        1_000_000_000,
+        "sweeps_far",
+    )(*far_right, weights, state)
+    far_solved = [exchange(p, "span", i) for p, i in zip(far_solved, far_peers, strict=True)]
+    near_solved = call(
+        functools.partial(upper_kernel, half),
+        (piece,) * half,
+        [VMEM] * (half + 3),
+        [right, solved],
+        1_000_000_000,
+        "sweeps_upper",
+    )(*near_right, weights, state, done)
+    near_solved = [p if i == 0 else exchange(p, "span", i) for i, p in enumerate(near_solved)]
+    return call(
+        functools.partial(place_kernel, (*far_peers, *near_peers)),
+        (((count, circum, block_rows), F32),),
+        [ANY] * count,
+        [pltpu.SemaphoreType.DMA((count,))],
+        0,
+        "place",
+        out_specs=(ANY,),
+    )(*far_solved, *near_solved)[0]
 
 
 def extended(block, sides, width):
@@ -51,7 +467,7 @@
     return right_side + coupling * (widened[:, :-2, :] + widened[:, 2:, :])
 
 
-def body(adj_source, face_flux, face_owner, face_cell, block_inverse, carry_gain):
+def by_lines(adj_source, face_flux, face_owner, face_cell, block_inverse, carry_gain):
     harm_rows, circum, block_rows = adj_source.shape
     blades = lax.axis_size("blade")
     faces_dev = face_owner.shape[0]
@@ -98,6 +514,13 @@
     return field
 
 
+def body(adj_source, *others):
+    harm_rows, circum, block_rows = adj_source.shape
+    if lax.axis_size("span") == harm_rows == 8 and lax.axis_size("blade") == 4:
+        return by_harmonics(adj_source, *others)
+    return by_lines(adj_source, *others)
+
+
 def solution(mesh):
     in_specs = (
         P(None, "blade", "span"),

time: 338 us -> 77 us (0.23)
  blocking collectives: 138 us -> 0 us
  local copies, waits for them, and re-layouts: 59.8 us -> 0.79 us
  other arithmetic: 39.4 us -> 0 us
  waiting for transfers between devices: 62.3 us -> 36.7 us
  Pallas kernels: 0 us -> 15.9 us
  matrix products: 9.59 us -> 0 us
  starting transfers between devices: 27.4 us -> 23.3 us
    all_to_all x3 -> x0, blocking collectives: 88.7 us -> none  [transposed(): lax.all_to_all(pencil_solve(pencil, blocks, gains), 'span', split_axis=2,...]
    all_to_all x5 -> x0, waiting for transfers between devices: 57.8 us -> none  [the longest x3 53 us: transposed(): lax.all_to_all(rhs_rows, 'span', split_axis=1, concat_axis=2, tiled=True)]
    all_gather x2 -> x0, blocking collectives: 49.6 us -> none  [the longest x1 34.7 us: body(): lax.all_gather(block_inverse, 'span', axis=0, tiled=True)]
    ppermute x4 -> x21, waiting for transfers between devices: 4.41 us -> 36.7 us  [exchange(): return lax.ppermute(array, axis, [(i, i ^ bits) for i in range(count)])]
    unnamed x13 -> x6, local copies, waits for them, and re-layouts: 22.6 us -> 0.79 us
    all_to_all x5 -> x0, starting transfers between devices: 21.3 us -> none  [the longest x3 12 us: transposed(): lax.all_to_all(rhs_rows, 'span', split_axis=1, concat_axis=2, tiled=True)]
    scatter-add x1 -> x0, other arithmetic: 20.4 us -> none  [body(): jnp.zeros((harm_rows, circum * block_rows), jnp.float32).at[:, cell_ids]]
    reshape x6 -> x0, local copies, waits for them, and re-layouts: 17.7 us -> none  [the longest x1 9.2 us: body(): right_side = adj_source + wall_flux.reshape(harm_rows, circum, block_rows)]
  transfers between devices with their start and end apart: 9 -> 21, of which waited for: 6 -> 10; matrix products, arithmetic and copies ran while one was open for 2% -> 0% of each run, Pallas kernels for 0% -> 14%
where the time goes in v2:
time: 77 us; the launch traced here: 76.9 us
  waiting for transfers between devices  36.7 us (48%)
  starting transfers between devices  23.3 us (30%)
  Pallas kernels  15.9 us (21%)
  local copies, waits for them, and re-layouts  0.79 us (1%)
    ppermute x21, waiting for transfers between devices, exchange(): return lax.ppermute(array, axis, [(i, i ^ bits) for i in range(count)])  36.7 us
    ppermute x21, starting transfers between devices, exchange(): return lax.ppermute(array, axis, [(i, i ^ bits) for i in range(count)])  23.3 us
    pallas_call x2, Pallas kernels, right_pieces(): call(functools.partial(right_kernel, peers), (((circum + 8, block_rows),...  6.96 us
    pallas_call x1, Pallas kernels, by_harmonics(): call(functools.partial(far_kernel, half), (piece,) * half + (state_shape,...  2.2 us
    pallas_call x1, Pallas kernels, by_harmonics(): call(functools.partial(lower_kernel, half), (state_shape, ((half, circum,...  2.11 us
    pallas_call x1, Pallas kernels, pack(): call(pack_kernel, (with_halo, faces, with_halo, ((2 * block_rows, block_r...  1.71 us
    pallas_call x1, Pallas kernels, own_faces(): call(own_faces_kernel, (((rows, lanes), F32),), [VMEM], [pltpu.VMEM((rows...  1.67 us
  transfers between devices with their start and end apart: 21, of which 10 were waited for; matrix products, arithmetic and copies ran while one was open for 0% of the time, Pallas kernels for 14%

profile of v2, /device:TPU:0, one launch (start us, length us, event | category | flops | bytes accessed | tf_op | source)
XLA Modules:
  0.0 76.9 jit_solution(4486638887775457553)
XLA Ops:
  0.0 1.7 %pack.1 = (f32[12,8,128]{2,1,0:T(8,128)}, f32[10,8,128]{2,1,0:T(8,128)}, f32[12,8,128]{2,1,0:T(8,128)}, f32[256,128]{1,0:T(8,128)}) custom-call(f32[8,1024]{1,0:T(8,128)} %flux.1, s32[8,128]{1,0:T(8,128)} %bitcast.2, s32[8,128]{1,0:T(8,128)} %bitcast.3, f32[8,256,128]{2,1,0:T(8,128)} %adj.5, f32[128,128]{1,0:T(8,128)} %inverse.1, f32[128,128]{1,0:T(8,128)} %gain.1), custom_call_target="tpu_custom_call" | custom-call | bytes 1048576 | tf_op jit(solution)/shard_map/pack/pallas_call | solution.py:81
  1.7 5.1 %collective-permute-start.9 = (f32[256,128]{1,0:T(8,128)}, f32[256,128]{1,0:T(8,128)S(1)}, u32[]{:S(2)}, u32[]{:S(2)}) collective-permute-start(f32[256,128]{1,0:T(8,128)} %get-tuple-element.36.refs_0_), channel_id=1, source_target_pairs={{0,6},{1,7},{2,4},{3,5},{4,2},{5,3},{6,0},{7,1},{8,14},{9,15},{10,... | collective-permute-start | bytes 393224 | tf_op jit(solution)/shard_map/ppermute | solution.py:347
  6.8 1.5 %collective-permute-start.1 = (f32[10,8,128]{2,1,0:T(8,128)}, f32[10,8,128]{2,1,0:T(8,128)S(1)}, u32[]{:S(2)}, u32[]{:S(2)}) collective-permute-start(f32[10,8,128]{2,1,0:T(8,128)} %get-tuple-element.29.own), channel_id=1, source_target_pairs={{0,16},{8,24},{16,0},{24,8},{1,17},{9,25},{17,1},{25,9},{2,18},{10... | collective-permute-start | bytes 122888 | tf_op jit(solution)/shard_map/ppermute | solution.py:347
  8.4 1.5 %collective-permute-start = (f32[12,8,128]{2,1,0:T(8,128)}, f32[12,8,128]{2,1,0:T(8,128)S(1)}, u32[]{:S(2)}, u32[]{:S(2)}) collective-permute-start(f32[12,8,128]{2,1,0:T(8,128)} %get-tuple-element.30), channel_id=1, source_target_pairs={{0,8},{8,0},{16,24},{24,16},{1,9},{9,1},{17,25},{25,17},{2,10},{10... | collective-permute-start | bytes 147464 | tf_op jit(solution)/shard_map/ppermute | solution.py:347
  11.1 1.7 %own_faces.1.start = f32[272,1024]{1,0:T(8,128)S(1)} custom-call(f32[10,8,128]{2,1,0:T(8,128)S(1)} %copy-done.2), custom_call_target="tpu_custom_call" | custom-call | flops 1200000000 | bytes 1048576 | tf_op jit(solution)/shard_map/own_faces/pallas_call | solution.py:155
  13.6 1.5 %collective-permute-done.2.diag = f32[12,8,128]{2,1,0:T(8,128)S(1)} collective-permute-done((f32[12,8,128]{2,1,0:T(8,128)}, f32[12,8,128]{2,1,0:T(8,128)S(1)}, u32[]{:S(2)}, u32[]{:S(2)}) %collective-permute-start.2) | collective-permute-done | bytes 49184 | tf_op jit(solution)/shard_map/ppermute | solution.py:347
  15.1 3.2 %right_far.1 = (f32[264,128]{1,0:T(8,128)S(1)}, f32[264,128]{1,0:T(8,128)S(1)}, f32[264,128]{1,0:T(8,128)S(1)}, f32[264,128]{1,0:T(8,128)S(1)}, f32[8,128]{1,0:T(8,128)S(1)}) custom-call(f32[8,256,128]{2,1,0:T(8,128)S(1)} %copy-done, f32[272,1024]{1,0:T(8,128)S(1)} %own_faces.1.start, f32[12,8,128]{2,1,0:T(8,128)S(1)} %collective-permute-done.near, ...), custom_call_target="tpu_custom_call" | custom-call | flops 1800000000 | bytes 1048576 | tf_op jit(solution)/shard_map/right_far/pallas_call | solution.py:209
  18.3 1.6 %collective-permute-done.7.refs_1_ = f32[256,128]{1,0:T(8,128)S(1)} collective-permute-done((f32[256,128]{1,0:T(8,128)S(1)}, f32[256,128]{1,0:T(8,128)S(1)}, u32[]{:S(2)}, u32[]{:S(2)}) %collective-permute-start.7) | collective-permute-done | bytes 131104 | tf_op jit(solution)/shard_map/ppermute | solution.py:347
  20.1 1.4 %collective-permute-start.3 = (f32[264,128]{1,0:T(8,128)S(1)}, f32[264,128]{1,0:T(8,128)S(1)}, u32[]{:S(2)}, u32[]{:S(2)}) collective-permute-start(f32[264,128]{1,0:T(8,128)S(1)} %get-tuple-element.32), channel_id=1, source_target_pairs={{0,4},{1,5},{2,6},{3,7},{4,0},{5,1},{6,2},{7,3},{8,12},{9,13},{10,... | collective-permute-start | bytes 405512 | tf_op jit(solution)/shard_map/ppermute | solution.py:347
  21.4 1.4 %collective-permute-start.4 = (f32[264,128]{1,0:T(8,128)S(1)}, f32[264,128]{1,0:T(8,128)S(1)}, u32[]{:S(2)}, u32[]{:S(2)}) collective-permute-start(f32[264,128]{1,0:T(8,128)S(1)} %get-tuple-element.33), channel_id=1, source_target_pairs={{0,5},{1,4},{2,7},{3,6},{4,1},{5,0},{6,3},{7,2},{8,13},{9,12},{10,... | collective-permute-start | bytes 405512 | tf_op jit(solution)/shard_map/ppermute | solution.py:347
  22.8 2.2 %collective-permute-start.5 = (f32[264,128]{1,0:T(8,128)S(1)}, f32[264,128]{1,0:T(8,128)S(1)}, u32[]{:S(2)}, u32[]{:S(2)}) collective-permute-start(f32[264,128]{1,0:T(8,128)S(1)} %get-tuple-element.34), channel_id=1, source_target_pairs={{0,6},{1,7},{2,4},{3,5},{4,2},{5,3},{6,0},{7,1},{8,14},{9,15},{10,... | collective-permute-start | bytes 405512 | tf_op jit(solution)/shard_map/ppermute | solution.py:347
  25.2 3.8 %right_near.1 = (f32[264,128]{1,0:T(8,128)S(1)}, f32[264,128]{1,0:T(8,128)S(1)}, f32[264,128]{1,0:T(8,128)S(1)}, f32[264,128]{1,0:T(8,128)S(1)}, f32[8,128]{1,0:T(8,128)}) custom-call(f32[8,256,128]{2,1,0:T(8,128)S(1)} %copy-done, f32[272,1024]{1,0:T(8,128)S(1)} %own_faces.1.start, f32[12,8,128]{2,1,0:T(8,128)S(1)} %collective-permute-done.near, ...), custom_call_target="tpu_custom_call" | custom-call | flops 1800000000 | bytes 1048576 | tf_op jit(solution)/shard_map/right_near/pallas_call | solution.py:209
  29.1 6.2 %collective-permute-done.3.refs_0_ = f32[264,128]{1,0:T(8,128)S(1)} collective-permute-done((f32[264,128]{1,0:T(8,128)S(1)}, f32[264,128]{1,0:T(8,128)S(1)}, u32[]{:S(2)}, u32[]{:S(2)}) %collective-permute-start.3) | collective-permute-done | bytes 135200 | tf_op jit(solution)/shard_map/ppermute | solution.py:347
  35.3 2.8 %collective-permute-done.4.refs_1_ = f32[264,128]{1,0:T(8,128)S(1)} collective-permute-done((f32[264,128]{1,0:T(8,128)S(1)}, f32[264,128]{1,0:T(8,128)S(1)}, u32[]{:S(2)}, u32[]{:S(2)}) %collective-permute-start.4) | collective-permute-done | bytes 135200 | tf_op jit(solution)/shard_map/ppermute | solution.py:347
  38.1 2.3 %collective-permute-start.6 = (f32[264,128]{1,0:T(8,128)S(1)}, f32[264,128]{1,0:T(8,128)S(1)}, u32[]{:S(2)}, u32[]{:S(2)}) collective-permute-start(f32[264,128]{1,0:T(8,128)S(1)} %get-tuple-element.35), channel_id=1, source_target_pairs={{0,7},{1,6},{2,5},{3,4},{4,3},{5,2},{6,1},{7,0},{8,15},{9,14},{10,... | collective-permute-start | bytes 405512 | tf_op jit(solution)/shard_map/ppermute | solution.py:347
  41.0 5.7 %collective-permute-done.13.refs_6_.refs_3_ = f32[264,128]{1,0:T(8,128)S(1)} collective-permute-done((f32[264,128]{1,0:T(8,128)S(1)}, f32[264,128]{1,0:T(8,128)S(1)}, u32[]{:S(2)}, u32[]{:S(2)}) %collective-permute-start.13) | collective-permute-done | bytes 135200 | tf_op jit(solution)/shard_map/ppermute | solution.py:347
  46.7 2.1 %sweeps_lower.1 = (f32[3,272,128]{2,1,0:T(8,128)S(1)}, f32[4,256,128]{2,1,0:T(8,128)S(1)}) custom-call(f32[264,128]{1,0:T(8,128)S(1)} %collective-permute-done.3.refs_0_, f32[264,128]{1,0:T(8,128)S(1)} %collective-permute-done.4.refs_1_, f32[264,128]{1,0:T(8,128)S(1)} %collective-permute-done.5.refs_2_, f32[264,128]{1,0:T(8,128)S(1)} %get-tuple-element.38.refs_3_.refs_0_, ...), custom_call_target="tpu_custom_call" | custom-call | flops 1000000000 | bytes 1048576 | tf_op jit(solution)/shard_map/sweeps_lower/pallas_call | solution.py:392
  48.8 2.2 %sweeps_far.1 = (f32[256,128]{1,0:T(8,128)S(1)}, f32[256,128]{1,0:T(8,128)S(1)}, f32[256,128]{1,0:T(8,128)S(1)}, f32[256,128]{1,0:T(8,128)S(1)}, f32[3,272,128]{2,1,0:T(8,128)S(1)}) custom-call(f32[264,128]{1,0:T(8,128)S(1)} %collective-permute-done.3.refs_0_, f32[264,128]{1,0:T(8,128)S(1)} %collective-permute-done.4.refs_1_, ...), custom_call_target="tpu_custom_call" | custom-call | flops 1000000000 | bytes 1048576 | tf_op jit(solution)/shard_map/sweeps_far/pallas_call | solution.py:400
  51.1 2.4 %collective-permute-start.15 = (f32[256,128]{1,0:T(8,128)S(1)}, f32[256,128]{1,0:T(8,128)S(1)}, u32[]{:S(2)}, u32[]{:S(2)}) collective-permute-start(f32[256,128]{1,0:T(8,128)S(1)} %get-tuple-element.44), channel_id=1, source_target_pairs={{0,5},{1,4},{2,7},{3,6},{4,1},{5,0},{6,3},{7,2},{8,13},{9,12},{10,... | collective-permute-start | bytes 393224 | tf_op jit(solution)/shard_map/ppermute | solution.py:347
  54.1 3.2 %collective-permute-start.17 = (f32[256,128]{1,0:T(8,128)S(1)}, f32[256,128]{1,0:T(8,128)S(1)}, u32[]{:S(2)}, u32[]{:S(2)}) collective-permute-start(f32[256,128]{1,0:T(8,128)S(1)} %get-tuple-element.46), channel_id=1, source_target_pairs={{0,7},{1,6},{2,5},{3,4},{4,3},{5,2},{6,1},{7,0},{8,15},{9,14},{10,... | collective-permute-start | bytes 393224 | tf_op jit(solution)/shard_map/ppermute | solution.py:347
  57.6 10.1 %collective-permute-done.14.refs_0_ = f32[256,128]{1,0:T(8,128)S(1)} collective-permute-done((f32[256,128]{1,0:T(8,128)S(1)}, f32[256,128]{1,0:T(8,128)S(1)}, u32[]{:S(2)}, u32[]{:S(2)}) %collective-permute-start.14) | collective-permute-done | bytes 131104 | tf_op jit(solution)/shard_map/ppermute | solution.py:347
  67.7 2.7 %collective-permute-done.15.refs_1_ = f32[256,128]{1,0:T(8,128)S(1)} collective-permute-done((f32[256,128]{1,0:T(8,128)S(1)}, f32[256,128]{1,0:T(8,128)S(1)}, u32[]{:S(2)}, u32[]{:S(2)}) %collective-permute-start.15) | collective-permute-done | bytes 131104 | tf_op jit(solution)/shard_map/ppermute | solution.py:347
  70.4 2.9 %collective-permute-done.19.refs_6_ = f32[256,128]{1,0:T(8,128)S(1)} collective-permute-done((f32[256,128]{1,0:T(8,128)S(1)}, f32[256,128]{1,0:T(8,128)S(1)}, u32[]{:S(2)}, u32[]{:S(2)}) %collective-permute-start.19) | collective-permute-done | bytes 131104 | tf_op jit(solution)/shard_map/ppermute | solution.py:347
  73.2 2.6 %collective-permute-done.20.refs_7_ = f32[256,128]{1,0:T(8,128)S(1)} collective-permute-done((f32[256,128]{1,0:T(8,128)S(1)}, f32[256,128]{1,0:T(8,128)S(1)}, u32[]{:S(2)}, u32[]{:S(2)}) %collective-permute-start.20) | collective-permute-done | bytes 131104 | tf_op jit(solution)/shard_map/ppermute | solution.py:347
  (34 shorter events, 4.9 us)
Async XLA Ops:
  1.7 16.5 %collective-permute-start.9 = (f32[256,128]{1,0:T(8,128)}, f32[256,128]{1,0:T(8,128)S(1)}, u32[]{:S(2)}, u32[]{:S(2)}) collective-permute-start(f32[256,128]{1,0:T(8,128)} %get-tuple-element.36.refs_0_), channel_id=1, source_target_pairs={{0,6},{1,7},{2,4},{3,5},{4,2},{5,3},{6,0},{7,1},{8,14},{9,15},{10,... | collective-permute-start | bytes 393224 | tf_op jit(solution)/shard_map/ppermute | solution.py:347
  6.8 11.4 %collective-permute-start.8 = (f32[256,128]{1,0:T(8,128)}, f32[256,128]{1,0:T(8,128)S(1)}, u32[]{:S(2)}, u32[]{:S(2)}) collective-permute-start(f32[256,128]{1,0:T(8,128)} %get-tuple-element.36.refs_0_), channel_id=1, source_target_pairs={{0,4},{1,5},{2,6},{3,7},{4,0},{5,1},{6,2},{7,3},{8,12},{9,13},{10,... | collective-permute-start | bytes 393224 | tf_op jit(solution)/shard_map/ppermute | solution.py:347
  6.8 6.0 %collective-permute-start.1 = (f32[10,8,128]{2,1,0:T(8,128)}, f32[10,8,128]{2,1,0:T(8,128)S(1)}, u32[]{:S(2)}, u32[]{:S(2)}) collective-permute-start(f32[10,8,128]{2,1,0:T(8,128)} %get-tuple-element.29.own), channel_id=1, source_target_pairs={{0,16},{8,24},{16,0},{24,8},{1,17},{9,25},{17,1},{25,9},{2,18},{10... | collective-permute-start | bytes 122888 | tf_op jit(solution)/shard_map/ppermute | solution.py:347
  8.4 5.2 %collective-permute-start = (f32[12,8,128]{2,1,0:T(8,128)}, f32[12,8,128]{2,1,0:T(8,128)S(1)}, u32[]{:S(2)}, u32[]{:S(2)}) collective-permute-start(f32[12,8,128]{2,1,0:T(8,128)} %get-tuple-element.30), channel_id=1, source_target_pairs={{0,8},{8,0},{16,24},{24,16},{1,9},{9,1},{17,25},{25,17},{2,10},{10... | collective-permute-start | bytes 147464 | tf_op jit(solution)/shard_map/ppermute | solution.py:347
  9.9 3.0 %copy-start.1 = (f32[256,128]{1,0:T(8,128)S(1)}, f32[256,128]{1,0:T(8,128)}, u32[]{:S(2)}) copy-start(f32[256,128]{1,0:T(8,128)} %get-tuple-element.36.refs_0_) | copy-start | bytes 393220
  9.9 5.2 %copy-start = (f32[8,256,128]{2,1,0:T(8,128)S(1)}, f32[8,256,128]{2,1,0:T(8,128)}, u32[]{:S(2)}) copy-start(f32[8,256,128]{2,1,0:T(8,128)} %adj.5) | copy-start | bytes 3145732
  9.9 5.2 %collective-permute-start.2 = (f32[12,8,128]{2,1,0:T(8,128)}, f32[12,8,128]{2,1,0:T(8,128)S(1)}, u32[]{:S(2)}, u32[]{:S(2)}) collective-permute-start(f32[12,8,128]{2,1,0:T(8,128)} %get-tuple-element.31), channel_id=1, source_target_pairs={{0,24},{8,16},{16,8},{24,0},{1,25},{9,17},{17,9},{25,1},{2,26},{10... | collective-permute-start | bytes 147464 | tf_op jit(solution)/shard_map/ppermute | solution.py:347
  10.3 0.8 %copy-start.2 = (f32[10,8,128]{2,1,0:T(8,128)S(1)}, f32[10,8,128]{2,1,0:T(8,128)}, u32[]{:S(2)}) copy-start(f32[10,8,128]{2,1,0:T(8,128)} %get-tuple-element.29.own) | copy-start | bytes 122884
  12.8 7.1 %collective-permute-start.7 = (f32[256,128]{1,0:T(8,128)S(1)}, f32[256,128]{1,0:T(8,128)S(1)}, u32[]{:S(2)}, u32[]{:S(2)}) collective-permute-start(f32[256,128]{1,0:T(8,128)S(1)} %copy-done.1), channel_id=1, source_target_pairs={{0,2},{1,3},{2,0},{3,1},{4,6},{5,7},{6,4},{7,5},{8,10},{9,11},{10,... | collective-permute-start | bytes 393224 | tf_op jit(solution)/shard_map/ppermute | solution.py:347
  20.0 5.0 %collective-permute-start.10 = (f32[4,256,128]{2,1,0:T(8,128)S(1)}, f32[4,256,128]{2,1,0:T(8,128)S(1)}, u32[]{:S(2)}, u32[]{:S(2)}) collective-permute-start(f32[4,256,128]{2,1,0:T(8,128)S(1)} %stack.1.mine), channel_id=1, source_target_pairs={{0,1},{1,0},{2,3},{3,2},{4,5},{5,4},{6,7},{7,6},{8,9},{9,8},{10,11... | collective-permute-start | bytes 1572872 | tf_op jit(solution)/shard_map/ppermute | solution.py:347
  20.1 15.3 %collective-permute-start.3 = (f32[264,128]{1,0:T(8,128)S(1)}, f32[264,128]{1,0:T(8,128)S(1)}, u32[]{:S(2)}, u32[]{:S(2)}) collective-permute-start(f32[264,128]{1,0:T(8,128)S(1)} %get-tuple-element.32), channel_id=1, source_target_pairs={{0,4},{1,5},{2,6},{3,7},{4,0},{5,1},{6,2},{7,3},{8,12},{9,13},{10,... | collective-permute-start | bytes 405512 | tf_op jit(solution)/shard_map/ppermute | solution.py:347
  21.4 16.7 %collective-permute-start.4 = (f32[264,128]{1,0:T(8,128)S(1)}, f32[264,128]{1,0:T(8,128)S(1)}, u32[]{:S(2)}, u32[]{:S(2)}) collective-permute-start(f32[264,128]{1,0:T(8,128)S(1)} %get-tuple-element.33), channel_id=1, source_target_pairs={{0,5},{1,4},{2,7},{3,6},{4,1},{5,0},{6,3},{7,2},{8,13},{9,12},{10,... | collective-permute-start | bytes 405512 | tf_op jit(solution)/shard_map/ppermute | solution.py:347
  22.8 17.6 %collective-permute-start.5 = (f32[264,128]{1,0:T(8,128)S(1)}, f32[264,128]{1,0:T(8,128)S(1)}, u32[]{:S(2)}, u32[]{:S(2)}) collective-permute-start(f32[264,128]{1,0:T(8,128)S(1)} %get-tuple-element.34), channel_id=1, source_target_pairs={{0,6},{1,7},{2,4},{3,5},{4,2},{5,3},{6,0},{7,1},{8,14},{9,15},{10,... | collective-permute-start | bytes 405512 | tf_op jit(solution)/shard_map/ppermute | solution.py:347
  29.0 11.5 %collective-permute-start.11 = (f32[264,128]{1,0:T(8,128)S(1)}, f32[264,128]{1,0:T(8,128)S(1)}, u32[]{:S(2)}, u32[]{:S(2)}) collective-permute-start(f32[264,128]{1,0:T(8,128)S(1)} %get-tuple-element.39), channel_id=1, source_target_pairs={{0,1},{1,0},{2,3},{3,2},{4,5},{5,4},{6,7},{7,6},{8,9},{9,8},{10,11... | collective-permute-start | bytes 405512 | tf_op jit(solution)/shard_map/ppermute | solution.py:347
  29.1 11.9 %collective-permute-start.12 = (f32[264,128]{1,0:T(8,128)S(1)}, f32[264,128]{1,0:T(8,128)S(1)}, u32[]{:S(2)}, u32[]{:S(2)}) collective-permute-start(f32[264,128]{1,0:T(8,128)S(1)} %get-tuple-element.40), channel_id=1, source_target_pairs={{0,2},{1,3},{2,0},{3,1},{4,6},{5,7},{6,4},{7,5},{8,10},{9,11},{10,... | collective-permute-start | bytes 405512 | tf_op jit(solution)/shard_map/ppermute | solution.py:347
  35.3 11.4 %collective-permute-start.13 = (f32[264,128]{1,0:T(8,128)S(1)}, f32[264,128]{1,0:T(8,128)S(1)}, u32[]{:S(2)}, u32[]{:S(2)}) collective-permute-start(f32[264,128]{1,0:T(8,128)S(1)} %get-tuple-element.41), channel_id=1, source_target_pairs={{0,3},{1,2},{2,1},{3,0},{4,7},{5,6},{6,5},{7,4},{8,11},{9,10},{10,... | collective-permute-start | bytes 405512 | tf_op jit(solution)/shard_map/ppermute | solution.py:347
  38.1 10.7 %collective-permute-start.6 = (f32[264,128]{1,0:T(8,128)S(1)}, f32[264,128]{1,0:T(8,128)S(1)}, u32[]{:S(2)}, u32[]{:S(2)}) collective-permute-start(f32[264,128]{1,0:T(8,128)S(1)} %get-tuple-element.35), channel_id=1, source_target_pairs={{0,7},{1,6},{2,5},{3,4},{4,3},{5,2},{6,1},{7,0},{8,15},{9,14},{10,... | collective-permute-start | bytes 405512 | tf_op jit(solution)/shard_map/ppermute | solution.py:347
  51.0 16.6 %collective-permute-start.14 = (f32[256,128]{1,0:T(8,128)S(1)}, f32[256,128]{1,0:T(8,128)S(1)}, u32[]{:S(2)}, u32[]{:S(2)}) collective-permute-start(f32[256,128]{1,0:T(8,128)S(1)} %get-tuple-element.43), channel_id=1, source_target_pairs={{0,4},{1,5},{2,6},{3,7},{4,0},{5,1},{6,2},{7,3},{8,12},{9,13},{10,... | collective-permute-start | bytes 393224 | tf_op jit(solution)/shard_map/ppermute | solution.py:347
  51.1 19.2 %collective-permute-start.15 = (f32[256,128]{1,0:T(8,128)S(1)}, f32[256,128]{1,0:T(8,128)S(1)}, u32[]{:S(2)}, u32[]{:S(2)}) collective-permute-start(f32[256,128]{1,0:T(8,128)S(1)} %get-tuple-element.44), channel_id=1, source_target_pairs={{0,5},{1,4},{2,7},{3,6},{4,1},{5,0},{6,3},{7,2},{8,13},{9,12},{10,... | collective-permute-start | bytes 393224 | tf_op jit(solution)/shard_map/ppermute | solution.py:347
  53.5 16.9 %collective-permute-start.16 = (f32[256,128]{1,0:T(8,128)S(1)}, f32[256,128]{1,0:T(8,128)S(1)}, u32[]{:S(2)}, u32[]{:S(2)}) collective-permute-start(f32[256,128]{1,0:T(8,128)S(1)} %get-tuple-element.45), channel_id=1, source_target_pairs={{0,6},{1,7},{2,4},{3,5},{4,2},{5,3},{6,0},{7,1},{8,14},{9,15},{10,... | collective-permute-start | bytes 393224 | tf_op jit(solution)/shard_map/ppermute | solution.py:347
  54.1 16.3 %collective-permute-start.17 = (f32[256,128]{1,0:T(8,128)S(1)}, f32[256,128]{1,0:T(8,128)S(1)}, u32[]{:S(2)}, u32[]{:S(2)}) collective-permute-start(f32[256,128]{1,0:T(8,128)S(1)} %get-tuple-element.46), channel_id=1, source_target_pairs={{0,7},{1,6},{2,5},{3,4},{4,3},{5,2},{6,1},{7,0},{8,15},{9,14},{10,... | collective-permute-start | bytes 393224 | tf_op jit(solution)/shard_map/ppermute | solution.py:347
  57.3 13.0 %collective-permute-start.18 = (f32[256,128]{1,0:T(8,128)S(1)}, f32[256,128]{1,0:T(8,128)S(1)}, u32[]{:S(2)}, u32[]{:S(2)}) collective-permute-start(f32[256,128]{1,0:T(8,128)S(1)} %get-tuple-element.50), channel_id=1, source_target_pairs={{0,1},{1,0},{2,3},{3,2},{4,5},{5,4},{6,7},{7,6},{8,9},{9,8},{10,11... | collective-permute-start | bytes 393224 | tf_op jit(solution)/shard_map/ppermute | solution.py:347
  67.7 5.5 %collective-permute-start.19 = (f32[256,128]{1,0:T(8,128)S(1)}, f32[256,128]{1,0:T(8,128)S(1)}, u32[]{:S(2)}, u32[]{:S(2)}) collective-permute-start(f32[256,128]{1,0:T(8,128)S(1)} %get-tuple-element.51), channel_id=1, source_target_pairs={{0,2},{1,3},{2,0},{3,1},{4,6},{5,7},{6,4},{7,5},{8,10},{9,11},{10,... | collective-permute-start | bytes 393224 | tf_op jit(solution)/shard_map/ppermute | solution.py:347
  70.3 5.5 %collective-permute-start.20 = (f32[256,128]{1,0:T(8,128)S(1)}, f32[256,128]{1,0:T(8,128)S(1)}, u32[]{:S(2)}, u32[]{:S(2)}) collective-permute-start(f32[256,128]{1,0:T(8,128)S(1)} %get-tuple-element.52), channel_id=1, source_target_pairs={{0,3},{1,2},{2,1},{3,0},{4,7},{5,6},{6,5},{7,4},{8,11},{9,10},{10,... | collective-permute-start | bytes 393224 | tf_op jit(solution)/shard_map/ppermute | solution.py:347

commit v3 on v2

--- a/solution.py
+++ b/solution.py
@@ -142,27 +142,27 @@
     )
 
 
-def own_faces_kernel(own, acc, hot_rows, weights):
+def own_faces_kernel(peers, own, acc, hot_rows, weights):
     block_rows = 128
     circum = acc.shape[0] - 16
-    harmonics = range(acc.shape[1] // block_rows)
+    harmonics = [peer(i) for i in peers]
     acc[...] = face_product(own, hot_rows, weights, harmonics, circum, block_rows)
 
 
-def own_faces(own, harm_rows, circum):
+def own_faces(peers, own, circum):
     faces = (own.shape[0] - 2) * 128
-    rows, lanes = circum + 16, harm_rows * 128
+    rows, lanes = circum + 16, len(peers) * 128
     return call(
-        own_faces_kernel,
+        functools.partial(own_faces_kernel, peers),
         (((rows, lanes), F32),),
         [VMEM],
         [pltpu.VMEM((rows, 2 * faces), BF16), pltpu.VMEM((lanes, 2 * faces), BF16)],
-        1_200_000_000,
+        600_000_000,
         "own_faces",
     )(own)[0]
 
 
-def right_kernel(peers, adj, start, near, far, diag, *rest):
+def right_kernel(peers, own, adj, start, near, far, diag, *rest):
     count = len(peers)
     *outs, hot_rows, weights, acc, source, sems = rest
     del outs[: len(outs) - count - 1]
@@ -177,14 +177,19 @@
     groups = weights.shape[2] // 256
     odd = lax.rem(lax.axis_index("blade"), 2)
     harmonics = [peer(i) for i in peers]
-    for at, h in enumerate(harmonics):
-        lanes = pl.ds(pl.multiple_of(h * block_rows, block_rows), block_rows)
-        acc[:, at * block_rows : (at + 1) * block_rows] = start[:, lanes]
-    for step, message in enumerate((near, far, diag)):
+    messages = (near, far, diag)
+    if own:
+        messages = (start, *messages)
+    else:
+        acc[...] = start[...]
+    for step, message in enumerate(messages):
         product = face_product(
             message, hot_rows.at[step], weights.at[step], harmonics, circum, block_rows
         )
-        acc[...] += product
+        if own and step == 0:
+            acc[...] = product
+        else:
+            acc[...] += product
     gap = jnp.zeros((8 - 2 * HALO, 128), F32)
     for copy in copies:
         copy.wait()
@@ -201,18 +206,18 @@
         )
 
 
-def right_pieces(peers, adj_source, start, messages, after, name):
+def right_pieces(peers, own, adj_source, start, messages, after, name):
     _, circum, block_rows = adj_source.shape
     count = len(peers)
     faces = (messages[1].shape[0] - 2) * 128
     rows = circum + 16
     return call(
-        functools.partial(right_kernel, peers),
+        functools.partial(right_kernel, peers, own),
         (((circum + 8, block_rows), F32),) * count + (((8, 128), F32),),
         [HBM] + [VMEM] * 4 + [ANY] * len(after),
         [
-            pltpu.VMEM((3, rows, 2 * faces), BF16),
-            pltpu.VMEM((3, count * block_rows, 2 * faces), BF16),
+            pltpu.VMEM((3 + own, rows, 2 * faces), BF16),
+            pltpu.VMEM((3 + own, count * block_rows, 2 * faces), BF16),
             pltpu.VMEM((rows, count * block_rows), F32),
             pltpu.VMEM((count, circum, block_rows), F32),
             pltpu.SemaphoreType.DMA((count,)),
@@ -248,16 +253,22 @@
         cross = low[:, :block_rows] + high[:, block_rows:]
         return (high[:, :block_rows] + cross) + low[:, block_rows:]
 
+    def advance(fields, k, sweep):
+        rhs = right[k]
+        if sweep > 0:
+            around = pltpu.roll(fields[sweep - 1], 1, 0)
+            around += pltpu.roll(fields[sweep - 1], rows - 1, 0)
+            rhs = rhs + coupling * around
+        return solve(rhs, fields[sweep], k)
+
     fields = list(fields)
-    for k in range(half):
-        base = rhs = right[k]
-        for sweep in range(ITERS):
-            if sweep > 0:
-                field = fields[sweep - 1]
-                around = pltpu.roll(field, 1, 0) + pltpu.roll(field, rows - 1, 0)
-                rhs = base + coupling * around
-            fields[sweep] = solve(rhs, fields[sweep], k)
-        solved[k] = fields[-1][:circum]
+    for wave in range(half + ITERS - 1):
+        active = [j for j in range(ITERS) if 0 <= wave - j < half]
+        news = [advance(fields, wave - j, j) for j in active]
+        for j, new in zip(active, news, strict=True):
+            fields[j] = new
+        if wave >= ITERS - 1:
+            solved[wave - ITERS + 1] = fields[-1][:circum]
     return fields
 
 
@@ -279,9 +290,9 @@
             weights[k, block_rows : 2 * block_rows, part] = lo
 
 
-def lower_kernel(half, *refs):
+def lower_kernel(half, near, *refs):
     *rest, weights, state, solved, right = refs
-    pieces = rest[len(rest) - half :]
+    pieces = [rest[i] for i in near]
     upper = lax.axis_index("span") // half
     zero = jnp.zeros(state.shape[1:], F32)
 
@@ -330,11 +341,11 @@
             out[...] = solved[lax.rem(peer(i), half)]
 
 
-def place_kernel(peers, *refs):
+def place_kernel(order, *refs):
     *pieces, out, sems = refs
     copies = [
         pltpu.make_async_copy(piece, out.at[peer(i)], sems.at[i])
-        for i, piece in zip(peers, pieces, strict=True)
+        for i, piece in zip(order, pieces, strict=True)
     ]
     for copy in copies:
         copy.start()
@@ -359,11 +370,13 @@
         exchange(far, "blade", 2),
         exchange(diag, "blade", 3),
     ]
-    start = own_faces(far, harm_rows, circum)
     operators = [operators] + [exchange(operators, "span", bits) for bits in range(2, count, 2)]
-    far_peers, near_peers = range(half, count), range(half)
-    *far_right, token = right_pieces(far_peers, adj_source, start, messages, [], "right_far")
-    far_right = [exchange(p, "span", i) for p, i in zip(far_right, far_peers, strict=True)]
+    first, second = (4, 5, 6, 3), (2, 7, 1, 0)
+    start = own_faces(first, far, circum)
+    *pieces, token = right_pieces(
+        first, False, adj_source, start, messages, [], "right_first"
+    )
+    right_side = dict(zip(first, pieces, strict=True))
     mine = call(
         stack_kernel,
         (((half, *operators[0].shape), F32),),
@@ -381,8 +394,13 @@
         0,
         "operators",
     )(mine, partner)[0]
-    *near_right, _ = right_pieces(near_peers, adj_source, start, messages, [token, weights], "right_near")
-    near_right = [p if i == 0 else exchange(p, "span", i) for i, p in enumerate(near_right)]
+    *pieces, _ = right_pieces(
+        second, True, adj_source, far, messages, [token, weights], "right_second"
+    )
+    right_side |= dict(zip(second, pieces, strict=True))
+    far_peers, near_peers = range(half, count), range(half)
+    far_right = [exchange(right_side[i], "span", i) for i in far_peers]
+    near_right = [right_side[0]] + [exchange(right_side[i], "span", i) for i in near_peers[1:]]
 
     rows = circum + 16
     right = pltpu.VMEM((half, rows, block_rows), F32)
@@ -390,13 +408,13 @@
     state_shape = ((ITERS, rows, block_rows), F32)
     piece = ((circum, block_rows), F32)
     state, done = call(
-        functools.partial(lower_kernel, half),
+        functools.partial(lower_kernel, half, (6, 5, 3, 2)),
         (state_shape, ((half, circum, block_rows), F32)),
-        [ANY] * 3 + [VMEM] * (half + 1),
+        [ANY, ANY, VMEM, VMEM, ANY, VMEM, VMEM, VMEM],
         [right],
         1_000_000_000,
         "sweeps_lower",
-    )(*far_right[:3], *near_right, weights)
+    )(far_right[0], far_right[1], near_right[3], near_right[2], far_right[2], near_right[1], near_right[0], weights)
     *far_solved, state = call(
         functools.partial(far_kernel, half),
         (piece,) * half + (state_shape,),
@@ -415,15 +433,17 @@
         "sweeps_upper",
     )(*near_right, weights, state, done)
     near_solved = [p if i == 0 else exchange(p, "span", i) for i, p in enumerate(near_solved)]
+    order = (4, 5, 6, 3, 2, 7, 1, 0)
+    pieces = [*near_solved, *far_solved]
     return call(
-        functools.partial(place_kernel, (*far_peers, *near_peers)),
+        functools.partial(place_kernel, order),
         (((count, circum, block_rows), F32),),
         [ANY] * count,
         [pltpu.SemaphoreType.DMA((count,))],
         0,
         "place",
         out_specs=(ANY,),
-    )(*far_solved, *near_solved)[0]
+    )(*[pieces[i] for i in order])[0]
 
 
 def extended(block, sides, width):

time: 77 us -> 72.3 us (0.939); the launches traced: 76.9 us -> 71.1 us
  waiting for transfers between devices: 36.7 us -> 27.4 us
  starting transfers between devices: 23.3 us -> 27.3 us
  Pallas kernels: 15.9 us -> 14.9 us
    ppermute x21, waiting for transfers between devices: 36.7 us -> 27.4 us  [exchange(): return lax.ppermute(array, axis, [(i, i ^ bits) for i in range(count)])]
    ppermute x21, starting transfers between devices: 23.3 us -> 27.3 us  [exchange(): return lax.ppermute(array, axis, [(i, i ^ bits) for i in range(count)])]
  transfers between devices with their start and end apart: 21 -> 21, of which waited for: 10 -> 10; matrix products, arithmetic and copies ran while one was open for 0% -> 0% of each run, Pallas kernels for 14% -> 15%
where the time goes in v3:
time: 72.3 us; the launch traced here: 71.1 us
  waiting for transfers between devices  27.4 us (38%)
  starting transfers between devices  27.3 us (38%)
  Pallas kernels  14.9 us (21%)
  local copies, waits for them, and re-layouts  1.37 us (2%)
    ppermute x21, waiting for transfers between devices, exchange(): return lax.ppermute(array, axis, [(i, i ^ bits) for i in range(count)])  27.4 us
    ppermute x21, starting transfers between devices, exchange(): return lax.ppermute(array, axis, [(i, i ^ bits) for i in range(count)])  27.3 us
    pallas_call x2, Pallas kernels, right_pieces(): call(functools.partial(right_kernel, peers, own), (((circum + 8, block_ro...  7.6 us
    pallas_call x1, Pallas kernels, pack(): call(pack_kernel, (with_halo, faces, with_halo, ((2 * block_rows, block_r...  1.71 us
    pallas_call x1, Pallas kernels, by_harmonics(): call(functools.partial(far_kernel, half), (piece,) * half + (state_shape,...  1.65 us
    pallas_call x1, Pallas kernels, by_harmonics(): call(functools.partial(lower_kernel, half, (6, 5, 3, 2)), (state_shape, (...  1.56 us
  transfers between devices with their start and end apart: 21, of which 10 were waited for; matrix products, arithmetic and copies ran while one was open for 0% of the time, Pallas kernels for 15%

profile of v3, /device:TPU:0, one launch (start us, length us, event | category | flops | bytes accessed | tf_op | source)
XLA Modules:
  0.0 71.1 jit_solution(6858213320534890637)
XLA Ops:
  0.0 1.7 %pack.1 = (f32[12,8,128]{2,1,0:T(8,128)}, f32[10,8,128]{2,1,0:T(8,128)}, f32[12,8,128]{2,1,0:T(8,128)}, f32[256,128]{1,0:T(8,128)}) custom-call(f32[8,1024]{1,0:T(8,128)} %flux.1, s32[8,128]{1,0:T(8,128)} %bitcast.2, s32[8,128]{1,0:T(8,128)} %bitcast.3, f32[8,256,128]{2,1,0:T(8,128)} %adj.5, f32[128,128]{1,0:T(8,128)} %inverse.1, f32[128,128]{1,0:T(8,128)} %gain.1), custom_call_target="tpu_custom_call" | custom-call | bytes 1048576 | tf_op jit(solution)/shard_map/pack/pallas_call | solution.py:81
  1.7 5.1 %collective-permute-start.8 = (f32[256,128]{1,0:T(8,128)}, f32[256,128]{1,0:T(8,128)S(1)}, u32[]{:S(2)}, u32[]{:S(2)}) collective-permute-start(f32[256,128]{1,0:T(8,128)} %get-tuple-element.36.refs_0_), channel_id=1, source_target_pairs={{0,6},{1,7},{2,4},{3,5},{4,2},{5,3},{6,0},{7,1},{8,14},{9,15},{10,... | collective-permute-start | bytes 393224 | tf_op jit(solution)/shard_map/ppermute | solution.py:358
  6.8 1.5 %collective-permute-start.1 = (f32[10,8,128]{2,1,0:T(8,128)}, f32[10,8,128]{2,1,0:T(8,128)S(1)}, u32[]{:S(2)}, u32[]{:S(2)}) collective-permute-start(f32[10,8,128]{2,1,0:T(8,128)} %get-tuple-element.29.own.start), channel_id=1, source_target_pairs={{0,16},{8,24},{16,0},{24,8},{1,17},{9,25},{17,1},{25,9},{2,18},{10... | collective-permute-start | bytes 122888 | tf_op jit(solution)/shard_map/ppermute | solution.py:358
  8.4 1.5 %collective-permute-start = (f32[12,8,128]{2,1,0:T(8,128)}, f32[12,8,128]{2,1,0:T(8,128)S(1)}, u32[]{:S(2)}, u32[]{:S(2)}) collective-permute-start(f32[12,8,128]{2,1,0:T(8,128)} %get-tuple-element.30), channel_id=1, source_target_pairs={{0,8},{8,0},{16,24},{24,16},{1,9},{9,1},{17,25},{25,17},{2,10},{10... | collective-permute-start | bytes 147464 | tf_op jit(solution)/shard_map/ppermute | solution.py:358
  11.1 1.1 %own_faces.1.start = f32[272,512]{1,0:T(8,128)S(1)} custom-call(f32[10,8,128]{2,1,0:T(8,128)S(1)} %copy-done.2), custom_call_target="tpu_custom_call" | custom-call | flops 600000000 | bytes 1048576 | tf_op jit(solution)/shard_map/own_faces/pallas_call | solution.py:155
  13.0 2.1 %collective-permute-done.2.diag = f32[12,8,128]{2,1,0:T(8,128)S(1)} collective-permute-done((f32[12,8,128]{2,1,0:T(8,128)}, f32[12,8,128]{2,1,0:T(8,128)S(1)}, u32[]{:S(2)}, u32[]{:S(2)}) %collective-permute-start.2) | collective-permute-done | bytes 49184 | tf_op jit(solution)/shard_map/ppermute | solution.py:358
  15.1 3.2 %right_first.1 = (f32[264,128]{1,0:T(8,128)S(1)}, f32[264,128]{1,0:T(8,128)S(1)}, f32[264,128]{1,0:T(8,128)S(1)}, f32[264,128]{1,0:T(8,128)S(1)}, f32[8,128]{1,0:T(8,128)S(1)}) custom-call(f32[8,256,128]{2,1,0:T(8,128)S(1)} %copy-done, f32[272,512]{1,0:T(8,128)S(1)} %own_faces.1.start, f32[12,8,128]{2,1,0:T(8,128)S(1)} %collective-permute-done.near, ...), custom_call_target="tpu_custom_call" | custom-call | flops 1800000000 | bytes 1048576 | tf_op jit(solution)/shard_map/right_first/pallas_call | solution.py:214
  18.3 1.1 %collective-permute-done.6.refs_1_ = f32[256,128]{1,0:T(8,128)S(1)} collective-permute-done((f32[256,128]{1,0:T(8,128)S(1)}, f32[256,128]{1,0:T(8,128)S(1)}, u32[]{:S(2)}, u32[]{:S(2)}) %collective-permute-start.6) | collective-permute-done | bytes 131104 | tf_op jit(solution)/shard_map/ppermute | solution.py:358
  19.5 1.9 %collective-permute-start.3 = (f32[264,128]{1,0:T(8,128)S(1)}, f32[264,128]{1,0:T(8,128)S(1)}, u32[]{:S(2)}, u32[]{:S(2)}) collective-permute-start(f32[264,128]{1,0:T(8,128)S(1)} %get-tuple-element.32), channel_id=1, source_target_pairs={{0,4},{1,5},{2,6},{3,7},{4,0},{5,1},{6,2},{7,3},{8,12},{9,13},{10,... | collective-permute-start | bytes 405512 | tf_op jit(solution)/shard_map/ppermute | solution.py:358
  22.2 2.3 %collective-permute-start.5 = (f32[264,128]{1,0:T(8,128)S(1)}, f32[264,128]{1,0:T(8,128)S(1)}, u32[]{:S(2)}, u32[]{:S(2)}) collective-permute-start(f32[264,128]{1,0:T(8,128)S(1)} %get-tuple-element.34), channel_id=1, source_target_pairs={{0,6},{1,7},{2,4},{3,5},{4,2},{5,3},{6,0},{7,1},{8,14},{9,15},{10,... | collective-permute-start | bytes 405512 | tf_op jit(solution)/shard_map/ppermute | solution.py:358
  25.3 4.4 %right_second.1 = (f32[264,128]{1,0:T(8,128)S(1)}, f32[264,128]{1,0:T(8,128)S(1)}, f32[264,128]{1,0:T(8,128)S(1)}, f32[264,128]{1,0:T(8,128)S(1)}, f32[8,128]{1,0:T(8,128)}) custom-call(f32[8,256,128]{2,1,0:T(8,128)S(1)} %copy-done, f32[10,8,128]{2,1,0:T(8,128)S(1)} %copy-done.3, f32[12,8,128]{2,1,0:T(8,128)S(1)} %collective-permute-done.near, ...), custom_call_target="tpu_custom_call" | custom-call | flops 1800000000 | bytes 1048576 | tf_op jit(solution)/shard_map/right_second/pallas_call | solution.py:214
  29.7 1.2 %collective-permute-start.12 = (f32[264,128]{1,0:T(8,128)S(1)}, f32[264,128]{1,0:T(8,128)S(1)}, u32[]{:S(2)}, u32[]{:S(2)}) collective-permute-start(f32[264,128]{1,0:T(8,128)S(1)} %get-tuple-element.39), channel_id=1, source_target_pairs={{0,2},{1,3},{2,0},{3,1},{4,6},{5,7},{6,4},{7,5},{8,10},{9,11},{10,... | collective-permute-start | bytes 405512 | tf_op jit(solution)/shard_map/ppermute | solution.py:358
  30.9 3.9 %collective-permute-done.3.refs_0_ = f32[264,128]{1,0:T(8,128)S(1)} collective-permute-done((f32[264,128]{1,0:T(8,128)S(1)}, f32[264,128]{1,0:T(8,128)S(1)}, u32[]{:S(2)}, u32[]{:S(2)}) %collective-permute-start.3) | collective-permute-done | bytes 135200 | tf_op jit(solution)/shard_map/ppermute | solution.py:358
  34.8 2.8 %collective-permute-done.4.refs_1_ = f32[264,128]{1,0:T(8,128)S(1)} collective-permute-done((f32[264,128]{1,0:T(8,128)S(1)}, f32[264,128]{1,0:T(8,128)S(1)}, u32[]{:S(2)}, u32[]{:S(2)}) %collective-permute-start.4) | collective-permute-done | bytes 135200 | tf_op jit(solution)/shard_map/ppermute | solution.py:358
  37.6 2.5 %collective-permute-start.10 = (f32[264,128]{1,0:T(8,128)S(1)}, f32[264,128]{1,0:T(8,128)S(1)}, u32[]{:S(2)}, u32[]{:S(2)}) collective-permute-start(f32[264,128]{1,0:T(8,128)S(1)} %get-tuple-element.37), channel_id=1, source_target_pairs={{0,7},{1,6},{2,5},{3,4},{4,3},{5,2},{6,1},{7,0},{8,15},{9,14},{10,... | collective-permute-start | bytes 405512 | tf_op jit(solution)/shard_map/ppermute | solution.py:358
  40.2 1.7 %collective-permute-done.12.refs_3_.refs_2_ = f32[264,128]{1,0:T(8,128)S(1)} collective-permute-done((f32[264,128]{1,0:T(8,128)S(1)}, f32[264,128]{1,0:T(8,128)S(1)}, u32[]{:S(2)}, u32[]{:S(2)}) %collective-permute-start.12) | collective-permute-done | bytes 135200 | tf_op jit(solution)/shard_map/ppermute | solution.py:358
  41.9 1.6 %sweeps_lower.1 = (f32[3,272,128]{2,1,0:T(8,128)S(1)}, f32[4,256,128]{2,1,0:T(8,128)S(1)}) custom-call(f32[264,128]{1,0:T(8,128)S(1)} %collective-permute-done.3.refs_0_, f32[264,128]{1,0:T(8,128)S(1)} %collective-permute-done.4.refs_1_, f32[264,128]{1,0:T(8,128)S(1)} %collective-permute-done.11.refs_2_.refs_3_, ...), custom_call_target="tpu_custom_call" | custom-call | flops 1000000000 | bytes 1048576 | tf_op jit(solution)/shard_map/sweeps_lower/pallas_call | solution.py:410
  43.5 1.7 %collective-permute-done.10.refs_3_ = f32[264,128]{1,0:T(8,128)S(1)} collective-permute-done((f32[264,128]{1,0:T(8,128)S(1)}, f32[264,128]{1,0:T(8,128)S(1)}, u32[]{:S(2)}, u32[]{:S(2)}) %collective-permute-start.10) | collective-permute-done | bytes 135200 | tf_op jit(solution)/shard_map/ppermute | solution.py:358
  45.2 1.6 %sweeps_far.1 = (f32[256,128]{1,0:T(8,128)S(1)}, f32[256,128]{1,0:T(8,128)S(1)}, f32[256,128]{1,0:T(8,128)S(1)}, f32[256,128]{1,0:T(8,128)S(1)}, f32[3,272,128]{2,1,0:T(8,128)S(1)}) custom-call(f32[264,128]{1,0:T(8,128)S(1)} %collective-permute-done.3.refs_0_, f32[264,128]{1,0:T(8,128)S(1)} %collective-permute-done.4.refs_1_, ...), custom_call_target="tpu_custom_call" | custom-call | flops 1000000000 | bytes 1048576 | tf_op jit(solution)/shard_map/sweeps_far/pallas_call | solution.py:418
  46.8 2.5 %collective-permute-start.14 = (f32[256,128]{1,0:T(8,128)S(1)}, f32[256,128]{1,0:T(8,128)S(1)}, u32[]{:S(2)}, u32[]{:S(2)}) collective-permute-start(f32[256,128]{1,0:T(8,128)S(1)} %get-tuple-element.43), channel_id=1, source_target_pairs={{0,4},{1,5},{2,6},{3,7},{4,0},{5,1},{6,2},{7,3},{8,12},{9,13},{10,... | collective-permute-start | bytes 393224 | tf_op jit(solution)/shard_map/ppermute | solution.py:358
  49.4 2.1 %collective-permute-start.16 = (f32[256,128]{1,0:T(8,128)S(1)}, f32[256,128]{1,0:T(8,128)S(1)}, u32[]{:S(2)}, u32[]{:S(2)}) collective-permute-start(f32[256,128]{1,0:T(8,128)S(1)} %get-tuple-element.45), channel_id=1, source_target_pairs={{0,6},{1,7},{2,4},{3,5},{4,2},{5,3},{6,0},{7,1},{8,14},{9,15},{10,... | collective-permute-start | bytes 393224 | tf_op jit(solution)/shard_map/ppermute | solution.py:358
  53.1 9.6 %collective-permute-done.14.refs_0_ = f32[256,128]{1,0:T(8,128)S(1)} collective-permute-done((f32[256,128]{1,0:T(8,128)S(1)}, f32[256,128]{1,0:T(8,128)S(1)}, u32[]{:S(2)}, u32[]{:S(2)}) %collective-permute-start.14) | collective-permute-done | bytes 131104 | tf_op jit(solution)/shard_map/ppermute | solution.py:358
  63.7 2.8 %collective-permute-start.19 = (f32[256,128]{1,0:T(8,128)S(1)}, f32[256,128]{1,0:T(8,128)S(1)}, u32[]{:S(2)}, u32[]{:S(2)}) collective-permute-start(f32[256,128]{1,0:T(8,128)S(1)} %get-tuple-element.50), channel_id=1, source_target_pairs={{0,7},{1,6},{2,5},{3,4},{4,3},{5,2},{6,1},{7,0},{8,15},{9,14},{10,... | collective-permute-start | bytes 393224 | tf_op jit(solution)/shard_map/ppermute | solution.py:358
  67.4 2.6 %collective-permute-done.19.refs_5_ = f32[256,128]{1,0:T(8,128)S(1)} collective-permute-done((f32[256,128]{1,0:T(8,128)S(1)}, f32[256,128]{1,0:T(8,128)S(1)}, u32[]{:S(2)}, u32[]{:S(2)}) %collective-permute-start.19) | collective-permute-done | bytes 131104 | tf_op jit(solution)/shard_map/ppermute | solution.py:358
  (36 shorter events, 8.2 us)
Async XLA Ops:
  1.7 16.5 %collective-permute-start.8 = (f32[256,128]{1,0:T(8,128)}, f32[256,128]{1,0:T(8,128)S(1)}, u32[]{:S(2)}, u32[]{:S(2)}) collective-permute-start(f32[256,128]{1,0:T(8,128)} %get-tuple-element.36.refs_0_), channel_id=1, source_target_pairs={{0,6},{1,7},{2,4},{3,5},{4,2},{5,3},{6,0},{7,1},{8,14},{9,15},{10,... | collective-permute-start | bytes 393224 | tf_op jit(solution)/shard_map/ppermute | solution.py:358
  6.8 11.4 %collective-permute-start.7 = (f32[256,128]{1,0:T(8,128)}, f32[256,128]{1,0:T(8,128)S(1)}, u32[]{:S(2)}, u32[]{:S(2)}) collective-permute-start(f32[256,128]{1,0:T(8,128)} %get-tuple-element.36.refs_0_), channel_id=1, source_target_pairs={{0,4},{1,5},{2,6},{3,7},{4,0},{5,1},{6,2},{7,3},{8,12},{9,13},{10,... | collective-permute-start | bytes 393224 | tf_op jit(solution)/shard_map/ppermute | solution.py:358
  6.8 5.4 %collective-permute-start.1 = (f32[10,8,128]{2,1,0:T(8,128)}, f32[10,8,128]{2,1,0:T(8,128)S(1)}, u32[]{:S(2)}, u32[]{:S(2)}) collective-permute-start(f32[10,8,128]{2,1,0:T(8,128)} %get-tuple-element.29.own.start), channel_id=1, source_target_pairs={{0,16},{8,24},{16,0},{24,8},{1,17},{9,25},{17,1},{25,9},{2,18},{10... | collective-permute-start | bytes 122888 | tf_op jit(solution)/shard_map/ppermute | solution.py:358
  8.4 4.6 %collective-permute-start = (f32[12,8,128]{2,1,0:T(8,128)}, f32[12,8,128]{2,1,0:T(8,128)S(1)}, u32[]{:S(2)}, u32[]{:S(2)}) collective-permute-start(f32[12,8,128]{2,1,0:T(8,128)} %get-tuple-element.30), channel_id=1, source_target_pairs={{0,8},{8,0},{16,24},{24,16},{1,9},{9,1},{17,25},{25,17},{2,10},{10... | collective-permute-start | bytes 147464 | tf_op jit(solution)/shard_map/ppermute | solution.py:358
  9.9 2.4 %copy-start.1 = (f32[256,128]{1,0:T(8,128)S(1)}, f32[256,128]{1,0:T(8,128)}, u32[]{:S(2)}) copy-start(f32[256,128]{1,0:T(8,128)} %get-tuple-element.36.refs_0_) | copy-start | bytes 393220
  9.9 5.2 %copy-start = (f32[8,256,128]{2,1,0:T(8,128)S(1)}, f32[8,256,128]{2,1,0:T(8,128)}, u32[]{:S(2)}) copy-start(f32[8,256,128]{2,1,0:T(8,128)} %adj.5) | copy-start | bytes 3145732
  9.9 5.2 %collective-permute-start.2 = (f32[12,8,128]{2,1,0:T(8,128)}, f32[12,8,128]{2,1,0:T(8,128)S(1)}, u32[]{:S(2)}, u32[]{:S(2)}) collective-permute-start(f32[12,8,128]{2,1,0:T(8,128)} %get-tuple-element.31), channel_id=1, source_target_pairs={{0,24},{8,16},{16,8},{24,0},{1,25},{9,17},{17,9},{25,1},{2,26},{10... | collective-permute-start | bytes 147464 | tf_op jit(solution)/shard_map/ppermute | solution.py:358
  10.3 0.8 %copy-start.2 = (f32[10,8,128]{2,1,0:T(8,128)S(1)}, f32[10,8,128]{2,1,0:T(8,128)}, u32[]{:S(2)}) copy-start(f32[10,8,128]{2,1,0:T(8,128)} %get-tuple-element.29.own.start) | copy-start | bytes 122884
  12.2 7.1 %collective-permute-start.6 = (f32[256,128]{1,0:T(8,128)S(1)}, f32[256,128]{1,0:T(8,128)S(1)}, u32[]{:S(2)}, u32[]{:S(2)}) collective-permute-start(f32[256,128]{1,0:T(8,128)S(1)} %copy-done.1), channel_id=1, source_target_pairs={{0,2},{1,3},{2,0},{3,1},{4,6},{5,7},{6,4},{7,5},{8,10},{9,11},{10,... | collective-permute-start | bytes 393224 | tf_op jit(solution)/shard_map/ppermute | solution.py:358
  19.4 5.2 %collective-permute-start.9 = (f32[4,256,128]{2,1,0:T(8,128)S(1)}, f32[4,256,128]{2,1,0:T(8,128)S(1)}, u32[]{:S(2)}, u32[]{:S(2)}) collective-permute-start(f32[4,256,128]{2,1,0:T(8,128)S(1)} %stack.1.mine), channel_id=1, source_target_pairs={{0,1},{1,0},{2,3},{3,2},{4,5},{5,4},{6,7},{7,6},{8,9},{9,8},{10,11... | collective-permute-start | bytes 1572872 | tf_op jit(solution)/shard_map/ppermute | solution.py:358
  19.5 15.4 %collective-permute-start.3 = (f32[264,128]{1,0:T(8,128)S(1)}, f32[264,128]{1,0:T(8,128)S(1)}, u32[]{:S(2)}, u32[]{:S(2)}) collective-permute-start(f32[264,128]{1,0:T(8,128)S(1)} %get-tuple-element.32), channel_id=1, source_target_pairs={{0,4},{1,5},{2,6},{3,7},{4,0},{5,1},{6,2},{7,3},{8,12},{9,13},{10,... | collective-permute-start | bytes 405512 | tf_op jit(solution)/shard_map/ppermute | solution.py:358
  21.4 16.2 %collective-permute-start.4 = (f32[264,128]{1,0:T(8,128)S(1)}, f32[264,128]{1,0:T(8,128)S(1)}, u32[]{:S(2)}, u32[]{:S(2)}) collective-permute-start(f32[264,128]{1,0:T(8,128)S(1)} %get-tuple-element.33), channel_id=1, source_target_pairs={{0,5},{1,4},{2,7},{3,6},{4,1},{5,0},{6,3},{7,2},{8,13},{9,12},{10,... | collective-permute-start | bytes 405512 | tf_op jit(solution)/shard_map/ppermute | solution.py:358
  22.2 17.9 %collective-permute-start.5 = (f32[264,128]{1,0:T(8,128)S(1)}, f32[264,128]{1,0:T(8,128)S(1)}, u32[]{:S(2)}, u32[]{:S(2)}) collective-permute-start(f32[264,128]{1,0:T(8,128)S(1)} %get-tuple-element.34), channel_id=1, source_target_pairs={{0,6},{1,7},{2,4},{3,5},{4,2},{5,3},{6,0},{7,1},{8,14},{9,15},{10,... | collective-permute-start | bytes 405512 | tf_op jit(solution)/shard_map/ppermute | solution.py:358
  24.5 15.6 %collective-permute-start.11 = (f32[264,128]{1,0:T(8,128)S(1)}, f32[264,128]{1,0:T(8,128)S(1)}, u32[]{:S(2)}, u32[]{:S(2)}) collective-permute-start(f32[264,128]{1,0:T(8,128)S(1)} %get-tuple-element.38), channel_id=1, source_target_pairs={{0,3},{1,2},{2,1},{3,0},{4,7},{5,6},{6,5},{7,4},{8,11},{9,10},{10,... | collective-permute-start | bytes 405512 | tf_op jit(solution)/shard_map/ppermute | solution.py:358
  29.7 12.2 %collective-permute-start.12 = (f32[264,128]{1,0:T(8,128)S(1)}, f32[264,128]{1,0:T(8,128)S(1)}, u32[]{:S(2)}, u32[]{:S(2)}) collective-permute-start(f32[264,128]{1,0:T(8,128)S(1)} %get-tuple-element.39), channel_id=1, source_target_pairs={{0,2},{1,3},{2,0},{3,1},{4,6},{5,7},{6,4},{7,5},{8,10},{9,11},{10,... | collective-permute-start | bytes 405512 | tf_op jit(solution)/shard_map/ppermute | solution.py:358
  34.8 7.1 %collective-permute-start.13 = (f32[264,128]{1,0:T(8,128)S(1)}, f32[264,128]{1,0:T(8,128)S(1)}, u32[]{:S(2)}, u32[]{:S(2)}) collective-permute-start(f32[264,128]{1,0:T(8,128)S(1)} %get-tuple-element.40), channel_id=1, source_target_pairs={{0,1},{1,0},{2,3},{3,2},{4,5},{5,4},{6,7},{7,6},{8,9},{9,8},{10,11... | collective-permute-start | bytes 405512 | tf_op jit(solution)/shard_map/ppermute | solution.py:358
  37.6 7.5 %collective-permute-start.10 = (f32[264,128]{1,0:T(8,128)S(1)}, f32[264,128]{1,0:T(8,128)S(1)}, u32[]{:S(2)}, u32[]{:S(2)}) collective-permute-start(f32[264,128]{1,0:T(8,128)S(1)} %get-tuple-element.37), channel_id=1, source_target_pairs={{0,7},{1,6},{2,5},{3,4},{4,3},{5,2},{6,1},{7,0},{8,15},{9,14},{10,... | collective-permute-start | bytes 405512 | tf_op jit(solution)/shard_map/ppermute | solution.py:358
  46.8 15.8 %collective-permute-start.14 = (f32[256,128]{1,0:T(8,128)S(1)}, f32[256,128]{1,0:T(8,128)S(1)}, u32[]{:S(2)}, u32[]{:S(2)}) collective-permute-start(f32[256,128]{1,0:T(8,128)S(1)} %get-tuple-element.43), channel_id=1, source_target_pairs={{0,4},{1,5},{2,6},{3,7},{4,0},{5,1},{6,2},{7,3},{8,12},{9,13},{10,... | collective-permute-start | bytes 393224 | tf_op jit(solution)/shard_map/ppermute | solution.py:358
  49.3 14.4 %collective-permute-start.15 = (f32[256,128]{1,0:T(8,128)S(1)}, f32[256,128]{1,0:T(8,128)S(1)}, u32[]{:S(2)}, u32[]{:S(2)}) collective-permute-start(f32[256,128]{1,0:T(8,128)S(1)} %get-tuple-element.44), channel_id=1, source_target_pairs={{0,5},{1,4},{2,7},{3,6},{4,1},{5,0},{6,3},{7,2},{8,13},{9,12},{10,... | collective-permute-start | bytes 393224 | tf_op jit(solution)/shard_map/ppermute | solution.py:358
  49.4 17.2 %collective-permute-start.16 = (f32[256,128]{1,0:T(8,128)S(1)}, f32[256,128]{1,0:T(8,128)S(1)}, u32[]{:S(2)}, u32[]{:S(2)}) collective-permute-start(f32[256,128]{1,0:T(8,128)S(1)} %get-tuple-element.45), channel_id=1, source_target_pairs={{0,6},{1,7},{2,4},{3,5},{4,2},{5,3},{6,0},{7,1},{8,14},{9,15},{10,... | collective-permute-start | bytes 393224 | tf_op jit(solution)/shard_map/ppermute | solution.py:358
  51.5 15.1 %collective-permute-start.17 = (f32[256,128]{1,0:T(8,128)S(1)}, f32[256,128]{1,0:T(8,128)S(1)}, u32[]{:S(2)}, u32[]{:S(2)}) collective-permute-start(f32[256,128]{1,0:T(8,128)S(1)} %get-tuple-element.48), channel_id=1, source_target_pairs={{0,3},{1,2},{2,1},{3,0},{4,7},{5,6},{6,5},{7,4},{8,11},{9,10},{10,... | collective-permute-start | bytes 393224 | tf_op jit(solution)/shard_map/ppermute | solution.py:358
  52.4 15.0 %collective-permute-start.18 = (f32[256,128]{1,0:T(8,128)S(1)}, f32[256,128]{1,0:T(8,128)S(1)}, u32[]{:S(2)}, u32[]{:S(2)}) collective-permute-start(f32[256,128]{1,0:T(8,128)S(1)} %get-tuple-element.49), channel_id=1, source_target_pairs={{0,2},{1,3},{2,0},{3,1},{4,6},{5,7},{6,4},{7,5},{8,10},{9,11},{10,... | collective-permute-start | bytes 393224 | tf_op jit(solution)/shard_map/ppermute | solution.py:358
  62.7 4.7 %collective-permute-start.20 = (f32[256,128]{1,0:T(8,128)S(1)}, f32[256,128]{1,0:T(8,128)S(1)}, u32[]{:S(2)}, u32[]{:S(2)}) collective-permute-start(f32[256,128]{1,0:T(8,128)S(1)} %get-tuple-element.51), channel_id=1, source_target_pairs={{0,1},{1,0},{2,3},{3,2},{4,5},{5,4},{6,7},{7,6},{8,9},{9,8},{10,11... | collective-permute-start | bytes 393224 | tf_op jit(solution)/shard_map/ppermute | solution.py:358
  63.7 6.3 %collective-permute-start.19 = (f32[256,128]{1,0:T(8,128)S(1)}, f32[256,128]{1,0:T(8,128)S(1)}, u32[]{:S(2)}, u32[]{:S(2)}) collective-permute-start(f32[256,128]{1,0:T(8,128)S(1)} %get-tuple-element.50), channel_id=1, source_target_pairs={{0,7},{1,6},{2,5},{3,4},{4,3},{5,2},{6,1},{7,0},{8,15},{9,14},{10,... | collective-permute-start | bytes 393224 | tf_op jit(solution)/shard_map/ppermute | solution.py:358
  (1 other events, 0.8 us)

commit v4 on v3

--- a/solution.py
+++ b/solution.py
@@ -42,29 +42,14 @@
     return lax.bitwise_xor(lax.axis_index("span"), i)
 
 
-def pack_kernel(flux, owner, cell, adj, inverse, gain, near, far, diag, operators, *scratch):
-    faces, owners, cells, first, last, sems = scratch
-    groups, circum, block_rows = owner.shape[0], adj.shape[1], inverse.shape[0]
+def pack_kernel(flux, owner, cell, first, last, near, far, diag):
+    groups = owner.shape[0]
     odd = lax.rem(lax.axis_index("blade"), 2)
-    pairs = (
-        (flux, faces),
-        (owner, owners),
-        (cell, cells),
-        (adj.at[:, 0:8, :], first),
-        (adj.at[:, circum - 8 : circum, :], last),
-        (inverse, operators.at[0:block_rows, :]),
-        (gain, operators.at[block_rows : 2 * block_rows, :]),
-    )
-    copies = [pltpu.make_async_copy(a, b, sems.at[i]) for i, (a, b) in enumerate(pairs)]
-    for copy in copies:
-        copy.start()
-    for copy in copies:
-        copy.wait()
     for message in (near, far, diag):
         for group in range(groups):
-            message[group] = faces[:, group * 128 : (group + 1) * 128]
-        message[groups] = owners[...].astype(F32)
-        message[groups + 1] = cells[...].astype(F32)
+            message[group] = flux[:, group * 128 : (group + 1) * 128]
+        message[groups] = owner[...].astype(F32)
+        message[groups + 1] = cell[...].astype(F32)
     for row in range(HALO):
         low = first[:, row, :]
         high = last[:, 8 - HALO + row, :]
@@ -72,34 +57,24 @@
         diag[groups + 2 + row] = jnp.where(odd == 0, low, high)
 
 
-def pack(adj_source, face_flux, face_owner, face_cell, block_inverse, carry_gain):
+def pack(adj_source, face_flux, face_owner, face_cell):
     groups = face_owner.shape[0] // 128
-    block_rows = adj_source.shape[2]
+    circum = adj_source.shape[1]
     with_halo = ((groups + 2 + HALO, 8, 128), F32)
     faces = ((groups + 2, 8, 128), F32)
-    edge = pltpu.VMEM((8, 8, block_rows), F32)
     return call(
         pack_kernel,
-        (with_halo, faces, with_halo, ((2 * block_rows, block_rows), F32)),
-        [HBM] * 6,
-        [
-            pltpu.VMEM(face_flux.shape, F32),
-            pltpu.VMEM((groups, 128), jnp.int32),
-            pltpu.VMEM((groups, 128), jnp.int32),
-            edge,
-            edge,
-            pltpu.SemaphoreType.DMA((7,)),
-        ],
+        (with_halo, faces, with_halo),
+        [VMEM] * 5,
+        [],
         0,
         "pack",
-        vmem=60,
     )(
         face_flux,
         face_owner.reshape(groups, 128),
         face_cell.reshape(groups, 128),
-        adj_source,
-        block_inverse,
-        carry_gain,
+        adj_source[:, :8],
+        adj_source[:, circum - 8 :],
     )
 
 
@@ -142,27 +117,30 @@
     )
 
 
-def own_faces_kernel(peers, own, acc, hot_rows, weights):
-    block_rows = 128
-    circum = acc.shape[0] - 16
+def face_sums_kernel(peers, *refs):
+    *start, message, acc, hot_rows, weights = refs
+    circum, block_rows = acc.shape[0] - 16, acc.shape[1] // len(peers)
     harmonics = [peer(i) for i in peers]
-    acc[...] = face_product(own, hot_rows, weights, harmonics, circum, block_rows)
-
-
-def own_faces(peers, own, circum):
-    faces = (own.shape[0] - 2) * 128
-    rows, lanes = circum + 16, len(peers) * 128
+    sums = face_product(message, hot_rows, weights, harmonics, circum, block_rows)
+    for before in start:
+        sums += before[...]
+    acc[...] = sums
+
+
+def face_sums(peers, circum, block_rows, message, *start):
+    faces = (message.shape[0] - 2) * 128
+    rows, lanes = circum + 16, len(peers) * block_rows
     return call(
-        functools.partial(own_faces_kernel, peers),
+        functools.partial(face_sums_kernel, peers),
         (((rows, lanes), F32),),
-        [VMEM],
+        [VMEM] * (1 + len(start)),
         [pltpu.VMEM((rows, 2 * faces), BF16), pltpu.VMEM((lanes, 2 * faces), BF16)],
         600_000_000,
-        "own_faces",
-    )(own)[0]
-
-
-def right_kernel(peers, own, adj, start, near, far, diag, *rest):
+        "face_sums",
+    )(*start, message)[0]
+
+
+def right_kernel(peers, own, adj, start, diag, near, far, *rest):
     count = len(peers)
     *outs, hot_rows, weights, acc, source, sems = rest
     del outs[: len(outs) - count - 1]
@@ -177,10 +155,8 @@
     groups = weights.shape[2] // 256
     odd = lax.rem(lax.axis_index("blade"), 2)
     harmonics = [peer(i) for i in peers]
-    messages = (near, far, diag)
-    if own:
-        messages = (start, *messages)
-    else:
+    messages = (start, near, far, diag) if own else (diag, near)
+    if not own:
         acc[...] = start[...]
     for step, message in enumerate(messages):
         product = face_product(
@@ -209,20 +185,21 @@
 def right_pieces(peers, own, adj_source, start, messages, after, name):
     _, circum, block_rows = adj_source.shape
     count = len(peers)
-    faces = (messages[1].shape[0] - 2) * 128
+    faces = (min(m.shape[0] for m in messages) - 2) * 128
     rows = circum + 16
+    sums = 4 if own else 2
     return call(
         functools.partial(right_kernel, peers, own),
         (((circum + 8, block_rows), F32),) * count + (((8, 128), F32),),
         [HBM] + [VMEM] * 4 + [ANY] * len(after),
         [
-            pltpu.VMEM((3 + own, rows, 2 * faces), BF16),
-            pltpu.VMEM((3 + own, count * block_rows, 2 * faces), BF16),
+            pltpu.VMEM((sums, rows, 2 * faces), BF16),
+            pltpu.VMEM((sums, count * block_rows, 2 * faces), BF16),
             pltpu.VMEM((rows, count * block_rows), F32),
             pltpu.VMEM((count, circum, block_rows), F32),
             pltpu.SemaphoreType.DMA((count,)),
         ],
-        1_800_000_000,
+        600_000_000 * sums,
         name,
     )(adj_source, start, *messages, *after)
 
@@ -273,21 +250,44 @@
 
 
 def stack_kernel(*refs):
-    *pieces, _, out = refs
-    for i, piece in enumerate(pieces):
-        out[i] = piece[...]
-
-
-def operators_kernel(mine, partner, weights):
-    block_rows = mine.shape[2]
-    for i in range(weights.shape[0]):
-        k = peer(i)
-        source = (mine, partner)[i % 2]
-        for matrix in range(2):
-            part = slice(matrix * block_rows, (matrix + 1) * block_rows)
-            hi, lo = split(source[i // 2, part, :])
-            weights[k, 0:block_rows, part] = hi
-            weights[k, block_rows : 2 * block_rows, part] = lo
+    *pieces, out = refs
+    at = 0
+    for piece in pieces:
+        if piece.shape[0] > 8:
+            out[at : at + piece.shape[0], :] = piece[...]
+            at += piece.shape[0]
+
+
+def stack(*pieces):
+    rows = sum(piece.shape[0] for piece in pieces if piece.shape[0] > 8)
+    return call(
+        stack_kernel,
+        (((rows, pieces[0].shape[1]), F32),),
+        [VMEM] * len(pieces),
+        [],
+        0,
+        "stack",
+    )(*pieces)[0]
+
+
+def operators_kernel(chip, across, partner, weights):
+    block_rows = chip.shape[1]
+    first = 2 + 2 * lax.rem(lax.axis_index("span"), 2)
+    second = lax.bitwise_xor(first, 6)
+    places = (
+        (chip, (0, 1)),
+        (across, (first, first + 1, 6)),
+        (partner, (second + 1, second, 7)),
+    )
+    for source, bits in places:
+        for at, i in enumerate(bits):
+            k = peer(i)
+            for matrix in range(2):
+                low = (2 * at + matrix) * block_rows
+                part = slice(matrix * block_rows, (matrix + 1) * block_rows)
+                hi, lo = split(source[low : low + block_rows, :])
+                weights[k, 0:block_rows, part] = hi
+                weights[k, block_rows : 2 * block_rows, part] = lo
 
 
 def lower_kernel(half, near, *refs):
@@ -362,38 +362,33 @@
     harm_rows, circum, block_rows = adj_source.shape
     count = lax.axis_size("span")
     half = count // 2
-    near, far, diag, operators = pack(
-        adj_source, face_flux, face_owner, face_cell, block_inverse, carry_gain
-    )
+    operators = jnp.concatenate([block_inverse, carry_gain], axis=0)
+    near, far, diag = pack(adj_source, face_flux, face_owner, face_cell)
     messages = [
+        exchange(diag, "blade", 3),
         exchange(near, "blade", 1),
         exchange(far, "blade", 2),
-        exchange(diag, "blade", 3),
     ]
-    operators = [operators] + [exchange(operators, "span", bits) for bits in range(2, count, 2)]
+    chip = stack(operators, exchange(operators, "span", 1))
+    apart = lax.ppermute(chip, "span", [(i, i ^ (2 + 2 * (i % 2))) for i in range(count)])
+    farthest = exchange(operators, "span", 6)
     first, second = (4, 5, 6, 3), (2, 7, 1, 0)
-    start = own_faces(first, far, circum)
+    start = face_sums(first, circum, block_rows, far)
+    start = face_sums(first, circum, block_rows, messages[2], start)
     *pieces, token = right_pieces(
         first, False, adj_source, start, messages, [], "right_first"
     )
     right_side = dict(zip(first, pieces, strict=True))
-    mine = call(
-        stack_kernel,
-        (((half, *operators[0].shape), F32),),
-        [VMEM] * half + [ANY],
-        [],
-        0,
-        "stack",
-    )(*operators, token)[0]
-    partner = exchange(mine, "span", 1)
+    across = stack(apart, farthest, token)
+    partner = exchange(across, "span", 1)
     weights = call(
         operators_kernel,
         (((count, 2 * block_rows, 2 * block_rows), BF16),),
-        [VMEM] * 2,
+        [VMEM] * 3,
         [],
         0,
         "operators",
-    )(mine, partner)[0]
+    )(chip, across, partner)[0]
     *pieces, _ = right_pieces(
         second, True, adj_source, far, messages, [token, weights], "right_second"
     )

time: 72.3 us -> 70.8 us (0.979); the launches traced: 71.1 us -> 70.5 us
  Pallas kernels: 14.9 us -> 13.6 us
  local copies, waits for them, and re-layouts: 1.37 us -> 2.36 us
    slice x0 -> x1, local copies, waits for them, and re-layouts: none -> 0.79 us  [pack(): adj_source[:, circum - 8:]]
    ppermute x21 -> x20, waiting for transfers between devices: 27.4 us -> 26.7 us  [exchange(): return lax.ppermute(array, axis, [(i, i ^ bits) for i in range(count)])]
    pallas_call x3 -> x5, Pallas kernels: 2.83 us -> 2.23 us  [the longest x2 2.16 us: face_sums(): call(functools.partial(face_sums_kernel, peers), (((rows, lanes), F32),),...]
    ppermute x21 -> x20, starting transfers between devices: 27.3 us -> 27.6 us  [exchange(): return lax.ppermute(array, axis, [(i, i ^ bits) for i in range(count)])]
    unnamed x8 -> x11, local copies, waits for them, and re-layouts: 1.37 us -> 1.57 us
  transfers between devices with their start and end apart: 21 -> 21, of which waited for: 10 -> 10; matrix products, arithmetic and copies ran while one was open for 0% -> 1% of each run, Pallas kernels for 15% -> 16%
where the time goes in v4:
time: 70.8 us; the launch traced here: 70.5 us
  starting transfers between devices  27.7 us (39%)
  waiting for transfers between devices  26.7 us (38%)
  Pallas kernels  13.6 us (19%)
  local copies, waits for them, and re-layouts  2.36 us (3%)
    ppermute x20, starting transfers between devices, exchange(): return lax.ppermute(array, axis, [(i, i ^ bits) for i in range(count)])  27.6 us
    ppermute x20, waiting for transfers between devices, exchange(): return lax.ppermute(array, axis, [(i, i ^ bits) for i in range(count)])  26.7 us
    pallas_call x2, Pallas kernels, right_pieces(): call(functools.partial(right_kernel, peers, own), (((circum + 8, block_ro...  6.98 us
    pallas_call x2, Pallas kernels, face_sums(): call(functools.partial(face_sums_kernel, peers), (((rows, lanes), F32),),...  2.16 us
    pallas_call x1, Pallas kernels, by_harmonics(): call(functools.partial(far_kernel, half), (piece,) * half + (state_shape,...  1.65 us
    unnamed x11, local copies, waits for them, and re-layouts  1.57 us
    pallas_call x1, Pallas kernels, by_harmonics(): call(functools.partial(lower_kernel, half, (6, 5, 3, 2)), (state_shape, (...  1.56 us
  transfers between devices with their start and end apart: 21, of which 10 were waited for; matrix products, arithmetic and copies ran while one was open for 1% of the time, Pallas kernels for 16%

profile of v4, /device:TPU:0, one launch (start us, length us, event | category | flops | bytes accessed | tf_op | source)
XLA Modules:
  0.0 70.5 jit_solution(17446770184650193674)
XLA Ops:
  1.4 4.7 %collective-permute-start.8 = (f32[256,128]{1,0:T(8,128)S(1)}, f32[256,128]{1,0:T(8,128)S(1)}, u32[]{:S(2)}, u32[]{:S(2)}) collective-permute-start(f32[256,128]{1,0:T(8,128)S(1)} %constant_dynamic-update-slice_fusion.refs_0_), channel_id=1, source_target_pairs={{0,6},{1,7},{2,4},{3,5},{4,2},{5,3},{6,0},{7,1},{8,14},{9,15},{10,... | collective-permute-start | bytes 393224 | tf_op jit(solution)/shard_map/ppermute | solution.py:358
  7.7 1.6 %collective-permute-start = (f32[10,8,128]{2,1,0:T(8,128)S(1)}, f32[10,8,128]{2,1,0:T(8,128)S(1)}, u32[]{:S(2)}, u32[]{:S(2)}) collective-permute-start(f32[10,8,128]{2,1,0:T(8,128)S(1)} %get-tuple-element.28.refs_0_.start), channel_id=1, source_target_pairs={{0,16},{8,24},{16,0},{24,8},{1,17},{9,25},{17,1},{25,9},{2,18},{10... | collective-permute-start | bytes 122888 | tf_op jit(solution)/shard_map/ppermute | solution.py:358
  9.3 1.4 %collective-permute-start.1 = (f32[12,8,128]{2,1,0:T(8,128)S(1)}, f32[12,8,128]{2,1,0:T(8,128)S(1)}, u32[]{:S(2)}, u32[]{:S(2)}) collective-permute-start(f32[12,8,128]{2,1,0:T(8,128)S(1)} %get-tuple-element.29), channel_id=1, source_target_pairs={{0,24},{8,16},{16,8},{24,0},{1,25},{9,17},{17,9},{25,1},{2,26},{10... | collective-permute-start | bytes 147464 | tf_op jit(solution)/shard_map/ppermute | solution.py:358
  11.3 1.1 %face_sums.2.refs_0_ = f32[272,512]{1,0:T(8,128)S(1)} custom-call(f32[10,8,128]{2,1,0:T(8,128)S(1)} %get-tuple-element.28.refs_0_.start), custom_call_target="tpu_custom_call" | custom-call | flops 600000000 | bytes 1048576 | tf_op jit(solution)/shard_map/face_sums/pallas_call | solution.py:133
  12.4 1.1 %face_sums.3.start = f32[272,512]{1,0:T(8,128)S(1)} custom-call(f32[272,512]{1,0:T(8,128)S(1)} %face_sums.2.refs_0_, f32[10,8,128]{2,1,0:T(8,128)S(1)} %collective-permute-done.refs_1_.far), custom_call_target="tpu_custom_call" | custom-call | flops 600000000 | bytes 1048576 | tf_op jit(solution)/shard_map/face_sums/pallas_call | solution.py:133
  13.5 1.2 %collective-permute-done.1.diag = f32[12,8,128]{2,1,0:T(8,128)S(1)} collective-permute-done((f32[12,8,128]{2,1,0:T(8,128)S(1)}, f32[12,8,128]{2,1,0:T(8,128)S(1)}, u32[]{:S(2)}, u32[]{:S(2)}) %collective-permute-start.1) | collective-permute-done | bytes 49184 | tf_op jit(solution)/shard_map/ppermute | solution.py:358
  14.8 2.5 %right_first.1 = (f32[264,128]{1,0:T(8,128)S(1)}, f32[264,128]{1,0:T(8,128)S(1)}, f32[264,128]{1,0:T(8,128)S(1)}, f32[264,128]{1,0:T(8,128)S(1)}, f32[8,128]{1,0:T(8,128)S(1)}) custom-call(f32[8,256,128]{2,1,0:T(8,128)S(1)} %copy-done.1, f32[272,512]{1,0:T(8,128)S(1)} %face_sums.3.start, f32[12,8,128]{2,1,0:T(8,128)S(1)} %collective-permute-done.1.diag, ...), custom_call_target="tpu_custom_call" | custom-call | flops 1200000000 | bytes 1048576 | tf_op jit(solution)/shard_map/right_first/pallas_call | solution.py:191
  17.7 1.7 %collective-permute-start.3 = (f32[264,128]{1,0:T(8,128)S(1)}, f32[264,128]{1,0:T(8,128)S(1)}, u32[]{:S(2)}, u32[]{:S(2)}) collective-permute-start(f32[264,128]{1,0:T(8,128)S(1)} %get-tuple-element.31), channel_id=1, source_target_pairs={{0,4},{1,5},{2,6},{3,7},{4,0},{5,1},{6,2},{7,3},{8,12},{9,13},{10,... | collective-permute-start | bytes 405512 | tf_op jit(solution)/shard_map/ppermute | solution.py:358
  20.3 2.2 %collective-permute-start.5 = (f32[264,128]{1,0:T(8,128)S(1)}, f32[264,128]{1,0:T(8,128)S(1)}, u32[]{:S(2)}, u32[]{:S(2)}) collective-permute-start(f32[264,128]{1,0:T(8,128)S(1)} %get-tuple-element.33), channel_id=1, source_target_pairs={{0,6},{1,7},{2,4},{3,5},{4,2},{5,3},{6,0},{7,1},{8,14},{9,15},{10,... | collective-permute-start | bytes 405512 | tf_op jit(solution)/shard_map/ppermute | solution.py:358
  22.7 4.4 %right_second.1 = (f32[264,128]{1,0:T(8,128)S(1)}, f32[264,128]{1,0:T(8,128)S(1)}, f32[264,128]{1,0:T(8,128)S(1)}, f32[264,128]{1,0:T(8,128)S(1)}, f32[8,128]{1,0:T(8,128)}) custom-call(f32[8,256,128]{2,1,0:T(8,128)S(1)} %copy-done.1, f32[10,8,128]{2,1,0:T(8,128)S(1)} %get-tuple-element.28.refs_0_.start, f32[12,8,128]{2,1,0:T(8,128)S(1)} %collective-permute-done.1.diag, ...), custom_call_target="tpu_custom_call" | custom-call | flops 2400000000 | bytes 1048576 | tf_op jit(solution)/shard_map/right_second/pallas_call | solution.py:191
  27.1 2.1 %collective-permute-start.12 = (f32[264,128]{1,0:T(8,128)S(1)}, f32[264,128]{1,0:T(8,128)S(1)}, u32[]{:S(2)}, u32[]{:S(2)}) collective-permute-start(f32[264,128]{1,0:T(8,128)S(1)} %get-tuple-element.37), channel_id=1, source_target_pairs={{0,2},{1,3},{2,0},{3,1},{4,6},{5,7},{6,4},{7,5},{8,10},{9,11},{10,... | collective-permute-start | bytes 405512 | tf_op jit(solution)/shard_map/ppermute | solution.py:358
  29.3 4.5 %collective-permute-done.3.refs_0_ = f32[264,128]{1,0:T(8,128)S(1)} collective-permute-done((f32[264,128]{1,0:T(8,128)S(1)}, f32[264,128]{1,0:T(8,128)S(1)}, u32[]{:S(2)}, u32[]{:S(2)}) %collective-permute-start.3) | collective-permute-done | bytes 135200 | tf_op jit(solution)/shard_map/ppermute | solution.py:358
  33.8 1.7 %collective-permute-done.4.refs_1_ = f32[264,128]{1,0:T(8,128)S(1)} collective-permute-done((f32[264,128]{1,0:T(8,128)S(1)}, f32[264,128]{1,0:T(8,128)S(1)}, u32[]{:S(2)}, u32[]{:S(2)}) %collective-permute-start.4) | collective-permute-done | bytes 135200 | tf_op jit(solution)/shard_map/ppermute | solution.py:358
  35.5 2.8 %collective-permute-start.10 = (f32[264,128]{1,0:T(8,128)S(1)}, f32[264,128]{1,0:T(8,128)S(1)}, u32[]{:S(2)}, u32[]{:S(2)}) collective-permute-start(f32[264,128]{1,0:T(8,128)S(1)} %get-tuple-element.35), channel_id=1, source_target_pairs={{0,7},{1,6},{2,5},{3,4},{4,3},{5,2},{6,1},{7,0},{8,15},{9,14},{10,... | collective-permute-start | bytes 405512 | tf_op jit(solution)/shard_map/ppermute | solution.py:358
  38.9 1.6 %sweeps_lower.1 = (f32[3,272,128]{2,1,0:T(8,128)S(1)}, f32[4,256,128]{2,1,0:T(8,128)S(1)}) custom-call(f32[264,128]{1,0:T(8,128)S(1)} %collective-permute-done.3.refs_0_, f32[264,128]{1,0:T(8,128)S(1)} %collective-permute-done.4.refs_1_, f32[264,128]{1,0:T(8,128)S(1)} %collective-permute-done.11.refs_2_.refs_3_, ...), custom_call_target="tpu_custom_call" | custom-call | flops 1000000000 | bytes 1048576 | tf_op jit(solution)/shard_map/sweeps_lower/pallas_call | solution.py:405
  40.4 1.7 %collective-permute-done.10.refs_3_ = f32[264,128]{1,0:T(8,128)S(1)} collective-permute-done((f32[264,128]{1,0:T(8,128)S(1)}, f32[264,128]{1,0:T(8,128)S(1)}, u32[]{:S(2)}, u32[]{:S(2)}) %collective-permute-start.10) | collective-permute-done | bytes 135200 | tf_op jit(solution)/shard_map/ppermute | solution.py:358
  42.1 1.7 %sweeps_far.1 = (f32[256,128]{1,0:T(8,128)S(1)}, f32[256,128]{1,0:T(8,128)S(1)}, f32[256,128]{1,0:T(8,128)S(1)}, f32[256,128]{1,0:T(8,128)S(1)}, f32[3,272,128]{2,1,0:T(8,128)S(1)}) custom-call(f32[264,128]{1,0:T(8,128)S(1)} %collective-permute-done.3.refs_0_, f32[264,128]{1,0:T(8,128)S(1)} %collective-permute-done.4.refs_1_, ...), custom_call_target="tpu_custom_call" | custom-call | flops 1000000000 | bytes 1048576 | tf_op jit(solution)/shard_map/sweeps_far/pallas_call | solution.py:413
  43.8 3.5 %collective-permute-start.14 = (f32[256,128]{1,0:T(8,128)S(1)}, f32[256,128]{1,0:T(8,128)S(1)}, u32[]{:S(2)}, u32[]{:S(2)}) collective-permute-start(f32[256,128]{1,0:T(8,128)S(1)} %get-tuple-element.41), channel_id=1, source_target_pairs={{0,4},{1,5},{2,6},{3,7},{4,0},{5,1},{6,2},{7,3},{8,12},{9,13},{10,... | collective-permute-start | bytes 393224 | tf_op jit(solution)/shard_map/ppermute | solution.py:358
  47.3 2.1 %collective-permute-start.16 = (f32[256,128]{1,0:T(8,128)S(1)}, f32[256,128]{1,0:T(8,128)S(1)}, u32[]{:S(2)}, u32[]{:S(2)}) collective-permute-start(f32[256,128]{1,0:T(8,128)S(1)} %get-tuple-element.43), channel_id=1, source_target_pairs={{0,6},{1,7},{2,4},{3,5},{4,2},{5,3},{6,0},{7,1},{8,14},{9,15},{10,... | collective-permute-start | bytes 393224 | tf_op jit(solution)/shard_map/ppermute | solution.py:358
  50.7 9.4 %collective-permute-done.14.refs_0_ = f32[256,128]{1,0:T(8,128)S(1)} collective-permute-done((f32[256,128]{1,0:T(8,128)S(1)}, f32[256,128]{1,0:T(8,128)S(1)}, u32[]{:S(2)}, u32[]{:S(2)}) %collective-permute-start.14) | collective-permute-done | bytes 131104 | tf_op jit(solution)/shard_map/ppermute | solution.py:358
  60.1 2.2 %collective-permute-done.15.refs_1_ = f32[256,128]{1,0:T(8,128)S(1)} collective-permute-done((f32[256,128]{1,0:T(8,128)S(1)}, f32[256,128]{1,0:T(8,128)S(1)}, u32[]{:S(2)}, u32[]{:S(2)}) %collective-permute-start.15) | collective-permute-done | bytes 131104 | tf_op jit(solution)/shard_map/ppermute | solution.py:358
  62.3 2.0 %collective-permute-start.19 = (f32[256,128]{1,0:T(8,128)S(1)}, f32[256,128]{1,0:T(8,128)S(1)}, u32[]{:S(2)}, u32[]{:S(2)}) collective-permute-start(f32[256,128]{1,0:T(8,128)S(1)} %get-tuple-element.48), channel_id=1, source_target_pairs={{0,7},{1,6},{2,5},{3,4},{4,3},{5,2},{6,1},{7,0},{8,15},{9,14},{10,... | collective-permute-start | bytes 393224 | tf_op jit(solution)/shard_map/ppermute | solution.py:358
  64.7 4.8 %collective-permute-done.19.refs_5_ = f32[256,128]{1,0:T(8,128)S(1)} collective-permute-done((f32[256,128]{1,0:T(8,128)S(1)}, f32[256,128]{1,0:T(8,128)S(1)}, u32[]{:S(2)}, u32[]{:S(2)}) %collective-permute-start.19) | collective-permute-done | bytes 131104 | tf_op jit(solution)/shard_map/ppermute | solution.py:358
  69.5 1.0 %place.1 = f32[8,256,128]{2,1,0:T(8,128)} custom-call(f32[256,128]{1,0:T(8,128)S(1)} %collective-permute-done.14.refs_0_, f32[256,128]{1,0:T(8,128)S(1)} %collective-permute-done.15.refs_1_, f32[256,128]{1,0:T(8,128)S(1)} %collective-permute-done.16.refs_2_, f32[256,128]{1,0:T(8,128)S(1)} %collective-permute-done.17.refs_3_, ...), custom_call_target="tpu_custom_call" | custom-call | bytes 1048576 | tf_op jit(solution)/shard_map/place/pallas_call | solution.py:433
  (43 shorter events, 7.5 us)
Async XLA Ops:
  0.0 0.9 %copy-start.4 = (f32[128,128]{1,0:T(8,128)S(1)}, f32[128,128]{1,0:T(8,128)}, u32[]{:S(2)}) copy-start(f32[128,128]{1,0:T(8,128)} %param.11) | copy-start | bytes 196612
  0.9 5.2 %collective-permute-start.6 = (f32[256,128]{1,0:T(8,128)S(1)}, f32[256,128]{1,0:T(8,128)S(1)}, u32[]{:S(2)}, u32[]{:S(2)}) collective-permute-start(f32[256,128]{1,0:T(8,128)S(1)} %constant_dynamic-update-slice_fusion.refs_0_), channel_id=1, source_target_pairs={{0,1},{1,0},{2,3},{3,2},{4,5},{5,4},{6,7},{7,6},{8,9},{9,8},{10,11... | collective-permute-start | bytes 393224 | tf_op jit(solution)/shard_map/ppermute | solution.py:358
  1.4 16.0 %collective-permute-start.8 = (f32[256,128]{1,0:T(8,128)S(1)}, f32[256,128]{1,0:T(8,128)S(1)}, u32[]{:S(2)}, u32[]{:S(2)}) collective-permute-start(f32[256,128]{1,0:T(8,128)S(1)} %constant_dynamic-update-slice_fusion.refs_0_), channel_id=1, source_target_pairs={{0,6},{1,7},{2,4},{3,5},{4,2},{5,3},{6,0},{7,1},{8,14},{9,15},{10,... | collective-permute-start | bytes 393224 | tf_op jit(solution)/shard_map/ppermute | solution.py:358
  6.1 0.9 %copy-start = (f32[8,1024]{1,0:T(8,128)S(1)}, f32[8,1024]{1,0:T(8,128)}, u32[]{:S(2)}) copy-start(f32[8,1024]{1,0:T(8,128)} %flux.1) | copy-start | bytes 98308
  6.1 11.3 %collective-permute-start.7 = (f32[512,128]{1,0:T(8,128)S(1)}, f32[512,128]{1,0:T(8,128)S(1)}, u32[]{:S(2)}, u32[]{:S(2)}) collective-permute-start(f32[512,128]{1,0:T(8,128)S(1)} %stack.2.chip), channel_id=1, source_target_pairs={{0,2},{1,5},{2,0},{3,7},{4,6},{5,1},{6,4},{7,3},{8,10},{9,13},{10,... | collective-permute-start | bytes 786440 | tf_op jit(solution)/shard_map/ppermute | solution.py:373
  7.7 4.7 %collective-permute-start = (f32[10,8,128]{2,1,0:T(8,128)S(1)}, f32[10,8,128]{2,1,0:T(8,128)S(1)}, u32[]{:S(2)}, u32[]{:S(2)}) collective-permute-start(f32[10,8,128]{2,1,0:T(8,128)S(1)} %get-tuple-element.28.refs_0_.start), channel_id=1, source_target_pairs={{0,16},{8,24},{16,0},{24,8},{1,17},{9,25},{17,1},{25,9},{2,18},{10... | collective-permute-start | bytes 122888 | tf_op jit(solution)/shard_map/ppermute | solution.py:358
  9.3 5.4 %collective-permute-start.1 = (f32[12,8,128]{2,1,0:T(8,128)S(1)}, f32[12,8,128]{2,1,0:T(8,128)S(1)}, u32[]{:S(2)}, u32[]{:S(2)}) collective-permute-start(f32[12,8,128]{2,1,0:T(8,128)S(1)} %get-tuple-element.29), channel_id=1, source_target_pairs={{0,24},{8,16},{16,8},{24,0},{1,25},{9,17},{17,9},{25,1},{2,26},{10... | collective-permute-start | bytes 147464 | tf_op jit(solution)/shard_map/ppermute | solution.py:358
  10.7 4.1 %collective-permute-start.2 = (f32[12,8,128]{2,1,0:T(8,128)S(1)}, f32[12,8,128]{2,1,0:T(8,128)S(1)}, u32[]{:S(2)}, u32[]{:S(2)}) collective-permute-start(f32[12,8,128]{2,1,0:T(8,128)S(1)} %get-tuple-element.30), channel_id=1, source_target_pairs={{0,8},{8,0},{16,24},{24,16},{1,9},{9,1},{17,25},{25,17},{2,10},{10... | collective-permute-start | bytes 147464 | tf_op jit(solution)/shard_map/ppermute | solution.py:358
  12.4 2.5 %copy-start.1 = (f32[8,256,128]{2,1,0:T(8,128)S(1)}, f32[8,256,128]{2,1,0:T(8,128)}, u32[]{:S(2)}) copy-start(f32[8,256,128]{2,1,0:T(8,128)} %adj.3) | copy-start | bytes 3145732
  17.4 5.1 %collective-permute-start.9 = (f32[768,128]{1,0:T(8,128)S(1)}, f32[768,128]{1,0:T(8,128)S(1)}, u32[]{:S(2)}, u32[]{:S(2)}) collective-permute-start(f32[768,128]{1,0:T(8,128)S(1)} %stack.3.across), channel_id=1, source_target_pairs={{0,1},{1,0},{2,3},{3,2},{4,5},{5,4},{6,7},{7,6},{8,9},{9,8},{10,11... | collective-permute-start | bytes 1179656 | tf_op jit(solution)/shard_map/ppermute | solution.py:358
  17.7 16.1 %collective-permute-start.3 = (f32[264,128]{1,0:T(8,128)S(1)}, f32[264,128]{1,0:T(8,128)S(1)}, u32[]{:S(2)}, u32[]{:S(2)}) collective-permute-start(f32[264,128]{1,0:T(8,128)S(1)} %get-tuple-element.31), channel_id=1, source_target_pairs={{0,4},{1,5},{2,6},{3,7},{4,0},{5,1},{6,2},{7,3},{8,12},{9,13},{10,... | collective-permute-start | bytes 405512 | tf_op jit(solution)/shard_map/ppermute | solution.py:358
  19.4 16.1 %collective-permute-start.4 = (f32[264,128]{1,0:T(8,128)S(1)}, f32[264,128]{1,0:T(8,128)S(1)}, u32[]{:S(2)}, u32[]{:S(2)}) collective-permute-start(f32[264,128]{1,0:T(8,128)S(1)} %get-tuple-element.32), channel_id=1, source_target_pairs={{0,5},{1,4},{2,7},{3,6},{4,1},{5,0},{6,3},{7,2},{8,13},{9,12},{10,... | collective-permute-start | bytes 405512 | tf_op jit(solution)/shard_map/ppermute | solution.py:358
  20.3 18.0 %collective-permute-start.5 = (f32[264,128]{1,0:T(8,128)S(1)}, f32[264,128]{1,0:T(8,128)S(1)}, u32[]{:S(2)}, u32[]{:S(2)}) collective-permute-start(f32[264,128]{1,0:T(8,128)S(1)} %get-tuple-element.33), channel_id=1, source_target_pairs={{0,6},{1,7},{2,4},{3,5},{4,2},{5,3},{6,0},{7,1},{8,14},{9,15},{10,... | collective-permute-start | bytes 405512 | tf_op jit(solution)/shard_map/ppermute | solution.py:358
  22.5 15.8 %collective-permute-start.11 = (f32[264,128]{1,0:T(8,128)S(1)}, f32[264,128]{1,0:T(8,128)S(1)}, u32[]{:S(2)}, u32[]{:S(2)}) collective-permute-start(f32[264,128]{1,0:T(8,128)S(1)} %get-tuple-element.36), channel_id=1, source_target_pairs={{0,3},{1,2},{2,1},{3,0},{4,7},{5,6},{6,5},{7,4},{8,11},{9,10},{10,... | collective-permute-start | bytes 405512 | tf_op jit(solution)/shard_map/ppermute | solution.py:358
  27.1 11.7 %collective-permute-start.12 = (f32[264,128]{1,0:T(8,128)S(1)}, f32[264,128]{1,0:T(8,128)S(1)}, u32[]{:S(2)}, u32[]{:S(2)}) collective-permute-start(f32[264,128]{1,0:T(8,128)S(1)} %get-tuple-element.37), channel_id=1, source_target_pairs={{0,2},{1,3},{2,0},{3,1},{4,6},{5,7},{6,4},{7,5},{8,10},{9,11},{10,... | collective-permute-start | bytes 405512 | tf_op jit(solution)/shard_map/ppermute | solution.py:358
  33.8 5.1 %collective-permute-start.13 = (f32[264,128]{1,0:T(8,128)S(1)}, f32[264,128]{1,0:T(8,128)S(1)}, u32[]{:S(2)}, u32[]{:S(2)}) collective-permute-start(f32[264,128]{1,0:T(8,128)S(1)} %get-tuple-element.38), channel_id=1, source_target_pairs={{0,1},{1,0},{2,3},{3,2},{4,5},{5,4},{6,7},{7,6},{8,9},{9,8},{10,11... | collective-permute-start | bytes 405512 | tf_op jit(solution)/shard_map/ppermute | solution.py:358
  35.5 6.6 %collective-permute-start.10 = (f32[264,128]{1,0:T(8,128)S(1)}, f32[264,128]{1,0:T(8,128)S(1)}, u32[]{:S(2)}, u32[]{:S(2)}) collective-permute-start(f32[264,128]{1,0:T(8,128)S(1)} %get-tuple-element.35), channel_id=1, source_target_pairs={{0,7},{1,6},{2,5},{3,4},{4,3},{5,2},{6,1},{7,0},{8,15},{9,14},{10,... | collective-permute-start | bytes 405512 | tf_op jit(solution)/shard_map/ppermute | solution.py:358
  43.8 16.3 %collective-permute-start.14 = (f32[256,128]{1,0:T(8,128)S(1)}, f32[256,128]{1,0:T(8,128)S(1)}, u32[]{:S(2)}, u32[]{:S(2)}) collective-permute-start(f32[256,128]{1,0:T(8,128)S(1)} %get-tuple-element.41), channel_id=1, source_target_pairs={{0,4},{1,5},{2,6},{3,7},{4,0},{5,1},{6,2},{7,3},{8,12},{9,13},{10,... | collective-permute-start | bytes 393224 | tf_op jit(solution)/shard_map/ppermute | solution.py:358
  47.2 15.1 %collective-permute-start.15 = (f32[256,128]{1,0:T(8,128)S(1)}, f32[256,128]{1,0:T(8,128)S(1)}, u32[]{:S(2)}, u32[]{:S(2)}) collective-permute-start(f32[256,128]{1,0:T(8,128)S(1)} %get-tuple-element.42), channel_id=1, source_target_pairs={{0,5},{1,4},{2,7},{3,6},{4,1},{5,0},{6,3},{7,2},{8,13},{9,12},{10,... | collective-permute-start | bytes 393224 | tf_op jit(solution)/shard_map/ppermute | solution.py:358
  47.3 17.0 %collective-permute-start.16 = (f32[256,128]{1,0:T(8,128)S(1)}, f32[256,128]{1,0:T(8,128)S(1)}, u32[]{:S(2)}, u32[]{:S(2)}) collective-permute-start(f32[256,128]{1,0:T(8,128)S(1)} %get-tuple-element.43), channel_id=1, source_target_pairs={{0,6},{1,7},{2,4},{3,5},{4,2},{5,3},{6,0},{7,1},{8,14},{9,15},{10,... | collective-permute-start | bytes 393224 | tf_op jit(solution)/shard_map/ppermute | solution.py:358
  49.4 14.9 %collective-permute-start.17 = (f32[256,128]{1,0:T(8,128)S(1)}, f32[256,128]{1,0:T(8,128)S(1)}, u32[]{:S(2)}, u32[]{:S(2)}) collective-permute-start(f32[256,128]{1,0:T(8,128)S(1)} %get-tuple-element.46), channel_id=1, source_target_pairs={{0,3},{1,2},{2,1},{3,0},{4,7},{5,6},{6,5},{7,4},{8,11},{9,10},{10,... | collective-permute-start | bytes 393224 | tf_op jit(solution)/shard_map/ppermute | solution.py:358
  50.3 14.4 %collective-permute-start.18 = (f32[256,128]{1,0:T(8,128)S(1)}, f32[256,128]{1,0:T(8,128)S(1)}, u32[]{:S(2)}, u32[]{:S(2)}) collective-permute-start(f32[256,128]{1,0:T(8,128)S(1)} %get-tuple-element.47), channel_id=1, source_target_pairs={{0,2},{1,3},{2,0},{3,1},{4,6},{5,7},{6,4},{7,5},{8,10},{9,11},{10,... | collective-permute-start | bytes 393224 | tf_op jit(solution)/shard_map/ppermute | solution.py:358
  60.1 4.6 %collective-permute-start.20 = (f32[256,128]{1,0:T(8,128)S(1)}, f32[256,128]{1,0:T(8,128)S(1)}, u32[]{:S(2)}, u32[]{:S(2)}) collective-permute-start(f32[256,128]{1,0:T(8,128)S(1)} %get-tuple-element.49), channel_id=1, source_target_pairs={{0,1},{1,0},{2,3},{3,2},{4,5},{5,4},{6,7},{7,6},{8,9},{9,8},{10,11... | collective-permute-start | bytes 393224 | tf_op jit(solution)/shard_map/ppermute | solution.py:358
  62.3 7.2 %collective-permute-start.19 = (f32[256,128]{1,0:T(8,128)S(1)}, f32[256,128]{1,0:T(8,128)S(1)}, u32[]{:S(2)}, u32[]{:S(2)}) collective-permute-start(f32[256,128]{1,0:T(8,128)S(1)} %get-tuple-element.48), channel_id=1, source_target_pairs={{0,7},{1,6},{2,5},{3,4},{4,3},{5,2},{6,1},{7,0},{8,15},{9,14},{10,... | collective-permute-start | bytes 393224 | tf_op jit(solution)/shard_map/ppermute | solution.py:358
  (2 other events, 1.5 us)

commit v5 on v4

--- a/solution.py
+++ b/solution.py
@@ -82,7 +82,8 @@
     blades = lax.axis_size("blade")
     blade = lax.axis_index("blade")
     total = circum * blades
-    groups = weights.shape[1] // 256
+    faces = hot_rows.shape[1]
+    groups = faces // 128
     rows = hot_rows.shape[0]
     row = lax.broadcasted_iota(jnp.int32, (rows, 128), 0)
     label = jnp.where(
@@ -92,29 +93,39 @@
             (row >= circum + 8 - HALO) & (row < circum + 8), row - (circum + 8) + total, -1
         ),
     )
-    radial = lax.broadcasted_iota(jnp.int32, (block_rows, 128), 0)
+    radial = lax.broadcasted_iota(jnp.int32, (block_rows, 128), 0).astype(F32).astype(BF16)
+    zero = jnp.zeros((), BF16)
     owner = message[groups].astype(jnp.int32)
     cell = message[groups + 1].astype(jnp.int32)
     place = (owner - blade) * circum + cell // block_rows
     place = jnp.where(place < 0, place + total, place)
     inner = cell % block_rows
+    def wide(row):
+        return jnp.broadcast_to(row[None], (block_rows // 16, 16, 128)).reshape(block_rows, 128)
+
     for group in range(groups):
         lanes = slice(group * 128, (group + 1) * 128)
         lanes_low = slice((groups + group) * 128, (groups + group + 1) * 128)
         hot = jnp.where(label == place[group : group + 1, :], 1.0, 0.0).astype(BF16)
         hot_rows[:, lanes] = hot
-        hot_rows[:, lanes_low] = hot
-        hit = jnp.where(radial == inner[group : group + 1, :], 1.0, 0.0).astype(BF16)
-        hit = hit.reshape(block_rows // 16, 16, 128)
+        here = jnp.broadcast_to(inner[group : group + 1, :], (block_rows, 128)).astype(F32)
+        hit = radial == here.astype(BF16)
         for at, h in enumerate(harmonics):
             flux = jnp.broadcast_to(message[group, pl.ds(h, 1), :], (16, 128))
             flux_hi, flux_lo = split(flux)
             part = slice(at * block_rows, (at + 1) * block_rows)
-            weights[part, lanes] = (hit * flux_hi[None]).reshape(block_rows, 128)
-            weights[part, lanes_low] = (hit * flux_lo[None]).reshape(block_rows, 128)
-    return lax.dot_general(
-        hot_rows[...], weights[...], (((1,), (1,)), ((), ())), preferred_element_type=F32
-    )
+            weights[part, lanes] = jnp.where(hit, wide(flux_hi), zero)
+            weights[part, lanes_low] = jnp.where(hit, wide(flux_lo), zero)
+    high, low = (
+        lax.dot_general(
+            hot_rows[...],
+            weights[:, part],
+            (((1,), (1,)), ((), ())),
+            preferred_element_type=F32,
+        )
+        for part in (slice(0, faces), slice(faces, 2 * faces))
+    )
+    return high + low
 
 
 def face_sums_kernel(peers, *refs):
@@ -134,7 +145,7 @@
         functools.partial(face_sums_kernel, peers),
         (((rows, lanes), F32),),
         [VMEM] * (1 + len(start)),
-        [pltpu.VMEM((rows, 2 * faces), BF16), pltpu.VMEM((lanes, 2 * faces), BF16)],
+        [pltpu.VMEM((rows, faces), BF16), pltpu.VMEM((lanes, 2 * faces), BF16)],
         600_000_000,
         "face_sums",
     )(*start, message)[0]
@@ -152,7 +163,7 @@
     ]
     for copy in copies:
         copy.start()
-    groups = weights.shape[2] // 256
+    groups = hot_rows.shape[2] // 128
     odd = lax.rem(lax.axis_index("blade"), 2)
     harmonics = [peer(i) for i in peers]
     messages = (start, near, far, diag) if own else (diag, near)
@@ -193,7 +204,7 @@
         (((circum + 8, block_rows), F32),) * count + (((8, 128), F32),),
         [HBM] + [VMEM] * 4 + [ANY] * len(after),
         [
-            pltpu.VMEM((sums, rows, 2 * faces), BF16),
+            pltpu.VMEM((sums, rows, faces), BF16),
             pltpu.VMEM((sums, count * block_rows, 2 * faces), BF16),
             pltpu.VMEM((rows, count * block_rows), F32),
             pltpu.VMEM((count, circum, block_rows), F32),
@@ -216,19 +227,20 @@
     def solve(rhs, below, k):
         rhs_hi, rhs_lo = split(rhs)
         below_hi, below_lo = split(below)
-        left = jnp.concatenate(
-            [
-                jnp.concatenate([rhs_hi, below_hi], axis=1),
-                jnp.concatenate([rhs_lo, below_lo], axis=1),
-            ],
-            axis=0,
-        )
-        product = lax.dot_general(
-            left, weights[first + k], (((1,), (1,)), ((), ())), preferred_element_type=F32
-        )
-        high, low = product[:rows], product[rows:]
-        cross = low[:, :block_rows] + high[:, block_rows:]
-        return (high[:, :block_rows] + cross) + low[:, block_rows:]
+        contract = (((1,), (1,)), ((), ()))
+        high = lax.dot_general(
+            jnp.concatenate([rhs_hi, below_hi], axis=1),
+            weights[first + k],
+            contract,
+            preferred_element_type=F32,
+        )
+        low = lax.dot_general(
+            jnp.concatenate([rhs_lo, below_lo], axis=1),
+            weights[first + k, :block_rows],
+            contract,
+            preferred_element_type=F32,
+        )
+        return high[:, :block_rows] + (low + high[:, block_rows:])
 
     def advance(fields, k, sweep):
         rhs = right[k]

time: 70.8 us -> 70.2 us (level)
  starting transfers between devices: 27.7 us -> 30 us
  waiting for transfers between devices: 26.7 us -> 25 us
  Pallas kernels: 13.6 us -> 12.2 us
    ppermute x20, starting transfers between devices: 27.6 us -> 29.9 us  [exchange(): return lax.ppermute(array, axis, [(i, i ^ bits) for i in range(count)])]
    ppermute x20, waiting for transfers between devices: 26.7 us -> 25 us  [exchange(): return lax.ppermute(array, axis, [(i, i ^ bits) for i in range(count)])]
  transfers between devices with their start and end apart: 21 -> 21, of which waited for: 10 -> 10; matrix products, arithmetic and copies ran while one was open for 1% -> 1% of each run, Pallas kernels for 16% -> 14%
where the time goes in v5:
time: 70.2 us; the launch traced here: 69.8 us
  starting transfers between devices  30 us (43%)
  waiting for transfers between devices  25 us (36%)
  Pallas kernels  12.2 us (17%)
  local copies, waits for them, and re-layouts  2.36 us (3%)
    ppermute x20, starting transfers between devices, exchange(): return lax.ppermute(array, axis, [(i, i ^ bits) for i in range(count)])  29.9 us
    ppermute x20, waiting for transfers between devices, exchange(): return lax.ppermute(array, axis, [(i, i ^ bits) for i in range(count)])  25 us
    pallas_call x2, Pallas kernels, right_pieces(): call(functools.partial(right_kernel, peers, own), (((circum + 8, block_ro...  6.5 us
    pallas_call x2, Pallas kernels, face_sums(): call(functools.partial(face_sums_kernel, peers), (((rows, lanes), F32),),...  1.83 us
    unnamed x11, local copies, waits for them, and re-layouts  1.57 us
  transfers between devices with their start and end apart: 21, of which 10 were waited for; matrix products, arithmetic and copies ran while one was open for 1% of the time, Pallas kernels for 14%

profile of v5, /device:TPU:0, one launch (start us, length us, event | category | flops | bytes accessed | tf_op | source)
XLA Modules:
  0.0 69.8 jit_solution(10984062820360471910)
XLA Ops:
  1.4 4.7 %collective-permute-start.8 = (f32[256,128]{1,0:T(8,128)S(1)}, f32[256,128]{1,0:T(8,128)S(1)}, u32[]{:S(2)}, u32[]{:S(2)}) collective-permute-start(f32[256,128]{1,0:T(8,128)S(1)} %constant_dynamic-update-slice_fusion.refs_0_), channel_id=1, source_target_pairs={{0,6},{1,7},{2,4},{3,5},{4,2},{5,3},{6,0},{7,1},{8,14},{9,15},{10,... | collective-permute-start | bytes 393224 | tf_op jit(solution)/shard_map/ppermute | solution.py:370
  7.7 1.6 %collective-permute-start = (f32[10,8,128]{2,1,0:T(8,128)S(1)}, f32[10,8,128]{2,1,0:T(8,128)S(1)}, u32[]{:S(2)}, u32[]{:S(2)}) collective-permute-start(f32[10,8,128]{2,1,0:T(8,128)S(1)} %get-tuple-element.28.refs_0_.start), channel_id=1, source_target_pairs={{0,16},{8,24},{16,0},{24,8},{1,17},{9,25},{17,1},{25,9},{2,18},{10... | collective-permute-start | bytes 122888 | tf_op jit(solution)/shard_map/ppermute | solution.py:370
  9.3 1.4 %collective-permute-start.1 = (f32[12,8,128]{2,1,0:T(8,128)S(1)}, f32[12,8,128]{2,1,0:T(8,128)S(1)}, u32[]{:S(2)}, u32[]{:S(2)}) collective-permute-start(f32[12,8,128]{2,1,0:T(8,128)S(1)} %get-tuple-element.29), channel_id=1, source_target_pairs={{0,24},{8,16},{16,8},{24,0},{1,25},{9,17},{17,9},{25,1},{2,26},{10... | collective-permute-start | bytes 147464 | tf_op jit(solution)/shard_map/ppermute | solution.py:370
  11.3 0.9 %face_sums.2.refs_0_ = f32[272,512]{1,0:T(8,128)S(1)} custom-call(f32[10,8,128]{2,1,0:T(8,128)S(1)} %get-tuple-element.28.refs_0_.start), custom_call_target="tpu_custom_call" | custom-call | flops 600000000 | bytes 1048576 | tf_op jit(solution)/shard_map/face_sums/pallas_call | solution.py:144
  12.2 0.9 %face_sums.3.start = f32[272,512]{1,0:T(8,128)S(1)} custom-call(f32[272,512]{1,0:T(8,128)S(1)} %face_sums.2.refs_0_, f32[10,8,128]{2,1,0:T(8,128)S(1)} %collective-permute-done.refs_1_.far), custom_call_target="tpu_custom_call" | custom-call | flops 600000000 | bytes 1048576 | tf_op jit(solution)/shard_map/face_sums/pallas_call | solution.py:144
  13.1 1.5 %collective-permute-done.1.diag = f32[12,8,128]{2,1,0:T(8,128)S(1)} collective-permute-done((f32[12,8,128]{2,1,0:T(8,128)S(1)}, f32[12,8,128]{2,1,0:T(8,128)S(1)}, u32[]{:S(2)}, u32[]{:S(2)}) %collective-permute-start.1) | collective-permute-done | bytes 49184 | tf_op jit(solution)/shard_map/ppermute | solution.py:370
  14.8 2.3 %right_first.1 = (f32[264,128]{1,0:T(8,128)S(1)}, f32[264,128]{1,0:T(8,128)S(1)}, f32[264,128]{1,0:T(8,128)S(1)}, f32[264,128]{1,0:T(8,128)S(1)}, f32[8,128]{1,0:T(8,128)S(1)}) custom-call(f32[8,256,128]{2,1,0:T(8,128)S(1)} %copy-done.1, f32[272,512]{1,0:T(8,128)S(1)} %face_sums.3.start, f32[12,8,128]{2,1,0:T(8,128)S(1)} %collective-permute-done.1.diag, ...), custom_call_target="tpu_custom_call" | custom-call | flops 1200000000 | bytes 1048576 | tf_op jit(solution)/shard_map/right_first/pallas_call | solution.py:202
  17.7 1.5 %collective-permute-start.3 = (f32[264,128]{1,0:T(8,128)S(1)}, f32[264,128]{1,0:T(8,128)S(1)}, u32[]{:S(2)}, u32[]{:S(2)}) collective-permute-start(f32[264,128]{1,0:T(8,128)S(1)} %get-tuple-element.31), channel_id=1, source_target_pairs={{0,4},{1,5},{2,6},{3,7},{4,0},{5,1},{6,2},{7,3},{8,12},{9,13},{10,... | collective-permute-start | bytes 405512 | tf_op jit(solution)/shard_map/ppermute | solution.py:370
  20.1 2.4 %collective-permute-start.5 = (f32[264,128]{1,0:T(8,128)S(1)}, f32[264,128]{1,0:T(8,128)S(1)}, u32[]{:S(2)}, u32[]{:S(2)}) collective-permute-start(f32[264,128]{1,0:T(8,128)S(1)} %get-tuple-element.33), channel_id=1, source_target_pairs={{0,6},{1,7},{2,4},{3,5},{4,2},{5,3},{6,0},{7,1},{8,14},{9,15},{10,... | collective-permute-start | bytes 405512 | tf_op jit(solution)/shard_map/ppermute | solution.py:370
  22.7 4.2 %right_second.1 = (f32[264,128]{1,0:T(8,128)S(1)}, f32[264,128]{1,0:T(8,128)S(1)}, f32[264,128]{1,0:T(8,128)S(1)}, f32[264,128]{1,0:T(8,128)S(1)}, f32[8,128]{1,0:T(8,128)}) custom-call(f32[8,256,128]{2,1,0:T(8,128)S(1)} %copy-done.1, f32[10,8,128]{2,1,0:T(8,128)S(1)} %get-tuple-element.28.refs_0_.start, f32[12,8,128]{2,1,0:T(8,128)S(1)} %collective-permute-done.1.diag, ...), custom_call_target="tpu_custom_call" | custom-call | flops 2400000000 | bytes 1048576 | tf_op jit(solution)/shard_map/right_second/pallas_call | solution.py:202
  26.9 2.1 %collective-permute-start.12 = (f32[264,128]{1,0:T(8,128)S(1)}, f32[264,128]{1,0:T(8,128)S(1)}, u32[]{:S(2)}, u32[]{:S(2)}) collective-permute-start(f32[264,128]{1,0:T(8,128)S(1)} %get-tuple-element.37), channel_id=1, source_target_pairs={{0,2},{1,3},{2,0},{3,1},{4,6},{5,7},{6,4},{7,5},{8,10},{9,11},{10,... | collective-permute-start | bytes 405512 | tf_op jit(solution)/shard_map/ppermute | solution.py:370
  29.0 4.8 %collective-permute-done.3.refs_0_ = f32[264,128]{1,0:T(8,128)S(1)} collective-permute-done((f32[264,128]{1,0:T(8,128)S(1)}, f32[264,128]{1,0:T(8,128)S(1)}, u32[]{:S(2)}, u32[]{:S(2)}) %collective-permute-start.3) | collective-permute-done | bytes 135200 | tf_op jit(solution)/shard_map/ppermute | solution.py:370
  33.8 1.2 %collective-permute-done.4.refs_1_ = f32[264,128]{1,0:T(8,128)S(1)} collective-permute-done((f32[264,128]{1,0:T(8,128)S(1)}, f32[264,128]{1,0:T(8,128)S(1)}, u32[]{:S(2)}, u32[]{:S(2)}) %collective-permute-start.4) | collective-permute-done | bytes 135200 | tf_op jit(solution)/shard_map/ppermute | solution.py:370
  35.0 3.0 %collective-permute-start.10 = (f32[264,128]{1,0:T(8,128)S(1)}, f32[264,128]{1,0:T(8,128)S(1)}, u32[]{:S(2)}, u32[]{:S(2)}) collective-permute-start(f32[264,128]{1,0:T(8,128)S(1)} %get-tuple-element.35), channel_id=1, source_target_pairs={{0,7},{1,6},{2,5},{3,4},{4,3},{5,2},{6,1},{7,0},{8,15},{9,14},{10,... | collective-permute-start | bytes 405512 | tf_op jit(solution)/shard_map/ppermute | solution.py:370
  38.7 1.3 %sweeps_lower.1 = (f32[3,272,128]{2,1,0:T(8,128)S(1)}, f32[4,256,128]{2,1,0:T(8,128)S(1)}) custom-call(f32[264,128]{1,0:T(8,128)S(1)} %collective-permute-done.3.refs_0_, f32[264,128]{1,0:T(8,128)S(1)} %collective-permute-done.4.refs_1_, f32[264,128]{1,0:T(8,128)S(1)} %collective-permute-done.11.refs_2_.refs_3_, ...), custom_call_target="tpu_custom_call" | custom-call | flops 1000000000 | bytes 1048576 | tf_op jit(solution)/shard_map/sweeps_lower/pallas_call | solution.py:417
  40.0 1.4 %collective-permute-done.10.refs_3_ = f32[264,128]{1,0:T(8,128)S(1)} collective-permute-done((f32[264,128]{1,0:T(8,128)S(1)}, f32[264,128]{1,0:T(8,128)S(1)}, u32[]{:S(2)}, u32[]{:S(2)}) %collective-permute-start.10) | collective-permute-done | bytes 135200 | tf_op jit(solution)/shard_map/ppermute | solution.py:370
  41.4 1.3 %sweeps_far.1 = (f32[256,128]{1,0:T(8,128)S(1)}, f32[256,128]{1,0:T(8,128)S(1)}, f32[256,128]{1,0:T(8,128)S(1)}, f32[256,128]{1,0:T(8,128)S(1)}, f32[3,272,128]{2,1,0:T(8,128)S(1)}) custom-call(f32[264,128]{1,0:T(8,128)S(1)} %collective-permute-done.3.refs_0_, f32[264,128]{1,0:T(8,128)S(1)} %collective-permute-done.4.refs_1_, ...), custom_call_target="tpu_custom_call" | custom-call | flops 1000000000 | bytes 1048576 | tf_op jit(solution)/shard_map/sweeps_far/pallas_call | solution.py:425
  42.7 4.3 %collective-permute-start.14 = (f32[256,128]{1,0:T(8,128)S(1)}, f32[256,128]{1,0:T(8,128)S(1)}, u32[]{:S(2)}, u32[]{:S(2)}) collective-permute-start(f32[256,128]{1,0:T(8,128)S(1)} %get-tuple-element.41), channel_id=1, source_target_pairs={{0,4},{1,5},{2,6},{3,7},{4,0},{5,1},{6,2},{7,3},{8,12},{9,13},{10,... | collective-permute-start | bytes 393224 | tf_op jit(solution)/shard_map/ppermute | solution.py:370
  47.1 2.1 %collective-permute-start.16 = (f32[256,128]{1,0:T(8,128)S(1)}, f32[256,128]{1,0:T(8,128)S(1)}, u32[]{:S(2)}, u32[]{:S(2)}) collective-permute-start(f32[256,128]{1,0:T(8,128)S(1)} %get-tuple-element.43), channel_id=1, source_target_pairs={{0,6},{1,7},{2,4},{3,5},{4,2},{5,3},{6,0},{7,1},{8,14},{9,15},{10,... | collective-permute-start | bytes 393224 | tf_op jit(solution)/shard_map/ppermute | solution.py:370
  51.0 8.9 %collective-permute-done.14.refs_0_ = f32[256,128]{1,0:T(8,128)S(1)} collective-permute-done((f32[256,128]{1,0:T(8,128)S(1)}, f32[256,128]{1,0:T(8,128)S(1)}, u32[]{:S(2)}, u32[]{:S(2)}) %collective-permute-start.14) | collective-permute-done | bytes 131104 | tf_op jit(solution)/shard_map/ppermute | solution.py:370
  59.9 2.0 %collective-permute-done.15.refs_1_ = f32[256,128]{1,0:T(8,128)S(1)} collective-permute-done((f32[256,128]{1,0:T(8,128)S(1)}, f32[256,128]{1,0:T(8,128)S(1)}, u32[]{:S(2)}, u32[]{:S(2)}) %collective-permute-start.15) | collective-permute-done | bytes 131104 | tf_op jit(solution)/shard_map/ppermute | solution.py:370
  61.8 2.5 %collective-permute-start.19 = (f32[256,128]{1,0:T(8,128)S(1)}, f32[256,128]{1,0:T(8,128)S(1)}, u32[]{:S(2)}, u32[]{:S(2)}) collective-permute-start(f32[256,128]{1,0:T(8,128)S(1)} %get-tuple-element.48), channel_id=1, source_target_pairs={{0,7},{1,6},{2,5},{3,4},{4,3},{5,2},{6,1},{7,0},{8,15},{9,14},{10,... | collective-permute-start | bytes 393224 | tf_op jit(solution)/shard_map/ppermute | solution.py:370
  65.1 3.6 %collective-permute-done.19.refs_5_ = f32[256,128]{1,0:T(8,128)S(1)} collective-permute-done((f32[256,128]{1,0:T(8,128)S(1)}, f32[256,128]{1,0:T(8,128)S(1)}, u32[]{:S(2)}, u32[]{:S(2)}) %collective-permute-start.19) | collective-permute-done | bytes 131104 | tf_op jit(solution)/shard_map/ppermute | solution.py:370
  68.8 1.0 %place.1 = f32[8,256,128]{2,1,0:T(8,128)} custom-call(f32[256,128]{1,0:T(8,128)S(1)} %collective-permute-done.14.refs_0_, f32[256,128]{1,0:T(8,128)S(1)} %collective-permute-done.15.refs_1_, f32[256,128]{1,0:T(8,128)S(1)} %collective-permute-done.16.refs_2_, f32[256,128]{1,0:T(8,128)S(1)} %collective-permute-done.17.refs_3_, ...), custom_call_target="tpu_custom_call" | custom-call | bytes 1048576 | tf_op jit(solution)/shard_map/place/pallas_call | solution.py:445
  (43 shorter events, 8.4 us)
Async XLA Ops:
  0.0 0.9 %copy-start.4 = (f32[128,128]{1,0:T(8,128)S(1)}, f32[128,128]{1,0:T(8,128)}, u32[]{:S(2)}) copy-start(f32[128,128]{1,0:T(8,128)} %param.11) | copy-start | bytes 196612
  0.9 5.2 %collective-permute-start.6 = (f32[256,128]{1,0:T(8,128)S(1)}, f32[256,128]{1,0:T(8,128)S(1)}, u32[]{:S(2)}, u32[]{:S(2)}) collective-permute-start(f32[256,128]{1,0:T(8,128)S(1)} %constant_dynamic-update-slice_fusion.refs_0_), channel_id=1, source_target_pairs={{0,1},{1,0},{2,3},{3,2},{4,5},{5,4},{6,7},{7,6},{8,9},{9,8},{10,11... | collective-permute-start | bytes 393224 | tf_op jit(solution)/shard_map/ppermute | solution.py:370
  1.4 15.8 %collective-permute-start.8 = (f32[256,128]{1,0:T(8,128)S(1)}, f32[256,128]{1,0:T(8,128)S(1)}, u32[]{:S(2)}, u32[]{:S(2)}) collective-permute-start(f32[256,128]{1,0:T(8,128)S(1)} %constant_dynamic-update-slice_fusion.refs_0_), channel_id=1, source_target_pairs={{0,6},{1,7},{2,4},{3,5},{4,2},{5,3},{6,0},{7,1},{8,14},{9,15},{10,... | collective-permute-start | bytes 393224 | tf_op jit(solution)/shard_map/ppermute | solution.py:370
  6.1 0.9 %copy-start = (f32[8,1024]{1,0:T(8,128)S(1)}, f32[8,1024]{1,0:T(8,128)}, u32[]{:S(2)}) copy-start(f32[8,1024]{1,0:T(8,128)} %flux.1) | copy-start | bytes 98308
  6.1 11.1 %collective-permute-start.7 = (f32[512,128]{1,0:T(8,128)S(1)}, f32[512,128]{1,0:T(8,128)S(1)}, u32[]{:S(2)}, u32[]{:S(2)}) collective-permute-start(f32[512,128]{1,0:T(8,128)S(1)} %stack.2.chip), channel_id=1, source_target_pairs={{0,2},{1,5},{2,0},{3,7},{4,6},{5,1},{6,4},{7,3},{8,10},{9,13},{10,... | collective-permute-start | bytes 786440 | tf_op jit(solution)/shard_map/ppermute | solution.py:385
  7.7 4.5 %collective-permute-start = (f32[10,8,128]{2,1,0:T(8,128)S(1)}, f32[10,8,128]{2,1,0:T(8,128)S(1)}, u32[]{:S(2)}, u32[]{:S(2)}) collective-permute-start(f32[10,8,128]{2,1,0:T(8,128)S(1)} %get-tuple-element.28.refs_0_.start), channel_id=1, source_target_pairs={{0,16},{8,24},{16,0},{24,8},{1,17},{9,25},{17,1},{25,9},{2,18},{10... | collective-permute-start | bytes 122888 | tf_op jit(solution)/shard_map/ppermute | solution.py:370
  9.3 5.4 %collective-permute-start.1 = (f32[12,8,128]{2,1,0:T(8,128)S(1)}, f32[12,8,128]{2,1,0:T(8,128)S(1)}, u32[]{:S(2)}, u32[]{:S(2)}) collective-permute-start(f32[12,8,128]{2,1,0:T(8,128)S(1)} %get-tuple-element.29), channel_id=1, source_target_pairs={{0,24},{8,16},{16,8},{24,0},{1,25},{9,17},{17,9},{25,1},{2,26},{10... | collective-permute-start | bytes 147464 | tf_op jit(solution)/shard_map/ppermute | solution.py:370
  10.7 4.1 %collective-permute-start.2 = (f32[12,8,128]{2,1,0:T(8,128)S(1)}, f32[12,8,128]{2,1,0:T(8,128)S(1)}, u32[]{:S(2)}, u32[]{:S(2)}) collective-permute-start(f32[12,8,128]{2,1,0:T(8,128)S(1)} %get-tuple-element.30), channel_id=1, source_target_pairs={{0,8},{8,0},{16,24},{24,16},{1,9},{9,1},{17,25},{25,17},{2,10},{10... | collective-permute-start | bytes 147464 | tf_op jit(solution)/shard_map/ppermute | solution.py:370
  12.2 2.6 %copy-start.1 = (f32[8,256,128]{2,1,0:T(8,128)S(1)}, f32[8,256,128]{2,1,0:T(8,128)}, u32[]{:S(2)}) copy-start(f32[8,256,128]{2,1,0:T(8,128)} %adj.3) | copy-start | bytes 3145732
  17.2 5.3 %collective-permute-start.9 = (f32[768,128]{1,0:T(8,128)S(1)}, f32[768,128]{1,0:T(8,128)S(1)}, u32[]{:S(2)}, u32[]{:S(2)}) collective-permute-start(f32[768,128]{1,0:T(8,128)S(1)} %stack.3.across), channel_id=1, source_target_pairs={{0,1},{1,0},{2,3},{3,2},{4,5},{5,4},{6,7},{7,6},{8,9},{9,8},{10,11... | collective-permute-start | bytes 1179656 | tf_op jit(solution)/shard_map/ppermute | solution.py:370
  17.7 16.1 %collective-permute-start.3 = (f32[264,128]{1,0:T(8,128)S(1)}, f32[264,128]{1,0:T(8,128)S(1)}, u32[]{:S(2)}, u32[]{:S(2)}) collective-permute-start(f32[264,128]{1,0:T(8,128)S(1)} %get-tuple-element.31), channel_id=1, source_target_pairs={{0,4},{1,5},{2,6},{3,7},{4,0},{5,1},{6,2},{7,3},{8,12},{9,13},{10,... | collective-permute-start | bytes 405512 | tf_op jit(solution)/shard_map/ppermute | solution.py:370
  19.2 15.9 %collective-permute-start.4 = (f32[264,128]{1,0:T(8,128)S(1)}, f32[264,128]{1,0:T(8,128)S(1)}, u32[]{:S(2)}, u32[]{:S(2)}) collective-permute-start(f32[264,128]{1,0:T(8,128)S(1)} %get-tuple-element.32), channel_id=1, source_target_pairs={{0,5},{1,4},{2,7},{3,6},{4,1},{5,0},{6,3},{7,2},{8,13},{9,12},{10,... | collective-permute-start | bytes 405512 | tf_op jit(solution)/shard_map/ppermute | solution.py:370
  20.1 18.0 %collective-permute-start.5 = (f32[264,128]{1,0:T(8,128)S(1)}, f32[264,128]{1,0:T(8,128)S(1)}, u32[]{:S(2)}, u32[]{:S(2)}) collective-permute-start(f32[264,128]{1,0:T(8,128)S(1)} %get-tuple-element.33), channel_id=1, source_target_pairs={{0,6},{1,7},{2,4},{3,5},{4,2},{5,3},{6,0},{7,1},{8,14},{9,15},{10,... | collective-permute-start | bytes 405512 | tf_op jit(solution)/shard_map/ppermute | solution.py:370
  22.5 15.6 %collective-permute-start.11 = (f32[264,128]{1,0:T(8,128)S(1)}, f32[264,128]{1,0:T(8,128)S(1)}, u32[]{:S(2)}, u32[]{:S(2)}) collective-permute-start(f32[264,128]{1,0:T(8,128)S(1)} %get-tuple-element.36), channel_id=1, source_target_pairs={{0,3},{1,2},{2,1},{3,0},{4,7},{5,6},{6,5},{7,4},{8,11},{9,10},{10,... | collective-permute-start | bytes 405512 | tf_op jit(solution)/shard_map/ppermute | solution.py:370
  26.9 11.8 %collective-permute-start.12 = (f32[264,128]{1,0:T(8,128)S(1)}, f32[264,128]{1,0:T(8,128)S(1)}, u32[]{:S(2)}, u32[]{:S(2)}) collective-permute-start(f32[264,128]{1,0:T(8,128)S(1)} %get-tuple-element.37), channel_id=1, source_target_pairs={{0,2},{1,3},{2,0},{3,1},{4,6},{5,7},{6,4},{7,5},{8,10},{9,11},{10,... | collective-permute-start | bytes 405512 | tf_op jit(solution)/shard_map/ppermute | solution.py:370
  33.8 4.9 %collective-permute-start.13 = (f32[264,128]{1,0:T(8,128)S(1)}, f32[264,128]{1,0:T(8,128)S(1)}, u32[]{:S(2)}, u32[]{:S(2)}) collective-permute-start(f32[264,128]{1,0:T(8,128)S(1)} %get-tuple-element.38), channel_id=1, source_target_pairs={{0,1},{1,0},{2,3},{3,2},{4,5},{5,4},{6,7},{7,6},{8,9},{9,8},{10,11... | collective-permute-start | bytes 405512 | tf_op jit(solution)/shard_map/ppermute | solution.py:370
  35.0 6.3 %collective-permute-start.10 = (f32[264,128]{1,0:T(8,128)S(1)}, f32[264,128]{1,0:T(8,128)S(1)}, u32[]{:S(2)}, u32[]{:S(2)}) collective-permute-start(f32[264,128]{1,0:T(8,128)S(1)} %get-tuple-element.35), channel_id=1, source_target_pairs={{0,7},{1,6},{2,5},{3,4},{4,3},{5,2},{6,1},{7,0},{8,15},{9,14},{10,... | collective-permute-start | bytes 405512 | tf_op jit(solution)/shard_map/ppermute | solution.py:370
  42.7 17.2 %collective-permute-start.14 = (f32[256,128]{1,0:T(8,128)S(1)}, f32[256,128]{1,0:T(8,128)S(1)}, u32[]{:S(2)}, u32[]{:S(2)}) collective-permute-start(f32[256,128]{1,0:T(8,128)S(1)} %get-tuple-element.41), channel_id=1, source_target_pairs={{0,4},{1,5},{2,6},{3,7},{4,0},{5,1},{6,2},{7,3},{8,12},{9,13},{10,... | collective-permute-start | bytes 393224 | tf_op jit(solution)/shard_map/ppermute | solution.py:370
  47.1 14.8 %collective-permute-start.15 = (f32[256,128]{1,0:T(8,128)S(1)}, f32[256,128]{1,0:T(8,128)S(1)}, u32[]{:S(2)}, u32[]{:S(2)}) collective-permute-start(f32[256,128]{1,0:T(8,128)S(1)} %get-tuple-element.42), channel_id=1, source_target_pairs={{0,5},{1,4},{2,7},{3,6},{4,1},{5,0},{6,3},{7,2},{8,13},{9,12},{10,... | collective-permute-start | bytes 393224 | tf_op jit(solution)/shard_map/ppermute | solution.py:370
  47.1 17.3 %collective-permute-start.16 = (f32[256,128]{1,0:T(8,128)S(1)}, f32[256,128]{1,0:T(8,128)S(1)}, u32[]{:S(2)}, u32[]{:S(2)}) collective-permute-start(f32[256,128]{1,0:T(8,128)S(1)} %get-tuple-element.43), channel_id=1, source_target_pairs={{0,6},{1,7},{2,4},{3,5},{4,2},{5,3},{6,0},{7,1},{8,14},{9,15},{10,... | collective-permute-start | bytes 393224 | tf_op jit(solution)/shard_map/ppermute | solution.py:370
  49.2 15.1 %collective-permute-start.17 = (f32[256,128]{1,0:T(8,128)S(1)}, f32[256,128]{1,0:T(8,128)S(1)}, u32[]{:S(2)}, u32[]{:S(2)}) collective-permute-start(f32[256,128]{1,0:T(8,128)S(1)} %get-tuple-element.46), channel_id=1, source_target_pairs={{0,3},{1,2},{2,1},{3,0},{4,7},{5,6},{6,5},{7,4},{8,11},{9,10},{10,... | collective-permute-start | bytes 393224 | tf_op jit(solution)/shard_map/ppermute | solution.py:370
  50.1 15.0 %collective-permute-start.18 = (f32[256,128]{1,0:T(8,128)S(1)}, f32[256,128]{1,0:T(8,128)S(1)}, u32[]{:S(2)}, u32[]{:S(2)}) collective-permute-start(f32[256,128]{1,0:T(8,128)S(1)} %get-tuple-element.47), channel_id=1, source_target_pairs={{0,2},{1,3},{2,0},{3,1},{4,6},{5,7},{6,4},{7,5},{8,10},{9,11},{10,... | collective-permute-start | bytes 393224 | tf_op jit(solution)/shard_map/ppermute | solution.py:370
  59.9 5.3 %collective-permute-start.20 = (f32[256,128]{1,0:T(8,128)S(1)}, f32[256,128]{1,0:T(8,128)S(1)}, u32[]{:S(2)}, u32[]{:S(2)}) collective-permute-start(f32[256,128]{1,0:T(8,128)S(1)} %get-tuple-element.49), channel_id=1, source_target_pairs={{0,1},{1,0},{2,3},{3,2},{4,5},{5,4},{6,7},{7,6},{8,9},{9,8},{10,11... | collective-permute-start | bytes 393224 | tf_op jit(solution)/shard_map/ppermute | solution.py:370
  61.8 6.9 %collective-permute-start.19 = (f32[256,128]{1,0:T(8,128)S(1)}, f32[256,128]{1,0:T(8,128)S(1)}, u32[]{:S(2)}, u32[]{:S(2)}) collective-permute-start(f32[256,128]{1,0:T(8,128)S(1)} %get-tuple-element.48), channel_id=1, source_target_pairs={{0,7},{1,6},{2,5},{3,4},{4,3},{5,2},{6,1},{7,0},{8,15},{9,14},{10,... | collective-permute-start | bytes 393224 | tf_op jit(solution)/shard_map/ppermute | solution.py:370
  (2 other events, 1.5 us)
